TPU v7x, 1024 devices: a whole 4x4x32 slice. The times are simulated.
1024 devices in a mesh: member: 8 (over z_hi, core), region: 128 (over z_lo, y, x).
Axes of the slice: x: 4, y: 4, z: 32 (z_hi: 4, z_lo: 8; z = z_hi * 8 + z_lo), core: 2. Of those that a mesh axis runs over, the one named last changes fastest.
Arguments:
- members: float32 [512, 8, 32768], P('member', None, 'region'), may hold values from -12 to 12
- weights: float32 [2, 512, 8, 32768], P(None, 'member', None, 'region'), may hold values from -6 to 6
- taper_table: float32 [8], replicated, may hold values from 0.1 to 1
- pair_blocks: int32 [1024, 2], P('region'), may hold values from 0 to 3, as said below
- pair_taper: int32 [1024], P('region'), may hold values from 0 to 7
- pair_batch: int32 [1024], P('region'), may hold values from 0 to 1
Outputs:
- analysis: float32 [512, 8, 32768], P('member', None, 'region')
Inputs may be any that keep to these rules, and one draw needn't show every extreme that they name: `pair_blocks`: row p of group r is (t, s): t one of the region's 2 blocks and s = t + j with j in 0, 1, 2; no (t, s, pair_batch) repeats within a group; every group holds a pair with (t, s) = (0, 0) and one with (1, 3).
All inputs are finite; a program needn't handle non-finite values.
Results may differ from a plain program's by a relative error of at most 0.0003.
Values sent between devices are 32-bit elements; how exact they have to be, the bound alone decides.
No kernel may reach another device: no remote copies, remote signals or barrier semaphores. Data moves between devices by JAX's collectives and lax.ppermute only.
A program may use at most 32 MiB of HBM per device.

v0:
```python
import jax
import jax.numpy as jnp
from jax import lax
from jax.sharding import PartitionSpec as P

BLK = 128


def extended_2(x, sides, width):
    for axis, dim in sides:
        count, length = (lax.axis_size(axis), x.shape[dim])
        up = [(i, (i + 1) % count) for i in range(count)]
        down = [(j, i) for i, j in up]
        last = lax.slice_in_dim(x, length - width, length, axis=dim)
        leading = lax.slice_in_dim(x, 0, width, axis=dim)
        before = lax.ppermute(last, axis, up)
        after = lax.ppermute(leading, axis, down)
        x = jnp.concatenate([before, x, after], axis=dim)
    return x


def combine(coef_pair, weight_pair):
    return coef_pair[:, 0][:, None] * weight_pair[0] + coef_pair[:, 1][:, None] * weight_pair[1]


def local(members, weights, taper_table, pair_blocks, pair_taper, pair_batch):
    member_loc, levels, column_count = members.shape
    ensemble = member_loc * lax.axis_size("member")
    level_dev = levels // lax.axis_size("member")
    block_count = column_count // BLK
    moved_states, moved_weights = (
        lax.all_to_all(members[None], "member", split_axis=2, concat_axis=1, tiled=True),
        lax.all_to_all(weights, "member", split_axis=2, concat_axis=1, tiled=True),
    )
    level_states = moved_states[0]
    taper_hot = (
        pair_taper[:, None] == jnp.arange(taper_table.shape[0], dtype=jnp.int32)[None, :]
    ).astype(jnp.float32)
    tapers = jnp.dot(taper_hot, taper_table, precision=lax.Precision.HIGHEST) / (ensemble - 1)
    targets = pair_blocks[:, 0]
    offsets = pair_blocks[:, 1] - targets
    target_hot = (targets[:, None] == jnp.arange(block_count, dtype=jnp.int32)[None, :]).astype(
        jnp.float32
    )
    offset_hot = (offsets[:, None] == jnp.arange(3, dtype=jnp.int32)[None, :]).astype(jnp.float32)
    batch_hot = (pair_batch[:, None] == jnp.arange(2, dtype=jnp.int32)[None, :]).astype(jnp.float32)
    block_coefs = jnp.einsum(
        "p,pt,pj,pb->tjb",
        tapers,
        target_hot,
        offset_hot,
        batch_hot,
        precision=lax.Precision.HIGHEST,
    )
    stacked = jnp.concatenate([level_states[None], moved_weights], axis=0)
    extended = extended_2(stacked, (("region", 3),), BLK)
    states_ext = extended[0]
    weight_ext = extended[1:].reshape(2, ensemble, level_dev, block_count + 2, BLK)
    mixed_weights = [
        combine(
            block_coefs[:, offset_step],
            weight_ext[:, :, :, offset_step : offset_step + block_count],
        )
        for offset_step in range(3)
    ]
    member_mean = jnp.mean(states_ext, axis=0)
    anomalies = (states_ext - member_mean[None]).reshape(ensemble, level_dev, block_count + 2, BLK)
    target_blocks = anomalies[:, :, 1 : block_count + 1]
    increment = jnp.zeros((ensemble, level_dev, block_count, BLK), jnp.float32)
    for offset_step in range(3):
        source_blocks = anomalies[:, :, offset_step : offset_step + block_count]
        covariance = jnp.einsum(
            "kltc,kltd->ltcd", target_blocks, source_blocks, precision=lax.Precision.HIGHEST
        )
        increment = increment + jnp.einsum(
            "ltcd,mltd->mltc",
            covariance,
            mixed_weights[offset_step],
            precision=lax.Precision.HIGHEST,
        )
    returned = lax.all_to_all(
        increment.reshape(ensemble, level_dev, column_count),
        "member",
        split_axis=0,
        concat_axis=1,
        tiled=True,
    )
    return members + returned


def solution(mesh):
    placed = (
        P("member", None, "region"),
        P(None, "member", None, "region"),
        P(),
        P("region", None),
        P("region"),
        P("region"),
    )
    return jax.shard_map(
        local, mesh=mesh, in_specs=placed, out_specs=P("member", None, "region"), check_vma=False
    )
```

profile of v0, /device:TPU:1, one launch (start us, length us, event | category | flops | bytes accessed | tf_op | source)
XLA Modules:
  0.0 311.4 jit_solution(724319601564346345)
XLA Ops:
  0.0 0.0 copy-start
  0.0 2.6 copy.38
  2.6 30.0 %all-to-all-start.1 = ((f32[2,64,8,256]{3,1,0,2:T(8,128)}), f32[2,64,8,256]{3,1,0,2:T(8,128)S(1)}, u32[]{:S(2)}, u32[]{:S(2)}) async-start(f32[2,64,8,256]{3,1,0,2:T(8,128)} %copy.38), calls=%async_computation.1 | async-start | bytes 2097152 | tf_op jit(solution)/shard_map/all_to_all | solution.py:33
  32.6 0.0 copy-done.3
  32.6 1.0 copy.65
  33.6 86.0 %all-to-all-done.1 = f32[2,64,8,256]{3,1,0,2:T(8,128)S(1)} async-done(((f32[2,64,8,256]{3,1,0,2:T(8,128)}), f32[2,64,8,256]{3,1,0,2:T(8,128)S(1)}, u32[]{:S(2)}, u32[]{:S(2)}) %all-to-all-start.1) | async-done | bytes 1048608 | tf_op jit(solution)/shard_map/all_to_all | solution.py:33
  119.6 26.6 %all-to-all-start = ((f32[1,64,8,256]{3,1,0,2:T(8,128)}), f32[1,64,8,256]{3,1,0,2:T(8,128)S(1)}, u32[]{:S(2)}, u32[]{:S(2)}) async-start(f32[1,64,8,256]{3,1,0,2:T(8,128)} %bitcast.104), calls=%async_computation | async-start | bytes 1048576 | tf_op jit(solution)/shard_map/all_to_all | solution.py:32
  146.2 0.0 copy-done.9
  146.2 0.0 copy-done.8
  146.2 0.1 copy.39
  146.3 0.0 copy-start.10
  146.3 52.1 %all-to-all-done = f32[1,64,8,256]{3,1,0,2:T(8,128)S(1)} async-done(((f32[1,64,8,256]{3,1,0,2:T(8,128)}), f32[1,64,8,256]{3,1,0,2:T(8,128)S(1)}, u32[]{:S(2)}, u32[]{:S(2)}) %all-to-all-start) | async-done | bytes 524320 | tf_op jit(solution)/shard_map/all_to_all | solution.py:32
  198.4 0.1 fusion.1
  198.6 3.1 %collective-permute-start = (f32[3,512,1,128]{3,1,0,2:T(8,128)S(1)}, f32[3,512,1,128]{3,1,0,2:T(8,128)S(1)}, u32[]{:S(2)}, u32[]{:S(2)}) collective-permute-start(f32[3,512,1,128]{3,1,0,2:T(8,128)S(1)} %get-tuple-element.16), channel_id=1, source_target_pairs={{0,1},{1,2},{2,3},{3,4},{4,5},{5,6},{6,7},{7,8},{8,9},{9,10},{10,1... | collective-permute-start | bytes 2359304 | tf_op jit(solution)/shard_map/ppermute | solution.py:16
  201.7 13.0 %collective-permute-start.1 = (f32[3,512,1,128]{3,1,0,2:T(8,128)S(1)}, f32[3,512,1,128]{3,1,0,2:T(8,128)S(1)}, u32[]{:S(2)}, u32[]{:S(2)}) collective-permute-start(f32[3,512,1,128]{3,1,0,2:T(8,128)S(1)} %get-tuple-element.17), channel_id=1, source_target_pairs={{1,0},{2,1},{3,2},{4,3},{5,4},{6,5},{7,6},{8,7},{9,8},{10,9},{11,1... | collective-permute-start | bytes 2359304 | tf_op jit(solution)/shard_map/ppermute | solution.py:17
  214.7 0.0 copy-done
  214.7 0.0 copy-done.10
  214.7 0.2 fusion
  214.9 0.1 convolution_bitcast_fusion
  215.0 0.2 slice_reduce_fusion
  215.2 0.2 slice_reduce_fusion.8
  215.4 0.8 slice_reduce_fusion.4
  216.2 12.5 %collective-permute-done = f32[3,512,1,128]{3,1,0,2:T(8,128)S(1)} collective-permute-done((f32[3,512,1,128]{3,1,0,2:T(8,128)S(1)}, f32[3,512,1,128]{3,1,0,2:T(8,128)S(1)}, u32[]{:S(2)}, u32[]{:S(2)}) %collective-permute-start) | collective-permute-done | bytes 786464 | tf_op jit(solution)/shard_map/ppermute | solution.py:16
  228.7 0.6 collective-permute-done.1
  229.3 0.2 fusion.35
  229.4 0.7 copy-done.1
  230.2 1.3 copy.43
  231.5 1.5 copy.44
  233.1 0.0 copy-start.2
  233.1 0.1 broadcast_subtract_fusion
  233.2 1.0 fusion.2
  234.2 1.0 fusion.13
  235.2 1.0 fusion.20
  236.3 0.0 copy-done.2
  236.3 0.3 pad_maximum_fusion
  236.6 1.5 slice.109
  238.2 1.9 copy.41
  240.1 0.0 copy-start.5
  240.1 0.7 fusion.16
  240.9 0.0 copy-done.6
  240.9 0.0 copy-done.7
  240.9 0.7 convolution_add_fusion.1
  241.6 0.7 convolution_add_fusion
  242.4 0.0 copy-start.4
  242.4 0.4 copy.53
  242.8 67.2 %all_to_all.54 = f32[512,1,256]{2,1,0:T(1,128)S(1)} all-to-all(f32[512,1,256]{2,1,0:T(1,128)S(1)} %copy.53), channel_id=1, replica_groups=mesh['member'=8,'region'=128] {'member'}, dimensions={0} | all-to-all | bytes 1048576 | tf_op jit(solution)/shard_map/all_to_all | solution.py:81
  310.1 0.2 copy_add_fusion
  310.3 1.1 copy.55
  (13 shorter events, 0.1 us)
Async XLA Ops:
  0.0 214.7 %copy-start = (f32[8]{0:T(128)S(1)}, f32[8]{0:T(128)}, u32[]{:S(2)}) copy-start(f32[8]{0:T(128)} %param.8) | copy-start | bytes 100
  0.0 32.6 %copy-start.3 = (f32[64,8,256]{2,1,0:T(8,128)S(1)}, f32[64,8,256]{2,1,0:T(8,128)}, u32[]{:S(2)}) copy-start(f32[64,8,256]{2,1,0:T(8,128)} %param.6) | copy-start | bytes 1572868
  2.6 143.6 %copy-start.9 = (s32[8]{0:T(128)S(1)}, s32[8]{0:T(128)}, u32[]{:S(2)}) copy-start(s32[8]{0:T(128)} %param.11) | copy-start | bytes 100
  2.6 143.6 %copy-start.8 = (s32[8,2]{0,1:T(2,128)S(1)}, s32[8,2]{0,1:T(2,128)}, u32[]{:S(2)}) copy-start(s32[8,2]{0,1:T(2,128)} %param.9) | copy-start | bytes 196
  2.6 117.0 %all-to-all-start.1 = ((f32[2,64,8,256]{3,1,0,2:T(8,128)}), f32[2,64,8,256]{3,1,0,2:T(8,128)S(1)}, u32[]{:S(2)}, u32[]{:S(2)}) async-start(f32[2,64,8,256]{3,1,0,2:T(8,128)} %copy.38), calls=%async_computation.1 | async-start | bytes 2097152 | tf_op jit(solution)/shard_map/all_to_all | solution.py:33
  119.6 78.9 %all-to-all-start = ((f32[1,64,8,256]{3,1,0,2:T(8,128)}), f32[1,64,8,256]{3,1,0,2:T(8,128)S(1)}, u32[]{:S(2)}, u32[]{:S(2)}) async-start(f32[1,64,8,256]{3,1,0,2:T(8,128)} %bitcast.104), calls=%async_computation | async-start | bytes 1048576 | tf_op jit(solution)/shard_map/all_to_all | solution.py:32
  146.3 68.4 %copy-start.10 = (s32[8]{0:T(128)S(1)}, s32[8]{0:T(128)}, u32[]{:S(2)}) copy-start(s32[8]{0:T(128)} %param.10) | copy-start | bytes 100
  198.6 30.1 %collective-permute-start = (f32[3,512,1,128]{3,1,0,2:T(8,128)S(1)}, f32[3,512,1,128]{3,1,0,2:T(8,128)S(1)}, u32[]{:S(2)}, u32[]{:S(2)}) collective-permute-start(f32[3,512,1,128]{3,1,0,2:T(8,128)S(1)} %get-tuple-element.16), channel_id=1, source_target_pairs={{0,1},{1,2},{2,3},{3,4},{4,5},{5,6},{6,7},{7,8},{8,9},{9,10},{10,1... | collective-permute-start | bytes 2359304 | tf_op jit(solution)/shard_map/ppermute | solution.py:16
  201.7 27.6 %collective-permute-start.1 = (f32[3,512,1,128]{3,1,0,2:T(8,128)S(1)}, f32[3,512,1,128]{3,1,0,2:T(8,128)S(1)}, u32[]{:S(2)}, u32[]{:S(2)}) collective-permute-start(f32[3,512,1,128]{3,1,0,2:T(8,128)S(1)} %get-tuple-element.17), channel_id=1, source_target_pairs={{1,0},{2,1},{3,2},{4,3},{5,4},{6,5},{7,6},{8,7},{9,8},{10,9},{11,1... | collective-permute-start | bytes 2359304 | tf_op jit(solution)/shard_map/ppermute | solution.py:17
  229.3 0.9 copy-start.1
  233.1 3.2 %copy-start.2 = (f32[3,512,1,128]{3,1,0,2:T(8,128)S(1)}, f32[3,512,1,128]{3,1,0,2:T(8,128)}, u32[]{:S(2)}) copy-start(f32[3,512,1,128]{3,1,0,2:T(8,128)} %copy-done.1) | copy-start | bytes 2359300
  238.2 2.7 copy-start.6
  238.2 2.7 copy-start.7
  240.1 1.5 copy-start.5
  242.4 67.7 %copy-start.4 = (f32[64,8,256]{2,1,0:T(8,128)S(1)}, f32[64,8,256]{2,1,0:T(8,128)}, u32[]{:S(2)}) copy-start(f32[64,8,256]{2,1,0:T(8,128)} %param.6) | copy-start | bytes 1572868
where the time goes:
time: 312 us; the launch traced here: 311 us
  waiting for transfers between devices  151 us (48%)
  starting transfers between devices  72.7 us (23%)
  blocking collectives  67.2 us (22%)
  local copies, waits for them, and re-layouts  13.4 us (4%)
  matrix products  5.63 us (2%)
    all_to_all x1, waiting for transfers between devices, local(): lax.all_to_all(weights, 'member', split_axis=2, concat_axis=1, tiled=True)  86 us
    all_to_all x1, blocking collectives, local(): lax.all_to_all(increment.reshape(ensemble, level_dev, column_count), 'mem...  67.2 us
    all_to_all x1, waiting for transfers between devices, local(): lax.all_to_all(members[None], 'member', split_axis=2, concat_axis=1, tile...  52.1 us
    all_to_all x1, starting transfers between devices, local(): lax.all_to_all(weights, 'member', split_axis=2, concat_axis=1, tiled=True)  30 us
    all_to_all x1, starting transfers between devices, local(): lax.all_to_all(members[None], 'member', split_axis=2, concat_axis=1, tile...  26.6 us
    ppermute x1, starting transfers between devices, extended_2(): after = lax.ppermute(leading, axis, down)  13 us
    ppermute x1, waiting for transfers between devices, extended_2(): before = lax.ppermute(last, axis, up)  12.5 us
  transfers between devices with their start and end apart: 4, of which 4 were waited for; matrix products, arithmetic and copies ran while one was open for 1% of the time, Pallas kernels for 0%

commit v1 on v0

v1 whole, which is shorter than its diff:
```python
import functools

import jax
import jax.numpy as jnp
from jax import lax
from jax.experimental import pallas as pl
from jax.experimental.pallas import tpu as pltpu
from jax.sharding import PartitionSpec as P

BLK = 128
CHIPS = 4
GROUPS = [[2 * z + c for z in range(CHIPS)] for c in range(2)]
SWAP = [(i, i ^ 1) for i in range(2 * CHIPS)]
NEAR = [z ^ 1 for z in range(CHIPS)]
CROSS = [CHIPS - 1 - z for z in range(CHIPS)]


def pairing(step):
    moves = []
    for z in range(CHIPS):
        for core in range(2):
            partner = (NEAR if (core + step) % 2 == 0 else CROSS)[z]
            moves.append((2 * z + core, 2 * partner + core))
    return moves


def split(x):
    high = x.astype(jnp.bfloat16)
    return high, (x - high.astype(jnp.float32)).astype(jnp.bfloat16)


def product(a, b, dims):
    (ah, al), (bh, bl) = a, b
    dot = functools.partial(
        lax.dot_general, dimension_numbers=(dims, ((), ())), preferred_element_type=jnp.float32
    )
    return dot(ah, bh) + (dot(ah, bl) + dot(al, bh))


ROWS = ((0,), (0,))
PLAIN = ((1,), (0,))
LANES = ((1,), (1,))


def anomaly_kernel(a_ref, b_ref, c_ref, out_ref):
    a, b, c = a_ref[...], b_ref[...], c_ref[...]
    count = a.shape[0] + b.shape[0] + c.shape[0]
    total = (
        jnp.sum(a, axis=0, keepdims=True)
        + jnp.sum(b, axis=0, keepdims=True)
        + jnp.sum(c, axis=0, keepdims=True)
    )
    mean = total / count
    out_ref[: a.shape[0]] = a - mean
    out_ref[a.shape[0] : a.shape[0] + b.shape[0]] = b - mean
    out_ref[a.shape[0] + b.shape[0] :] = c - mean


def anomalies_of(parts):
    count = sum(p.shape[0] for p in parts)
    return pl.pallas_call(
        anomaly_kernel, out_shape=jax.ShapeDtypeStruct((count, BLK), jnp.float32)
    )(*parts)


def covariance_kernel(first_ref, second_ref, after_ref, edge_ref, own_ref):
    first, second, after = (split(r[...]) for r in (first_ref, second_ref, after_ref))
    edge_ref[...] = product(second, after, ROWS)
    d0 = product(first, first, ROWS)
    d1 = product(second, second, ROWS)
    row = lax.broadcasted_iota(jnp.int32, (BLK, BLK), 0)
    col = lax.broadcasted_iota(jnp.int32, (BLK, BLK), 1)
    own_ref[:BLK] = jnp.where(row <= col, d0, d1)
    own_ref[BLK : 2 * BLK] = product(first, second, ROWS)
    diagonal = jnp.sum(jnp.where(row == col, d1, 0.0), axis=0, keepdims=True)
    own_ref[2 * BLK :] = jnp.broadcast_to(diagonal, (8, BLK))


def covariances(first, second, after):
    return pl.pallas_call(
        covariance_kernel,
        out_shape=(
            jax.ShapeDtypeStruct((BLK, BLK), jnp.float32),
            jax.ShapeDtypeStruct((2 * BLK + 8, BLK), jnp.float32),
        ),
    )(first, second, after)


def increment_kernel(coef_ref, w_ref, wl_ref, wr_ref, own_ref, edge_ref, left_ref, out_ref):
    row = lax.broadcasted_iota(jnp.int32, (BLK, BLK), 0)
    col = lax.broadcasted_iota(jnp.int32, (BLK, BLK), 1)
    packed = own_ref[0, :BLK]
    upper = jnp.where(row <= col, packed, 0.0)
    strict = jnp.where(row < col, packed, 0.0)
    lower = jnp.where(row > col, packed, 0.0)
    d0 = split(upper + strict.T)
    d1 = split(lower + lower.T + jnp.where(row == col, own_ref[0, 2 * BLK : 2 * BLK + 1], 0.0))
    c01 = split(own_ref[0, BLK : 2 * BLK])
    edge = split(edge_ref[0])
    left = split(left_ref[0])

    def mixed(t, j, block):
        at = t * 6 + j * 2
        part = pl.ds(block * BLK, BLK)
        return split(coef_ref[at] * w_ref[0, 0, :, part] + coef_ref[at + 1] * w_ref[1, 0, :, part])

    out_ref[0, :, :BLK] = (
        product(split(wl_ref[0]), left, PLAIN)
        + product(mixed(0, 1, 0), d0, PLAIN)
        + product(mixed(0, 2, 1), c01, LANES)
    )
    out_ref[0, :, BLK:] = (
        product(mixed(1, 0, 0), c01, PLAIN)
        + product(mixed(1, 1, 1), d1, PLAIN)
        + product(split(wr_ref[0]), edge, LANES)
    )


def increments(coefs, w, w_left, w_right, own, edge, left):
    levels, members = w.shape[1:3]
    per_level = lambda *shape: pl.BlockSpec((1,) + shape, lambda i: (i, 0, 0))
    return pl.pallas_call(
        increment_kernel,
        grid=(levels,),
        in_specs=[
            pl.BlockSpec(memory_space=pltpu.SMEM),
            pl.BlockSpec((2, 1, members, 2 * BLK), lambda i: (0, i, 0, 0)),
            per_level(members, BLK),
            per_level(members, BLK),
            per_level(2 * BLK + 8, BLK),
            per_level(BLK, BLK),
            per_level(BLK, BLK),
        ],
        out_specs=per_level(members, 2 * BLK),
        out_shape=jax.ShapeDtypeStruct((levels, members, 2 * BLK), jnp.float32),
    )(coefs, w, w_left, w_right, own, edge, left)


def one_hot(index, count):
    return (index[:, None] == jnp.arange(count, dtype=jnp.int32)[None, :]).astype(jnp.float32)


def pick(x, index):
    return lax.dynamic_index_in_dim(x, index, 0, keepdims=False)


def local(members, weights, taper_table, pair_blocks, pair_taper, pair_batch):
    member_loc, levels, _ = members.shape
    ensemble = member_loc * lax.axis_size("member")
    regions = lax.axis_size("region")
    right = [(i, (i + 1) % regions) for i in range(regions)]
    left = [(j, i) for i, j in right]
    me = lax.axis_index("member")
    chip, core = me // 2, me % 2
    half = levels // 2

    states = jnp.transpose(members, (1, 0, 2))
    mine = lax.dynamic_slice_in_dim(states, core * half, half, 0)
    theirs = lax.dynamic_slice_in_dim(states, (1 - core) * half, half, 0)
    states = jnp.concatenate([mine, lax.ppermute(theirs, "member", SWAP)], axis=1)

    near = chip ^ 1
    cross = CHIPS - 1 - chip
    one = jnp.where(core == 0, near, cross)
    two = jnp.where(core == 0, cross, near)
    both = CHIPS - 1 - near
    step_one, step_two = pairing(0), pairing(1)

    def to_owner(block):
        x = states[:, :, block * BLK : (block + 1) * BLK]
        got = lax.ppermute(jnp.stack([pick(x, one), pick(x, both)]), "member", step_one)
        last = lax.ppermute(jnp.stack([pick(x, two), got[1]]), "member", step_two)
        return anomalies_of([pick(x, chip), got[0], last.reshape(-1, BLK)])

    first = to_owner(0)
    second = to_owner(1)
    after = lax.ppermute(first, "region", left)

    tapers = jnp.dot(
        one_hot(pair_taper, taper_table.shape[0]), taper_table, precision=lax.Precision.HIGHEST
    ) / (ensemble - 1)
    targets = pair_blocks[:, 0]
    slot = targets * 6 + (pair_blocks[:, 1] - targets) * 2 + pair_batch
    coefs = jnp.sum(one_hot(slot, 12) * tapers[:, None], axis=0)
    from_right = lax.ppermute(coefs, "region", left)
    from_left = lax.ppermute(coefs, "region", right)

    w = jnp.transpose(weights, (0, 2, 1, 3))
    mine = lax.dynamic_slice_in_dim(w, core * half, half, 1)
    theirs = lax.dynamic_slice_in_dim(w, (1 - core) * half, half, 1)
    w = jnp.concatenate([mine, lax.ppermute(theirs, "member", SWAP)], axis=2)
    w_first, w_last = w[..., :BLK], w[..., BLK:]
    w_left = lax.ppermute(
        from_right[0] * w_last[0] + from_right[1] * w_last[1], "region", right
    )
    w_right = lax.ppermute(
        from_left[10] * w_first[0] + from_left[11] * w_first[1], "region", left
    )

    edge, own = covariances(first, second, after)
    edges = lax.all_gather(edge, "member", axis_index_groups=GROUPS)
    left_edges = lax.ppermute(edges, "region", right)
    owns = lax.all_gather(own, "member", axis_index_groups=GROUPS)

    change = increments(coefs, w, w_left, w_right, owns, edges, left_edges)
    kept = change[:, :member_loc]
    came = lax.ppermute(change[:, member_loc:], "member", SWAP)
    change = jnp.where(
        core == 0, jnp.concatenate([kept, came]), jnp.concatenate([came, kept])
    )
    return members + jnp.transpose(change, (1, 0, 2))


def solution(mesh):
    placed = (
        P("member", None, "region"),
        P(None, "member", None, "region"),
        P(),
        P("region", None),
        P("region"),
        P("region"),
    )
    return jax.shard_map(
        local, mesh=mesh, in_specs=placed, out_specs=P("member", None, "region"), check_vma=False
    )
```

time: 312 us -> 217 us (0.70)
  the two profiles are of different devices: /device:TPU:1 before, /device:TPU:127 now
where the time goes in v1:
time: 217 us; the launch traced here: 216 us
  blocking collectives  89.5 us (41%)
  starting transfers between devices  75.8 us (35%)
  waiting for transfers between devices  25.4 us (12%)
  Pallas kernels  10.2 us (5%)
  local copies, waits for them, and re-layouts  10 us (5%)
  other arithmetic  4.6 us (2%)
    all_gather x1, blocking collectives, local(): owns = lax.all_gather(own, 'member', axis_index_groups=GROUPS)  51.1 us
    all_gather x1, blocking collectives, local(): edges = lax.all_gather(edge, 'member', axis_index_groups=GROUPS)  38.4 us
    ppermute x2, starting transfers between devices, to_owner(): lax.ppermute(jnp.stack([pick(x, one), pick(x, both)]), 'member', step_one)  21.3 us
    ppermute x1, starting transfers between devices, local(): left_edges = lax.ppermute(edges, 'region', right)  15.2 us
    ppermute x2, starting transfers between devices, to_owner(): last = lax.ppermute(jnp.stack([pick(x, two), got[1]]), 'member', step_two)  13.2 us
    ppermute x2, waiting for transfers between devices, to_owner(): last = lax.ppermute(jnp.stack([pick(x, two), got[1]]), 'member', step_two)  12.3 us
    ppermute x2, waiting for transfers between devices, to_owner(): lax.ppermute(jnp.stack([pick(x, one), pick(x, both)]), 'member', step_one)  12 us
    ppermute x1, starting transfers between devices, local(): lax.ppermute(from_right[0] * w_last[0] + from_right[1] * w_last[1], 'regi...  8.79 us
  transfers between devices with their start and end apart: 13, of which 4 were waited for; matrix products, arithmetic and copies ran while one was open for 4% of the time, Pallas kernels for 3%

profile of v1, /device:TPU:127, one launch (start us, length us, event | category | flops | bytes accessed | tf_op | source)
XLA Modules:
  0.0 216.0 jit_solution(13032858368655040788)
XLA Ops:
  0.0 1.3 copy.17
  1.3 0.1 dynamic-slice_bitcast_fusion
  1.4 0.0 copy-start.11
  1.4 2.7 %collective-permute-start.5 = (f32[4,64,256]{2,1,0:T(8,128)S(1)}, f32[4,64,256]{2,1,0:T(8,128)S(1)}, u32[]{:S(2)}, u32[]{:S(2)}) collective-permute-start(f32[4,64,256]{2,1,0:T(8,128)S(1)} %get-tuple-element.19), channel_id=1, source_target_pairs={{0,128},{128,0},{256,384},{384,256},{512,640},{640,512},{768,896},... | collective-permute-start | bytes 786440 | tf_op jit(solution)/shard_map/ppermute | solution.py:160
  4.2 0.2 fusion
  4.4 0.1 select_reduce_fusion.coef_ref
  4.5 4.3 %collective-permute-start.3 = (f32[12]{0:T(128)S(1)}, f32[12]{0:T(128)S(1)}, u32[]{:S(2)}, u32[]{:S(2)}) collective-permute-start(f32[12]{0:T(128)S(1)} %select_reduce_fusion.coef_ref), channel_id=1, source_target_pairs={{0,1},{1,2},{2,3},{3,4},{4,5},{5,6},{6,7},{7,8},{8,9},{9,10},{10,1... | collective-permute-start | bytes 152 | tf_op jit(solution)/shard_map/ppermute | solution.py:186
  8.8 1.9 collective-permute-start.1
  10.7 0.2 constant_dynamic-slice_fusion.4
  10.9 0.1 copy.24
  11.0 2.2 %collective-permute-start = (f32[2,4,64,256]{3,2,1,0:T(8,128)S(1)}, f32[2,4,64,256]{3,2,1,0:T(8,128)S(1)}, u32[]{:S(2)}, u32[]{:S(2)}) collective-permute-start(f32[2,4,64,256]{3,2,1,0:T(8,128)S(1)} %bitcast.48), channel_id=1, source_target_pairs={{0,128},{128,0},{256,384},{384,256},{512,640},{640,512},{768,896},... | collective-permute-start | bytes 1572872 | tf_op jit(solution)/shard_map/ppermute | solution.py:191
  13.3 0.1 copy.25
  13.4 0.6 fusion.26
  14.1 0.7 constant_dynamic-slice_fusion
  14.8 19.3 %collective-permute-start.6 = (f32[2,128,128]{2,1,0:T(8,128)S(1)}, f32[2,128,128]{2,1,0:T(8,128)S(1)}, u32[]{:S(2)}, u32[]{:S(2)}) collective-permute-start(f32[2,128,128]{2,1,0:T(8,128)S(1)} %pad_maximum_fusion.1), channel_id=1, source_target_pairs={{0,256},{128,896},{256,0},{384,640},{512,768},{640,384},{768,512},... | collective-permute-start | bytes 393224 | tf_op jit(solution)/shard_map/ppermute | solution.py:171
  34.1 0.7 fusion.16
  34.8 1.9 collective-permute-start.8
  36.7 8.8 %collective-permute-done.6 = f32[2,128,128]{2,1,0:T(8,128)S(1)} collective-permute-done((f32[2,128,128]{2,1,0:T(8,128)S(1)}, f32[2,128,128]{2,1,0:T(8,128)S(1)}, u32[]{:S(2)}, u32[]{:S(2)}) %collective-permute-start.6) | collective-permute-done | bytes 131104 | tf_op jit(solution)/shard_map/ppermute | solution.py:171
  45.5 0.6 fusion.25
  46.2 6.7 %collective-permute-start.7 = (f32[2,128,128]{2,1,0:T(8,128)S(1)}, f32[2,128,128]{2,1,0:T(8,128)S(1)}, u32[]{:S(2)}, u32[]{:S(2)}) collective-permute-start(f32[2,128,128]{2,1,0:T(8,128)S(1)} %pad_maximum_fusion.2), channel_id=1, source_target_pairs={{0,768},{128,384},{256,512},{384,128},{512,256},{640,896},{768,0},... | collective-permute-start | bytes 393224 | tf_op jit(solution)/shard_map/ppermute | solution.py:172
  52.9 3.2 %collective-permute-done.8 = f32[2,128,128]{2,1,0:T(8,128)S(1)} collective-permute-done((f32[2,128,128]{2,1,0:T(8,128)S(1)}, f32[2,128,128]{2,1,0:T(8,128)S(1)}, u32[]{:S(2)}, u32[]{:S(2)}) %collective-permute-start.8) | collective-permute-done | bytes 131104 | tf_op jit(solution)/shard_map/ppermute | solution.py:171
  56.0 0.6 fusion.24
  56.7 12.2 %collective-permute-done.7 = f32[2,128,128]{2,1,0:T(8,128)S(1)} collective-permute-done((f32[2,128,128]{2,1,0:T(8,128)S(1)}, f32[2,128,128]{2,1,0:T(8,128)S(1)}, u32[]{:S(2)}, u32[]{:S(2)}) %collective-permute-start.7) | collective-permute-done | bytes 131104 | tf_op jit(solution)/shard_map/ppermute | solution.py:172
  68.9 0.6 copy-done.10
  69.6 1.7 shard_map.64.first_ref
  71.3 1.9 collective-permute-start.10
  73.3 6.6 %collective-permute-start.9 = (f32[2,128,128]{2,1,0:T(8,128)S(1)}, f32[2,128,128]{2,1,0:T(8,128)S(1)}, u32[]{:S(2)}, u32[]{:S(2)}) collective-permute-start(f32[2,128,128]{2,1,0:T(8,128)S(1)} %pad_maximum_fusion.4), channel_id=1, source_target_pairs={{0,768},{128,384},{256,512},{384,128},{512,256},{640,896},{768,0},... | collective-permute-start | bytes 393224 | tf_op jit(solution)/shard_map/ppermute | solution.py:172
  79.8 0.6 fusion.27
  80.4 2.5 %fusion.13 = (f32[4,128,128]{2,1,0:T(8,128)S(1)}, f32[4,128,128]{2,1,0:T(8,128)S(1)}) fusion(f32[2,4,64,256]{3,2,1,0:T(8,128)S(1)} %bitcast.43, f32[2,4,64,256]{3,2,1,0:T(8,128)S(1)} %collective-permute-done, f32[]{:T(128)} %bitcast.9, f32[]{:T(128)} %bitcast.8, f32[]{:T(128)} %bitcast.6, f32[]{:T(128)} %bitcast.5), kind=kLoop, calls=%fused_computation.28 | loop fusion | flops 655360 | bytes 1572880 | tf_op jit(solution)/shard_map/add | solution.py:197
  83.0 8.8 %collective-permute-start.2 = (f32[4,128,128]{2,1,0:T(8,128)S(1)}, f32[4,128,128]{2,1,0:T(8,128)S(1)}, u32[]{:S(2)}, u32[]{:S(2)}) collective-permute-start(f32[4,128,128]{2,1,0:T(8,128)S(1)} %get-tuple-element.10), channel_id=1, source_target_pairs={{0,1},{1,2},{2,3},{3,4},{4,5},{5,6},{6,7},{7,8},{8,9},{9,10},{10,1... | collective-permute-start | bytes 786440 | tf_op jit(solution)/shard_map/ppermute | solution.py:193
  91.8 1.9 collective-permute-start.4
  93.7 0.6 copy-done.9
  94.3 1.7 shard_map.65.second_ref
  96.1 0.7 copy-done.4
  96.8 2.4 %shard_map.66 = (f32[128,128]{1,0:T(8,128)}, f32[264,128]{1,0:T(8,128)}) custom-call(f32[512,128]{1,0:T(8,128)} %shard_map.64.first_ref, f32[512,128]{1,0:T(8,128)} %shard_map.65.second_ref, f32[512,128]{1,0:T(8,128)} %copy-done.4), custom_call_target="tpu_custom_call" | custom-call | tf_op jit(solution)/shard_map/pallas_call | solution.py:80
  99.2 38.4 %all-gather.1 = f32[512,128]{1,0:T(8,128)S(1)} all-gather(f32[128,128]{1,0:T(8,128)} %get-tuple-element.8), channel_id=3, replica_groups={{0,256,512,768},{128,384,640,896},{1,257,513,769},{129,385,641,897},{2,..., dimensions={0}, use_global_device_ids=true | all-gather | bytes 327680 | tf_op jit(solution)/shard_map/all_gather | solution.py:201
  137.5 15.2 %collective-permute-start.11 = (f32[4,128,128]{2,1,0:T(8,128)S(1)}, f32[4,128,128]{2,1,0:T(8,128)S(1)}, u32[]{:S(2)}, u32[]{:S(2)}) collective-permute-start(f32[4,128,128]{2,1,0:T(8,128)S(1)} %bitcast.46), channel_id=1, source_target_pairs={{0,1},{1,2},{2,3},{3,4},{4,5},{5,6},{6,7},{7,8},{8,9},{9,10},{10,1... | collective-permute-start | bytes 786440 | tf_op jit(solution)/shard_map/ppermute | solution.py:202
  152.7 1.1 pad_maximum_fusion.w_ref
  153.8 51.1 %all-gather = f32[1056,128]{1,0:T(8,128)} all-gather(f32[264,128]{1,0:T(8,128)S(1)} %copy-done.8), channel_id=2, replica_groups={{0,256,512,768},{128,384,640,896},{1,257,513,769},{129,385,641,897},{2,..., dimensions={0}, use_global_device_ids=true | all-gather | bytes 675840 | tf_op jit(solution)/shard_map/all_gather | solution.py:203
  204.9 0.7 copy-done.5
  205.6 0.1 copy-done.6
  205.7 0.1 copy-done.7
  205.8 4.3 %shard_map.67 = f32[4,128,256]{2,1,0:T(8,128)} custom-call(f32[12]{0:T(128)} %copy-done.13, f32[2,4,128,256]{3,2,1,0:T(8,128)} %pad_maximum_fusion.w_ref, f32[4,128,128]{2,1,0:T(8,128)} %copy-done.5, f32[4,128,128]{2,1,0:T(8,128)} %copy-done.6, f32[4,264,128]{2,1,0:T(8,128)} %bitcast.45, f32[4,128,128]{2,1,0:T(8,128)} %bitcast.47, f32[4,128,128]{2,1,0:T(8,128)} %copy-done.7), custom_call_target="tpu_custom_call" | custom-call | tf_op jit(solution)/shard_map/pallas_call | solution.py:122
  210.1 1.1 fusion.23
  211.3 2.3 %collective-permute-start.12 = (f32[4,64,256]{2,1,0:T(8,128)S(1)}, f32[4,64,256]{2,1,0:T(8,128)S(1)}, u32[]{:S(2)}, u32[]{:S(2)}) collective-permute-start(f32[4,64,256]{2,1,0:T(8,128)S(1)} %get-tuple-element.14), channel_id=1, source_target_pairs={{0,128},{128,0},{256,384},{384,256},{512,640},{640,512},{768,896},... | collective-permute-start | bytes 786440 | tf_op jit(solution)/shard_map/ppermute | solution.py:207
  213.6 1.1 collective-permute-done.12
  214.7 0.2 fusion.2
  214.9 1.1 copy.18
  (38 shorter events, 0.1 us)
Async XLA Ops:
  0.0 4.1 %copy-start = (f32[8]{0:T(128)S(1)}, f32[8]{0:T(128)}, u32[]{:S(2)}) copy-start(f32[8]{0:T(128)} %param.8) | copy-start | bytes 100
  0.0 10.7 %copy-start.2 = (f32[2,64,8,256]{3,2,1,0:T(8,128)S(1)}, f32[2,64,8,256]{3,2,1,0:T(8,128)}, u32[]{:S(2)}) copy-start(f32[2,64,8,256]{3,2,1,0:T(8,128)} %param.7) | copy-start | bytes 3145732
  1.4 2.8 %copy-start.14 = (s32[8]{0:T(128)S(1)}, s32[8]{0:T(128)}, u32[]{:S(2)}) copy-start(s32[8]{0:T(128)} %param.10) | copy-start | bytes 100
  1.4 3.0 %copy-start.11 = (s32[8,2]{0,1:T(2,128)S(1)}, s32[8,2]{0,1:T(2,128)}, u32[]{:S(2)}) copy-start(s32[8,2]{0,1:T(2,128)} %param.9) | copy-start | bytes 196
  1.4 2.9 %copy-start.12 = (s32[8]{0:T(128)S(1)}, s32[8]{0:T(128)}, u32[]{:S(2)}) copy-start(s32[8]{0:T(128)} %param.11) | copy-start | bytes 100
  1.4 12.7 %collective-permute-start.5 = (f32[4,64,256]{2,1,0:T(8,128)S(1)}, f32[4,64,256]{2,1,0:T(8,128)S(1)}, u32[]{:S(2)}, u32[]{:S(2)}) collective-permute-start(f32[4,64,256]{2,1,0:T(8,128)S(1)} %get-tuple-element.19), channel_id=1, source_target_pairs={{0,128},{128,0},{256,384},{384,256},{512,640},{640,512},{768,896},... | collective-permute-start | bytes 786440 | tf_op jit(solution)/shard_map/ppermute | solution.py:160
  4.5 6.5 %copy-start.13 = (f32[12]{0:T(128)}, f32[12]{0:T(128)S(1)}, u32[]{:S(2)}) copy-start(f32[12]{0:T(128)S(1)} %select_reduce_fusion.coef_ref) | copy-start | bytes 148
  4.5 9.0 %collective-permute-start.3 = (f32[12]{0:T(128)S(1)}, f32[12]{0:T(128)S(1)}, u32[]{:S(2)}, u32[]{:S(2)}) collective-permute-start(f32[12]{0:T(128)S(1)} %select_reduce_fusion.coef_ref), channel_id=1, source_target_pairs={{0,1},{1,2},{2,3},{3,4},{4,5},{5,6},{6,7},{7,8},{8,9},{9,10},{10,1... | collective-permute-start | bytes 152 | tf_op jit(solution)/shard_map/ppermute | solution.py:186
  8.8 71.0 %collective-permute-start.1 = (f32[12]{0:T(128)S(1)}, f32[12]{0:T(128)S(1)}, u32[]{:S(2)}, u32[]{:S(2)}) collective-permute-start(f32[12]{0:T(128)S(1)} %select_reduce_fusion.coef_ref), channel_id=1, source_target_pairs={{1,0},{2,1},{3,2},{4,3},{5,4},{6,5},{7,6},{8,7},{9,8},{10,9},{11,1... | collective-permute-start | bytes 152 | tf_op jit(solution)/shard_map/ppermute | solution.py:185
  11.0 69.4 %collective-permute-start = (f32[2,4,64,256]{3,2,1,0:T(8,128)S(1)}, f32[2,4,64,256]{3,2,1,0:T(8,128)S(1)}, u32[]{:S(2)}, u32[]{:S(2)}) collective-permute-start(f32[2,4,64,256]{3,2,1,0:T(8,128)S(1)} %bitcast.48), channel_id=1, source_target_pairs={{0,128},{128,0},{256,384},{384,256},{512,640},{640,512},{768,896},... | collective-permute-start | bytes 1572872 | tf_op jit(solution)/shard_map/ppermute | solution.py:191
  14.8 30.8 %collective-permute-start.6 = (f32[2,128,128]{2,1,0:T(8,128)S(1)}, f32[2,128,128]{2,1,0:T(8,128)S(1)}, u32[]{:S(2)}, u32[]{:S(2)}) collective-permute-start(f32[2,128,128]{2,1,0:T(8,128)S(1)} %pad_maximum_fusion.1), channel_id=1, source_target_pairs={{0,256},{128,896},{256,0},{384,640},{512,768},{640,384},{768,512},... | collective-permute-start | bytes 393224 | tf_op jit(solution)/shard_map/ppermute | solution.py:171
  34.8 21.2 %collective-permute-start.8 = (f32[2,128,128]{2,1,0:T(8,128)S(1)}, f32[2,128,128]{2,1,0:T(8,128)S(1)}, u32[]{:S(2)}, u32[]{:S(2)}) collective-permute-start(f32[2,128,128]{2,1,0:T(8,128)S(1)} %pad_maximum_fusion.3), channel_id=1, source_target_pairs={{0,256},{128,896},{256,0},{384,640},{512,768},{640,384},{768,512},... | collective-permute-start | bytes 393224 | tf_op jit(solution)/shard_map/ppermute | solution.py:171
  46.2 22.7 %collective-permute-start.7 = (f32[2,128,128]{2,1,0:T(8,128)S(1)}, f32[2,128,128]{2,1,0:T(8,128)S(1)}, u32[]{:S(2)}, u32[]{:S(2)}) collective-permute-start(f32[2,128,128]{2,1,0:T(8,128)S(1)} %pad_maximum_fusion.2), channel_id=1, source_target_pairs={{0,768},{128,384},{256,512},{384,128},{512,256},{640,896},{768,0},... | collective-permute-start | bytes 393224 | tf_op jit(solution)/shard_map/ppermute | solution.py:172
  68.9 0.6 copy-start.10
  71.3 24.8 %collective-permute-start.10 = (f32[512,128]{1,0:T(8,128)}, f32[512,128]{1,0:T(8,128)S(1)}, u32[]{:S(2)}, u32[]{:S(2)}) collective-permute-start(f32[512,128]{1,0:T(8,128)} %shard_map.64.first_ref), channel_id=1, source_target_pairs={{1,0},{2,1},{3,2},{4,3},{5,4},{6,5},{7,6},{8,7},{9,8},{10,9},{11,1... | collective-permute-start | bytes 786440 | tf_op jit(solution)/shard_map/ppermute | solution.py:177
  73.3 20.4 %collective-permute-start.9 = (f32[2,128,128]{2,1,0:T(8,128)S(1)}, f32[2,128,128]{2,1,0:T(8,128)S(1)}, u32[]{:S(2)}, u32[]{:S(2)}) collective-permute-start(f32[2,128,128]{2,1,0:T(8,128)S(1)} %pad_maximum_fusion.4), channel_id=1, source_target_pairs={{0,768},{128,384},{256,512},{384,128},{512,256},{640,896},{768,0},... | collective-permute-start | bytes 393224 | tf_op jit(solution)/shard_map/ppermute | solution.py:172
  83.0 121.9 %collective-permute-start.2 = (f32[4,128,128]{2,1,0:T(8,128)S(1)}, f32[4,128,128]{2,1,0:T(8,128)S(1)}, u32[]{:S(2)}, u32[]{:S(2)}) collective-permute-start(f32[4,128,128]{2,1,0:T(8,128)S(1)} %get-tuple-element.10), channel_id=1, source_target_pairs={{0,1},{1,2},{2,3},{3,4},{4,5},{5,6},{6,7},{7,8},{8,9},{9,10},{10,1... | collective-permute-start | bytes 786440 | tf_op jit(solution)/shard_map/ppermute | solution.py:193
  91.8 113.1 %collective-permute-start.4 = (f32[4,128,128]{2,1,0:T(8,128)S(1)}, f32[4,128,128]{2,1,0:T(8,128)S(1)}, u32[]{:S(2)}, u32[]{:S(2)}) collective-permute-start(f32[4,128,128]{2,1,0:T(8,128)S(1)} %get-tuple-element.9), channel_id=1, source_target_pairs={{1,0},{2,1},{3,2},{4,3},{5,4},{6,5},{7,6},{8,7},{9,8},{10,9},{11,1... | collective-permute-start | bytes 786440 | tf_op jit(solution)/shard_map/ppermute | solution.py:196
  93.7 0.7 copy-start.9
  96.1 0.7 copy-start.4
  137.5 16.3 %copy-start.3 = (f32[512,128]{1,0:T(8,128)}, f32[512,128]{1,0:T(8,128)S(1)}, u32[]{:S(2)}) copy-start(f32[512,128]{1,0:T(8,128)S(1)} %all-gather.1) | copy-start | bytes 786436
  137.5 16.3 %copy-start.8 = (f32[264,128]{1,0:T(8,128)S(1)}, f32[264,128]{1,0:T(8,128)}, u32[]{:S(2)}) copy-start(f32[264,128]{1,0:T(8,128)} %get-tuple-element.7) | copy-start | bytes 405508
  137.5 67.4 %collective-permute-start.11 = (f32[4,128,128]{2,1,0:T(8,128)S(1)}, f32[4,128,128]{2,1,0:T(8,128)S(1)}, u32[]{:S(2)}, u32[]{:S(2)}) collective-permute-start(f32[4,128,128]{2,1,0:T(8,128)S(1)} %bitcast.46), channel_id=1, source_target_pairs={{0,1},{1,2},{2,3},{3,4},{4,5},{5,6},{6,7},{7,8},{8,9},{9,10},{10,1... | collective-permute-start | bytes 786440 | tf_op jit(solution)/shard_map/ppermute | solution.py:202
  204.9 0.7 copy-start.5
  204.9 0.8 copy-start.6
  204.9 0.9 copy-start.7
  210.1 4.6 %copy-start.1 = (f32[64,8,256]{2,1,0:T(8,128)S(1)}, f32[64,8,256]{2,1,0:T(8,128)}, u32[]{:S(2)}) copy-start(f32[64,8,256]{2,1,0:T(8,128)} %param.6) | copy-start | bytes 1572868
  211.3 3.5 %collective-permute-start.12 = (f32[4,64,256]{2,1,0:T(8,128)S(1)}, f32[4,64,256]{2,1,0:T(8,128)S(1)}, u32[]{:S(2)}, u32[]{:S(2)}) collective-permute-start(f32[4,64,256]{2,1,0:T(8,128)S(1)} %get-tuple-element.14), channel_id=1, source_target_pairs={{0,128},{128,0},{256,384},{384,256},{512,640},{640,512},{768,896},... | collective-permute-start | bytes 786440 | tf_op jit(solution)/shard_map/ppermute | solution.py:207

commit v2 on v1

--- a/solution.py
+++ b/solution.py
@@ -42,30 +42,16 @@
 LANES = ((1,), (1,))
 
 
-def anomaly_kernel(a_ref, b_ref, c_ref, out_ref):
-    a, b, c = a_ref[...], b_ref[...], c_ref[...]
-    count = a.shape[0] + b.shape[0] + c.shape[0]
-    total = (
-        jnp.sum(a, axis=0, keepdims=True)
-        + jnp.sum(b, axis=0, keepdims=True)
-        + jnp.sum(c, axis=0, keepdims=True)
-    )
-    mean = total / count
-    out_ref[: a.shape[0]] = a - mean
-    out_ref[a.shape[0] : a.shape[0] + b.shape[0]] = b - mean
-    out_ref[a.shape[0] + b.shape[0] :] = c - mean
-
-
-def anomalies_of(parts):
-    count = sum(p.shape[0] for p in parts)
-    return pl.pallas_call(
-        anomaly_kernel, out_shape=jax.ShapeDtypeStruct((count, BLK), jnp.float32)
-    )(*parts)
-
-
-def covariance_kernel(first_ref, second_ref, after_ref, edge_ref, own_ref):
-    first, second, after = (split(r[...]) for r in (first_ref, second_ref, after_ref))
+def covariance_kernel(first_ref, kept_ref, got_ref, last_ref, after_ref, edge_ref, own_ref):
+    def centred(*parts):
+        count = sum(p.shape[0] for p in parts)
+        mean = sum(jnp.sum(p, axis=0, keepdims=True) for p in parts) / count
+        return split(jnp.concatenate([p - mean for p in parts], axis=0))
+
+    second = centred(kept_ref[...], got_ref[...], last_ref[...])
+    after = centred(after_ref[...])
     edge_ref[...] = product(second, after, ROWS)
+    first = centred(first_ref[...])
     d0 = product(first, first, ROWS)
     d1 = product(second, second, ROWS)
     row = lax.broadcasted_iota(jnp.int32, (BLK, BLK), 0)
@@ -76,17 +62,22 @@
     own_ref[2 * BLK :] = jnp.broadcast_to(diagonal, (8, BLK))
 
 
-def covariances(first, second, after):
+LONG = pl.CostEstimate(flops=50_000_000_000, bytes_accessed=200_000_000, transcendentals=0)
+TINY = pl.CostEstimate(flops=1000, bytes_accessed=1000, transcendentals=0)
+
+
+def covariances(*parts):
     return pl.pallas_call(
         covariance_kernel,
         out_shape=(
             jax.ShapeDtypeStruct((BLK, BLK), jnp.float32),
             jax.ShapeDtypeStruct((2 * BLK + 8, BLK), jnp.float32),
         ),
-    )(first, second, after)
-
-
-def increment_kernel(coef_ref, w_ref, wl_ref, wr_ref, own_ref, edge_ref, left_ref, out_ref):
+        cost_estimate=TINY,
+    )(*parts)
+
+
+def increment_kernel(coef_ref, w_ref, wl_ref, wr_ref, own_ref, edge_ref, left_ref, kept_ref, sent_ref):
     row = lax.broadcasted_iota(jnp.int32, (BLK, BLK), 0)
     col = lax.broadcasted_iota(jnp.int32, (BLK, BLK), 1)
     packed = own_ref[0, :BLK]
@@ -99,41 +90,70 @@
     edge = split(edge_ref[0])
     left = split(left_ref[0])
 
-    def mixed(t, j, block):
+    def mixed(ref, t, j, part=slice(None)):
         at = t * 6 + j * 2
-        part = pl.ds(block * BLK, BLK)
-        return split(coef_ref[at] * w_ref[0, 0, :, part] + coef_ref[at + 1] * w_ref[1, 0, :, part])
-
-    out_ref[0, :, :BLK] = (
-        product(split(wl_ref[0]), left, PLAIN)
-        + product(mixed(0, 1, 0), d0, PLAIN)
-        + product(mixed(0, 2, 1), c01, LANES)
-    )
-    out_ref[0, :, BLK:] = (
-        product(mixed(1, 0, 0), c01, PLAIN)
-        + product(mixed(1, 1, 1), d1, PLAIN)
-        + product(split(wr_ref[0]), edge, LANES)
-    )
+        return split(coef_ref[at] * ref[0, 0, :, part] + coef_ref[at + 1] * ref[1, 0, :, part])
+
+    here, there = slice(0, BLK), slice(BLK, 2 * BLK)
+    zero = (
+        product(mixed(wl_ref, 0, 0), left, PLAIN)
+        + product(mixed(w_ref, 0, 1, here), d0, PLAIN)
+        + product(mixed(w_ref, 0, 2, there), c01, LANES)
+    )
+    one = (
+        product(mixed(w_ref, 1, 0, here), c01, PLAIN)
+        + product(mixed(w_ref, 1, 1, there), d1, PLAIN)
+        + product(mixed(wr_ref, 1, 2), edge, LANES)
+    )
+    keep = kept_ref.shape[1]
+    for ref, rows in ((kept_ref, slice(0, keep)), (sent_ref, slice(keep, 2 * keep))):
+        ref[0, :, here] = zero[rows]
+        ref[0, :, there] = one[rows]
 
 
 def increments(coefs, w, w_left, w_right, own, edge, left):
     levels, members = w.shape[1:3]
     per_level = lambda *shape: pl.BlockSpec((1,) + shape, lambda i: (i, 0, 0))
+    both = lambda width: pl.BlockSpec((2, 1, members, width), lambda i: (0, i, 0, 0))
+    half = jax.ShapeDtypeStruct((levels, members // 2, 2 * BLK), jnp.float32)
     return pl.pallas_call(
         increment_kernel,
         grid=(levels,),
         in_specs=[
             pl.BlockSpec(memory_space=pltpu.SMEM),
-            pl.BlockSpec((2, 1, members, 2 * BLK), lambda i: (0, i, 0, 0)),
-            per_level(members, BLK),
-            per_level(members, BLK),
+            both(2 * BLK),
+            both(BLK),
+            both(BLK),
             per_level(2 * BLK + 8, BLK),
             per_level(BLK, BLK),
             per_level(BLK, BLK),
         ],
-        out_specs=per_level(members, 2 * BLK),
-        out_shape=jax.ShapeDtypeStruct((levels, members, 2 * BLK), jnp.float32),
+        out_specs=(per_level(members // 2, 2 * BLK),) * 2,
+        out_shape=(half, half),
+        cost_estimate=TINY,
     )(coefs, w, w_left, w_right, own, edge, left)
+
+
+def gather_kernel(mine_ref, got_ref, w_ref, low_ref, high_ref):
+    keep = mine_ref.shape[2]
+    for ref, rows in ((mine_ref, slice(0, keep)), (got_ref, slice(keep, 2 * keep))):
+        w_ref[0, :, rows] = ref[0]
+        low_ref[0, :, rows] = ref[0, :, :, :BLK]
+        high_ref[0, :, rows] = ref[0, :, :, BLK:]
+
+
+def gathered(mine, got):
+    batches, levels, members, width = mine.shape
+    block = lambda m, c: pl.BlockSpec((1, levels, m, c), lambda i: (i, 0, 0, 0))
+    shape = lambda c: jax.ShapeDtypeStruct((batches, levels, 2 * members, c), jnp.float32)
+    return pl.pallas_call(
+        gather_kernel,
+        grid=(batches,),
+        in_specs=[block(members, width)] * 2,
+        out_specs=(block(2 * members, width),) + (block(2 * members, BLK),) * 2,
+        out_shape=(shape(width), shape(BLK), shape(BLK)),
+        cost_estimate=LONG,
+    )(mine, got)
 
 
 def one_hot(index, count):
@@ -157,6 +177,7 @@
     states = jnp.transpose(members, (1, 0, 2))
     mine = lax.dynamic_slice_in_dim(states, core * half, half, 0)
     theirs = lax.dynamic_slice_in_dim(states, (1 - core) * half, half, 0)
+    theirs, weights = lax.optimization_barrier((theirs, weights))
     states = jnp.concatenate([mine, lax.ppermute(theirs, "member", SWAP)], axis=1)
 
     near = chip ^ 1
@@ -170,9 +191,9 @@
         x = states[:, :, block * BLK : (block + 1) * BLK]
         got = lax.ppermute(jnp.stack([pick(x, one), pick(x, both)]), "member", step_one)
         last = lax.ppermute(jnp.stack([pick(x, two), got[1]]), "member", step_two)
-        return anomalies_of([pick(x, chip), got[0], last.reshape(-1, BLK)])
-
-    first = to_owner(0)
+        return pick(x, chip), got[0], last.reshape(-1, BLK)
+
+    first = jnp.concatenate(to_owner(0))
     second = to_owner(1)
     after = lax.ppermute(first, "region", left)
 
@@ -182,29 +203,21 @@
     targets = pair_blocks[:, 0]
     slot = targets * 6 + (pair_blocks[:, 1] - targets) * 2 + pair_batch
     coefs = jnp.sum(one_hot(slot, 12) * tapers[:, None], axis=0)
-    from_right = lax.ppermute(coefs, "region", left)
-    from_left = lax.ppermute(coefs, "region", right)
 
     w = jnp.transpose(weights, (0, 2, 1, 3))
     mine = lax.dynamic_slice_in_dim(w, core * half, half, 1)
     theirs = lax.dynamic_slice_in_dim(w, (1 - core) * half, half, 1)
-    w = jnp.concatenate([mine, lax.ppermute(theirs, "member", SWAP)], axis=2)
-    w_first, w_last = w[..., :BLK], w[..., BLK:]
-    w_left = lax.ppermute(
-        from_right[0] * w_last[0] + from_right[1] * w_last[1], "region", right
-    )
-    w_right = lax.ppermute(
-        from_left[10] * w_first[0] + from_left[11] * w_first[1], "region", left
-    )
-
-    edge, own = covariances(first, second, after)
+    w, low, high = gathered(mine, lax.ppermute(theirs, "member", SWAP))
+    w_left = lax.ppermute(high, "region", right)
+    w_right = lax.ppermute(low, "region", left)
+
+    edge, own = covariances(first, *second, after)
     edges = lax.all_gather(edge, "member", axis_index_groups=GROUPS)
     left_edges = lax.ppermute(edges, "region", right)
     owns = lax.all_gather(own, "member", axis_index_groups=GROUPS)
 
-    change = increments(coefs, w, w_left, w_right, owns, edges, left_edges)
-    kept = change[:, :member_loc]
-    came = lax.ppermute(change[:, member_loc:], "member", SWAP)
+    kept, sent = increments(coefs, w, w_left, w_right, owns, edges, left_edges)
+    came = lax.ppermute(sent, "member", SWAP)
     change = jnp.where(
         core == 0, jnp.concatenate([kept, came]), jnp.concatenate([came, kept])
     )

time: 217 us -> 213 us (0.982)
  the two profiles are of different devices: /device:TPU:127 before, /device:TPU:1 now
where the time goes in v2:
time: 213 us
  starting transfers between devices  101 us (47%)
  blocking collectives  78.9 us (37%)
  waiting for transfers between devices  12.6 us (6%)
  Pallas kernels  9.48 us (4%)
  local copies, waits for them, and re-layouts  7.54 us (4%)
  other arithmetic  2.65 us (1%)
    all_gather x1, blocking collectives, local(): edges = lax.all_gather(edge, 'member', axis_index_groups=GROUPS)  41.6 us
    all_gather x1, blocking collectives, local(): owns = lax.all_gather(own, 'member', axis_index_groups=GROUPS)  37.3 us
    ppermute x2, starting transfers between devices, to_owner(): last = lax.ppermute(jnp.stack([pick(x, two), got[1]]), 'member', step_two)  32.1 us
    ppermute x1, starting transfers between devices, local(): came = lax.ppermute(sent, 'member', SWAP)  17 us
    ppermute x1, starting transfers between devices, local(): lax.ppermute(theirs, 'member', SWAP)  16.1 us
    ppermute x2, starting transfers between devices, to_owner(): lax.ppermute(jnp.stack([pick(x, one), pick(x, both)]), 'member', step_one)  14 us
    ppermute x1, starting transfers between devices, local(): w_right = lax.ppermute(low, 'region', left)  12.7 us
    ppermute x2, waiting for transfers between devices, to_owner(): lax.ppermute(jnp.stack([pick(x, one), pick(x, both)]), 'member', step_one)  11.2 us
  transfers between devices with their start and end apart: 11, of which 3 were waited for; matrix products, arithmetic and copies ran while one was open for 2% of the time, Pallas kernels for 2%

profile of v2, /device:TPU:1, one launch (start us, length us, event | category | flops | bytes accessed | tf_op | source)
XLA Modules:
  0.0 212.8 jit_solution(7140132470002179798)
XLA Ops:
  0.0 1.3 copy.17
  1.4 16.1 %collective-permute-start.3 = (f32[4,64,256]{2,1,0:T(8,128)S(1)}, f32[4,64,256]{2,1,0:T(8,128)S(1)}, u32[]{:S(2)}, u32[]{:S(2)}) collective-permute-start(f32[4,64,256]{2,1,0:T(8,128)S(1)} %get-tuple-element.18), channel_id=1, source_target_pairs={{0,128},{128,0},{256,384},{384,256},{512,640},{640,512},{768,896},... | collective-permute-start | bytes 786440 | tf_op jit(solution)/shard_map/ppermute | solution.py:181
  17.4 0.0 copy-done.3
  17.4 0.3 copy.14
  17.8 0.9 dynamic-slice_bitcast_fusion
  18.6 1.9 collective-permute-start
  20.6 0.0 copy-start.11
  20.6 0.0 copy-start.12
  20.6 0.7 copy-done.11
  21.3 0.0 collective-permute-done.3
  21.4 10.1 %collective-permute-start.4 = (f32[2,128,128]{2,1,0:T(8,128)S(1)}, f32[2,128,128]{2,1,0:T(8,128)S(1)}, u32[]{:S(2)}, u32[]{:S(2)}) collective-permute-start(f32[2,128,128]{2,1,0:T(8,128)S(1)} %pad_maximum_fusion.1), channel_id=1, source_target_pairs={{0,256},{128,896},{256,0},{384,640},{512,768},{640,384},{768,512},... | collective-permute-start | bytes 393224 | tf_op jit(solution)/shard_map/ppermute | solution.py:192
  31.5 0.7 fusion.4
  32.1 3.9 %collective-permute-start.6 = (f32[2,128,128]{2,1,0:T(8,128)S(1)}, f32[2,128,128]{2,1,0:T(8,128)S(1)}, u32[]{:S(2)}, u32[]{:S(2)}) collective-permute-start(f32[2,128,128]{2,1,0:T(8,128)S(1)} %pad_maximum_fusion.3), channel_id=1, source_target_pairs={{0,256},{128,896},{256,0},{384,640},{512,768},{640,384},{768,512},... | collective-permute-start | bytes 393224 | tf_op jit(solution)/shard_map/ppermute | solution.py:192
  36.1 2.8 %collective-permute-done.4 = f32[2,128,128]{2,1,0:T(8,128)S(1)} collective-permute-done((f32[2,128,128]{2,1,0:T(8,128)S(1)}, f32[2,128,128]{2,1,0:T(8,128)S(1)}, u32[]{:S(2)}, u32[]{:S(2)}) %collective-permute-start.4) | collective-permute-done | bytes 131104 | tf_op jit(solution)/shard_map/ppermute | solution.py:192
  38.9 13.2 %collective-permute-start.5 = (f32[2,128,128]{2,1,0:T(8,128)S(1)}, f32[2,128,128]{2,1,0:T(8,128)S(1)}, u32[]{:S(2)}, u32[]{:S(2)}) collective-permute-start(f32[2,128,128]{2,1,0:T(8,128)S(1)} %pad_maximum_fusion.2), channel_id=1, source_target_pairs={{0,768},{128,384},{256,512},{384,128},{512,256},{640,896},{768,0},... | collective-permute-start | bytes 393224 | tf_op jit(solution)/shard_map/ppermute | solution.py:193
  52.1 8.4 %collective-permute-done.6 = f32[2,128,128]{2,1,0:T(8,128)S(1)} collective-permute-done((f32[2,128,128]{2,1,0:T(8,128)S(1)}, f32[2,128,128]{2,1,0:T(8,128)S(1)}, u32[]{:S(2)}, u32[]{:S(2)}) %collective-permute-start.6) | collective-permute-done | bytes 131104 | tf_op jit(solution)/shard_map/ppermute | solution.py:192
  60.6 0.6 fusion.11
  61.2 18.9 %collective-permute-start.7 = (f32[2,128,128]{2,1,0:T(8,128)S(1)}, f32[2,128,128]{2,1,0:T(8,128)S(1)}, u32[]{:S(2)}, u32[]{:S(2)}) collective-permute-start(f32[2,128,128]{2,1,0:T(8,128)S(1)} %pad_maximum_fusion.4), channel_id=1, source_target_pairs={{0,768},{128,384},{256,512},{384,128},{512,256},{640,896},{768,0},... | collective-permute-start | bytes 393224 | tf_op jit(solution)/shard_map/ppermute | solution.py:193
  80.1 0.0 collective-permute-done.5
  80.1 0.0 copy-start.2
  80.1 1.9 collective-permute-start.8
  82.1 0.0 collective-permute-done.got_ref
  82.1 0.8 copy-done.13
  82.9 2.4 %shard_map.64 = (f32[2,4,128,256]{3,2,1,0:T(8,128)}, f32[2,4,128,128]{3,2,1,0:T(8,128)}, f32[2,4,128,128]{3,2,1,0:T(8,128)}) custom-call(f32[2,4,64,256]{3,2,1,0:T(8,128)} %get-tuple-element.24.mine_ref, f32[2,4,64,256]{3,2,1,0:T(8,128)} %copy-done.13), custom_call_target="tpu_custom_call" | custom-call | flops 49999998976 | bytes 200000000 | tf_op jit(solution)/shard_map/pallas_call | solution.py:149
  85.3 3.4 %collective-permute-start.1 = (f32[2,4,128,128]{3,2,1,0:T(8,128)}, f32[2,4,128,128]{3,2,1,0:T(8,128)S(1)}, u32[]{:S(2)}, u32[]{:S(2)}) collective-permute-start(f32[2,4,128,128]{3,2,1,0:T(8,128)} %get-tuple-element.16), channel_id=1, source_target_pairs={{0,1},{1,2},{2,3},{3,4},{4,5},{5,6},{6,7},{7,8},{8,9},{9,10},{10,1... | collective-permute-start | bytes 1572872 | tf_op jit(solution)/shard_map/ppermute | solution.py:211
  88.7 12.7 %collective-permute-start.2 = (f32[2,4,128,128]{3,2,1,0:T(8,128)}, f32[2,4,128,128]{3,2,1,0:T(8,128)S(1)}, u32[]{:S(2)}, u32[]{:S(2)}) collective-permute-start(f32[2,4,128,128]{3,2,1,0:T(8,128)} %get-tuple-element.17), channel_id=1, source_target_pairs={{1,0},{2,1},{3,2},{4,3},{5,4},{6,5},{7,6},{8,7},{9,8},{10,9},{11,1... | collective-permute-start | bytes 1572872 | tf_op jit(solution)/shard_map/ppermute | solution.py:212
  101.5 0.2 fusion
  101.7 0.0 collective-permute-done.7
  101.7 0.0 collective-permute-done.8.after_ref
  101.7 0.0 copy-start.7
  101.7 0.6 copy-done.10
  102.3 0.1 copy-done.7
  102.4 2.5 %shard_map.65 = (f32[128,128]{1,0:T(8,128)}, f32[264,128]{1,0:T(8,128)}) custom-call(f32[512,128]{1,0:T(8,128)} %copy-done.2, f32[128,128]{1,0:T(8,128)} %get-tuple-element.26.kept_ref, f32[128,128]{1,0:T(8,128)} %get-tuple-element.36.got_ref, f32[256,128]{1,0:T(8,128)} %bitcast.36, f32[512,128]{1,0:T(8,128)} %copy-done.7), custom_call_target="tpu_custom_call" | custom-call | flops 1000 | bytes 1000 | tf_op jit(solution)/shard_map/pallas_call | solution.py:70
  105.0 41.6 %all-gather.1 = f32[512,128]{1,0:T(8,128)S(1)} all-gather(f32[128,128]{1,0:T(8,128)} %get-tuple-element.20), channel_id=3, replica_groups={{0,256,512,768},{128,384,640,896},{1,257,513,769},{129,385,641,897},{2,..., dimensions={0}, use_global_device_ids=true | all-gather | bytes 327680 | tf_op jit(solution)/shard_map/all_gather | solution.py:215
  146.6 1.9 collective-permute-start.9
  148.5 0.7 select_reduce_fusion.coef_ref
  149.2 37.3 %all-gather = f32[1056,128]{1,0:T(8,128)} all-gather(f32[264,128]{1,0:T(8,128)S(1)} %copy-done.9), channel_id=2, replica_groups={{0,256,512,768},{128,384,640,896},{1,257,513,769},{129,385,641,897},{2,..., dimensions={0}, use_global_device_ids=true | all-gather | bytes 675840 | tf_op jit(solution)/shard_map/all_gather | solution.py:217
  186.5 0.0 collective-permute-done.1.wl_ref
  186.5 0.0 collective-permute-done.2.wr_ref
  186.5 0.0 collective-permute-done.9.left_ref
  186.5 0.7 copy-done.5
  187.3 0.2 copy-done.6
  187.5 0.1 copy-done.8
  187.6 4.5 %shard_map.66 = (f32[4,64,256]{2,1,0:T(8,128)}, f32[4,64,256]{2,1,0:T(8,128)}) custom-call(f32[12]{0:T(128)} %select_reduce_fusion.coef_ref, f32[2,4,128,256]{3,2,1,0:T(8,128)} %get-tuple-element.15.w_ref, f32[2,4,128,128]{3,2,1,0:T(8,128)} %copy-done.5, f32[2,4,128,128]{3,2,1,0:T(8,128)} %copy-done.6, f32[4,264,128]{2,1,0:T(8,128)} %bitcast.33, ...), custom_call_target="tpu_custom_call" | custom-call | flops 1000 | bytes 1000 | tf_op jit(solution)/shard_map/pallas_call | solution.py:119
  192.1 17.0 %collective-permute-start.10 = (f32[4,64,256]{2,1,0:T(8,128)}, f32[4,64,256]{2,1,0:T(8,128)S(1)}, u32[]{:S(2)}, u32[]{:S(2)}) collective-permute-start(f32[4,64,256]{2,1,0:T(8,128)} %get-tuple-element.22), channel_id=1, source_target_pairs={{0,128},{128,0},{256,384},{384,256},{512,640},{640,512},{768,896},... | collective-permute-start | bytes 786440 | tf_op jit(solution)/shard_map/ppermute | solution.py:220
  209.1 1.4 collective-permute-done.10
  210.4 1.2 fusion.2
  211.7 1.1 copy.18
  (28 shorter events, 0.2 us)
Async XLA Ops:
  0.0 101.5 %copy-start = (f32[8]{0:T(128)S(1)}, f32[8]{0:T(128)}, u32[]{:S(2)}) copy-start(f32[8]{0:T(128)} %param.8) | copy-start | bytes 100
  0.0 17.4 %copy-start.3 = (f32[2,64,8,256]{3,2,1,0:T(8,128)S(1)}, f32[2,64,8,256]{3,2,1,0:T(8,128)}, u32[]{:S(2)}) copy-start(f32[2,64,8,256]{3,2,1,0:T(8,128)} %param.7) | copy-start | bytes 3145732
  1.4 19.9 %collective-permute-start.3 = (f32[4,64,256]{2,1,0:T(8,128)S(1)}, f32[4,64,256]{2,1,0:T(8,128)S(1)}, u32[]{:S(2)}, u32[]{:S(2)}) collective-permute-start(f32[4,64,256]{2,1,0:T(8,128)S(1)} %get-tuple-element.18), channel_id=1, source_target_pairs={{0,128},{128,0},{256,384},{384,256},{512,640},{640,512},{768,896},... | collective-permute-start | bytes 786440 | tf_op jit(solution)/shard_map/ppermute | solution.py:181
  18.6 63.4 %collective-permute-start = (f32[2,4,64,256]{3,2,1,0:T(8,128)S(1)}, f32[2,4,64,256]{3,2,1,0:T(8,128)S(1)}, u32[]{:S(2)}, u32[]{:S(2)}) collective-permute-start(f32[2,4,64,256]{3,2,1,0:T(8,128)S(1)} %get-tuple-element.23), channel_id=1, source_target_pairs={{0,128},{128,0},{256,384},{384,256},{512,640},{640,512},{768,896},... | collective-permute-start | bytes 1572872 | tf_op jit(solution)/shard_map/ppermute | solution.py:210
  20.6 0.7 copy-start.11
  20.6 0.7 copy-start.12
  21.4 17.5 %collective-permute-start.4 = (f32[2,128,128]{2,1,0:T(8,128)S(1)}, f32[2,128,128]{2,1,0:T(8,128)S(1)}, u32[]{:S(2)}, u32[]{:S(2)}) collective-permute-start(f32[2,128,128]{2,1,0:T(8,128)S(1)} %pad_maximum_fusion.1), channel_id=1, source_target_pairs={{0,256},{128,896},{256,0},{384,640},{512,768},{640,384},{768,512},... | collective-permute-start | bytes 393224 | tf_op jit(solution)/shard_map/ppermute | solution.py:192
  32.1 28.4 %collective-permute-start.6 = (f32[2,128,128]{2,1,0:T(8,128)S(1)}, f32[2,128,128]{2,1,0:T(8,128)S(1)}, u32[]{:S(2)}, u32[]{:S(2)}) collective-permute-start(f32[2,128,128]{2,1,0:T(8,128)S(1)} %pad_maximum_fusion.3), channel_id=1, source_target_pairs={{0,256},{128,896},{256,0},{384,640},{512,768},{640,384},{768,512},... | collective-permute-start | bytes 393224 | tf_op jit(solution)/shard_map/ppermute | solution.py:192
  38.9 41.2 %collective-permute-start.5 = (f32[2,128,128]{2,1,0:T(8,128)S(1)}, f32[2,128,128]{2,1,0:T(8,128)S(1)}, u32[]{:S(2)}, u32[]{:S(2)}) collective-permute-start(f32[2,128,128]{2,1,0:T(8,128)S(1)} %pad_maximum_fusion.2), channel_id=1, source_target_pairs={{0,768},{128,384},{256,512},{384,128},{512,256},{640,896},{768,0},... | collective-permute-start | bytes 393224 | tf_op jit(solution)/shard_map/ppermute | solution.py:193
  61.2 40.5 %collective-permute-start.7 = (f32[2,128,128]{2,1,0:T(8,128)S(1)}, f32[2,128,128]{2,1,0:T(8,128)S(1)}, u32[]{:S(2)}, u32[]{:S(2)}) collective-permute-start(f32[2,128,128]{2,1,0:T(8,128)S(1)} %pad_maximum_fusion.4), channel_id=1, source_target_pairs={{0,768},{128,384},{256,512},{384,128},{512,256},{640,896},{768,0},... | collective-permute-start | bytes 393224 | tf_op jit(solution)/shard_map/ppermute | solution.py:193
  80.1 5.2 %copy-start.2 = (f32[512,128]{1,0:T(8,128)}, f32[512,128]{1,0:T(8,128)S(1)}, u32[]{:S(2)}) copy-start(f32[512,128]{1,0:T(8,128)S(1)} %pad_maximum_fusion.first_ref) | copy-start | bytes 786436
  80.1 21.5 %collective-permute-start.8 = (f32[512,128]{1,0:T(8,128)S(1)}, f32[512,128]{1,0:T(8,128)S(1)}, u32[]{:S(2)}, u32[]{:S(2)}) collective-permute-start(f32[512,128]{1,0:T(8,128)S(1)} %pad_maximum_fusion.first_ref), channel_id=1, source_target_pairs={{1,0},{2,1},{3,2},{4,3},{5,4},{6,5},{7,6},{8,7},{9,8},{10,9},{11,1... | collective-permute-start | bytes 786440 | tf_op jit(solution)/shard_map/ppermute | solution.py:198
  82.1 0.8 copy-start.13
  85.3 16.1 %copy-start.14 = (s32[8]{0:T(128)S(1)}, s32[8]{0:T(128)}, u32[]{:S(2)}) copy-start(s32[8]{0:T(128)} %param.10) | copy-start | bytes 100
  85.3 101.2 %collective-permute-start.1 = (f32[2,4,128,128]{3,2,1,0:T(8,128)}, f32[2,4,128,128]{3,2,1,0:T(8,128)S(1)}, u32[]{:S(2)}, u32[]{:S(2)}) collective-permute-start(f32[2,4,128,128]{3,2,1,0:T(8,128)} %get-tuple-element.16), channel_id=1, source_target_pairs={{0,1},{1,2},{2,3},{3,4},{4,5},{5,6},{6,7},{7,8},{8,9},{9,10},{10,1... | collective-permute-start | bytes 1572872 | tf_op jit(solution)/shard_map/ppermute | solution.py:211
  88.7 97.8 %collective-permute-start.2 = (f32[2,4,128,128]{3,2,1,0:T(8,128)}, f32[2,4,128,128]{3,2,1,0:T(8,128)S(1)}, u32[]{:S(2)}, u32[]{:S(2)}) collective-permute-start(f32[2,4,128,128]{3,2,1,0:T(8,128)} %get-tuple-element.17), channel_id=1, source_target_pairs={{1,0},{2,1},{3,2},{4,3},{5,4},{6,5},{7,6},{8,7},{9,8},{10,9},{11,1... | collective-permute-start | bytes 1572872 | tf_op jit(solution)/shard_map/ppermute | solution.py:212
  101.7 0.7 copy-start.10
  101.7 0.7 copy-start.7
  105.0 44.2 %copy-start.9 = (f32[264,128]{1,0:T(8,128)S(1)}, f32[264,128]{1,0:T(8,128)}, u32[]{:S(2)}) copy-start(f32[264,128]{1,0:T(8,128)} %get-tuple-element.19) | copy-start | bytes 405508
  146.6 39.9 %copy-start.4 = (f32[512,128]{1,0:T(8,128)}, f32[512,128]{1,0:T(8,128)S(1)}, u32[]{:S(2)}) copy-start(f32[512,128]{1,0:T(8,128)S(1)} %all-gather.1) | copy-start | bytes 786436
  146.6 39.9 %collective-permute-start.9 = (f32[4,128,128]{2,1,0:T(8,128)S(1)}, f32[4,128,128]{2,1,0:T(8,128)S(1)}, u32[]{:S(2)}, u32[]{:S(2)}) collective-permute-start(f32[4,128,128]{2,1,0:T(8,128)S(1)} %bitcast.34), channel_id=1, source_target_pairs={{0,1},{1,2},{2,3},{3,4},{4,5},{5,6},{6,7},{7,8},{8,9},{9,10},{10,1... | collective-permute-start | bytes 786440 | tf_op jit(solution)/shard_map/ppermute | solution.py:216
  186.5 0.8 copy-start.5
  186.5 0.9 copy-start.6
  186.5 1.0 copy-start.8
  187.6 22.9 %copy-start.1 = (f32[64,8,256]{2,1,0:T(8,128)S(1)}, f32[64,8,256]{2,1,0:T(8,128)}, u32[]{:S(2)}) copy-start(f32[64,8,256]{2,1,0:T(8,128)} %param.6) | copy-start | bytes 1572868
  192.1 18.4 %collective-permute-start.10 = (f32[4,64,256]{2,1,0:T(8,128)}, f32[4,64,256]{2,1,0:T(8,128)S(1)}, u32[]{:S(2)}, u32[]{:S(2)}) collective-permute-start(f32[4,64,256]{2,1,0:T(8,128)} %get-tuple-element.22), channel_id=1, source_target_pairs={{0,128},{128,0},{256,384},{384,256},{512,640},{640,512},{768,896},... | collective-permute-start | bytes 786440 | tf_op jit(solution)/shard_map/ppermute | solution.py:220

commit v3 on v2

--- a/solution.py
+++ b/solution.py
@@ -42,21 +42,29 @@
 LANES = ((1,), (1,))
 
 
-def covariance_kernel(first_ref, kept_ref, got_ref, last_ref, after_ref, edge_ref, own_ref):
-    def centred(*parts):
-        count = sum(p.shape[0] for p in parts)
-        mean = sum(jnp.sum(p, axis=0, keepdims=True) for p in parts) / count
-        return split(jnp.concatenate([p - mean for p in parts], axis=0))
-
+def centred(*parts):
+    count = sum(p.shape[0] for p in parts)
+    mean = sum(jnp.sum(p, axis=0, keepdims=True) for p in parts) / count
+    return split(jnp.concatenate([p - mean for p in parts], axis=0))
+
+
+def first_kernel(message_ref, high_ref, low_ref, square_ref):
+    first = centred(message_ref[: high_ref.shape[0]])
+    high_ref[...], low_ref[...] = first
+    square_ref[...] = product(first, first, ROWS)
+
+
+def covariance_kernel(
+    high_ref, low_ref, square_ref, kept_ref, got_ref, last_ref, message_ref, edge_ref, own_ref
+):
     second = centred(kept_ref[...], got_ref[...], last_ref[...])
-    after = centred(after_ref[...])
+    after = centred(message_ref[: high_ref.shape[0]])
     edge_ref[...] = product(second, after, ROWS)
-    first = centred(first_ref[...])
-    d0 = product(first, first, ROWS)
+    first = high_ref[...], low_ref[...]
     d1 = product(second, second, ROWS)
     row = lax.broadcasted_iota(jnp.int32, (BLK, BLK), 0)
     col = lax.broadcasted_iota(jnp.int32, (BLK, BLK), 1)
-    own_ref[:BLK] = jnp.where(row <= col, d0, d1)
+    own_ref[:BLK] = jnp.where(row <= col, square_ref[...], d1)
     own_ref[BLK : 2 * BLK] = product(first, second, ROWS)
     diagonal = jnp.sum(jnp.where(row == col, d1, 0.0), axis=0, keepdims=True)
     own_ref[2 * BLK :] = jnp.broadcast_to(diagonal, (8, BLK))
@@ -66,18 +74,41 @@
 TINY = pl.CostEstimate(flops=1000, bytes_accessed=1000, transcendentals=0)
 
 
-def covariances(*parts):
+def covariances(message, kept, got, last, after):
+    ensemble = message.shape[0] - 8
+    square = jax.ShapeDtypeStruct((BLK, BLK), jnp.float32)
+    half = jax.ShapeDtypeStruct((ensemble, BLK), jnp.bfloat16)
+    first = pl.pallas_call(first_kernel, out_shape=(half, half, square), cost_estimate=LONG)(message)
     return pl.pallas_call(
         covariance_kernel,
-        out_shape=(
-            jax.ShapeDtypeStruct((BLK, BLK), jnp.float32),
-            jax.ShapeDtypeStruct((2 * BLK + 8, BLK), jnp.float32),
-        ),
+        out_shape=(square, jax.ShapeDtypeStruct((2 * BLK + 8, BLK), jnp.float32)),
         cost_estimate=TINY,
-    )(*parts)
-
-
-def increment_kernel(coef_ref, w_ref, wl_ref, wr_ref, own_ref, edge_ref, left_ref, kept_ref, sent_ref):
+    )(*first, kept, got, last, after)
+
+
+def outward_kernel(message_ref, w_ref, edge_ref, out_ref):
+    mixed = message_ref[:1, :1] * w_ref[0, 0] + message_ref[:1, 1:2] * w_ref[1, 0]
+    out_ref[0] = product(split(mixed), split(edge_ref[0]), PLAIN)
+
+
+def outward(message, w, edge):
+    levels, members = w.shape[1:3]
+    per_level = pl.BlockSpec((1, BLK, BLK), lambda i: (i, 0, 0))
+    return pl.pallas_call(
+        outward_kernel,
+        grid=(levels,),
+        in_specs=[
+            pl.BlockSpec((8, BLK), lambda i: (message.shape[0] // 8 - 1, 0)),
+            pl.BlockSpec((2, 1, members, BLK), lambda i: (0, i, 0, 1)),
+            per_level,
+        ],
+        out_specs=per_level,
+        out_shape=jax.ShapeDtypeStruct((levels, members, BLK), jnp.float32),
+        cost_estimate=TINY,
+    )(message, w, edge)
+
+
+def increment_kernel(coef_ref, w_ref, wr_ref, own_ref, edge_ref, left_ref, kept_ref, sent_ref):
     row = lax.broadcasted_iota(jnp.int32, (BLK, BLK), 0)
     col = lax.broadcasted_iota(jnp.int32, (BLK, BLK), 1)
     packed = own_ref[0, :BLK]
@@ -88,7 +119,6 @@
     d1 = split(lower + lower.T + jnp.where(row == col, own_ref[0, 2 * BLK : 2 * BLK + 1], 0.0))
     c01 = split(own_ref[0, BLK : 2 * BLK])
     edge = split(edge_ref[0])
-    left = split(left_ref[0])
 
     def mixed(ref, t, j, part=slice(None)):
         at = t * 6 + j * 2
@@ -96,7 +126,7 @@
 
     here, there = slice(0, BLK), slice(BLK, 2 * BLK)
     zero = (
-        product(mixed(wl_ref, 0, 0), left, PLAIN)
+        left_ref[0]
         + product(mixed(w_ref, 0, 1, here), d0, PLAIN)
         + product(mixed(w_ref, 0, 2, there), c01, LANES)
     )
@@ -111,7 +141,7 @@
         ref[0, :, there] = one[rows]
 
 
-def increments(coefs, w, w_left, w_right, own, edge, left):
+def increments(coefs, w, w_right, own, edge, left):
     levels, members = w.shape[1:3]
     per_level = lambda *shape: pl.BlockSpec((1,) + shape, lambda i: (i, 0, 0))
     both = lambda width: pl.BlockSpec((2, 1, members, width), lambda i: (0, i, 0, 0))
@@ -123,23 +153,21 @@
             pl.BlockSpec(memory_space=pltpu.SMEM),
             both(2 * BLK),
             both(BLK),
-            both(BLK),
             per_level(2 * BLK + 8, BLK),
             per_level(BLK, BLK),
-            per_level(BLK, BLK),
+            per_level(members, BLK),
         ],
         out_specs=(per_level(members // 2, 2 * BLK),) * 2,
         out_shape=(half, half),
         cost_estimate=TINY,
-    )(coefs, w, w_left, w_right, own, edge, left)
-
-
-def gather_kernel(mine_ref, got_ref, w_ref, low_ref, high_ref):
+    )(coefs, w, w_right, own, edge, left)
+
+
+def gather_kernel(mine_ref, got_ref, w_ref, low_ref):
     keep = mine_ref.shape[2]
     for ref, rows in ((mine_ref, slice(0, keep)), (got_ref, slice(keep, 2 * keep))):
         w_ref[0, :, rows] = ref[0]
         low_ref[0, :, rows] = ref[0, :, :, :BLK]
-        high_ref[0, :, rows] = ref[0, :, :, BLK:]
 
 
 def gathered(mine, got):
@@ -150,8 +178,8 @@
         gather_kernel,
         grid=(batches,),
         in_specs=[block(members, width)] * 2,
-        out_specs=(block(2 * members, width),) + (block(2 * members, BLK),) * 2,
-        out_shape=(shape(width), shape(BLK), shape(BLK)),
+        out_specs=(block(2 * members, width), block(2 * members, BLK)),
+        out_shape=(shape(width), shape(BLK)),
         cost_estimate=LONG,
     )(mine, got)
 
@@ -193,30 +221,31 @@
         last = lax.ppermute(jnp.stack([pick(x, two), got[1]]), "member", step_two)
         return pick(x, chip), got[0], last.reshape(-1, BLK)
 
-    first = jnp.concatenate(to_owner(0))
-    second = to_owner(1)
-    after = lax.ppermute(first, "region", left)
-
+    first, second = to_owner(0), to_owner(1)
+    taken, pair_taper = lax.optimization_barrier((second[1], pair_taper))
+    second = second[0], taken, second[2]
     tapers = jnp.dot(
         one_hot(pair_taper, taper_table.shape[0]), taper_table, precision=lax.Precision.HIGHEST
     ) / (ensemble - 1)
     targets = pair_blocks[:, 0]
     slot = targets * 6 + (pair_blocks[:, 1] - targets) * 2 + pair_batch
     coefs = jnp.sum(one_hot(slot, 12) * tapers[:, None], axis=0)
+    rows = jnp.pad(coefs[None], ((0, 7), (0, BLK - 12)))
+    message = jnp.concatenate([*first, rows])
+    after = lax.ppermute(message, "region", left)
 
     w = jnp.transpose(weights, (0, 2, 1, 3))
     mine = lax.dynamic_slice_in_dim(w, core * half, half, 1)
     theirs = lax.dynamic_slice_in_dim(w, (1 - core) * half, half, 1)
-    w, low, high = gathered(mine, lax.ppermute(theirs, "member", SWAP))
-    w_left = lax.ppermute(high, "region", right)
+    w, low = gathered(mine, lax.ppermute(theirs, "member", SWAP))
     w_right = lax.ppermute(low, "region", left)
 
-    edge, own = covariances(first, *second, after)
+    edge, own = covariances(message, *second, after)
     edges = lax.all_gather(edge, "member", axis_index_groups=GROUPS)
-    left_edges = lax.ppermute(edges, "region", right)
+    from_left = lax.ppermute(outward(after, w, edges), "region", right)
     owns = lax.all_gather(own, "member", axis_index_groups=GROUPS)
 
-    kept, sent = increments(coefs, w, w_left, w_right, owns, edges, left_edges)
+    kept, sent = increments(coefs, w, w_right, owns, edges, from_left)
     came = lax.ppermute(sent, "member", SWAP)
     change = jnp.where(
         core == 0, jnp.concatenate([kept, came]), jnp.concatenate([came, kept])

time: 213 us -> 211 us (level)
  the two profiles are of different devices: /device:TPU:1 before, /device:TPU:95 now
where the time goes in v3:
time: 211 us; the launch traced here: 210 us
  blocking collectives  85.1 us (40%)
  starting transfers between devices  79.3 us (38%)
  waiting for transfers between devices  20.4 us (10%)
  Pallas kernels  14.8 us (7%)
  local copies, waits for them, and re-layouts  8.66 us (4%)
    all_gather x1, blocking collectives, local(): owns = lax.all_gather(own, 'member', axis_index_groups=GROUPS)  50 us
    all_gather x1, blocking collectives, local(): edges = lax.all_gather(edge, 'member', axis_index_groups=GROUPS)  35.2 us
    ppermute x2, starting transfers between devices, to_owner(): lax.ppermute(jnp.stack([pick(x, one), pick(x, both)]), 'member', step_one)  22.8 us
    ppermute x1, starting transfers between devices, local(): from_left = lax.ppermute(outward(after, w, edges), 'region', right)  17.8 us
    ppermute x2, starting transfers between devices, to_owner(): last = lax.ppermute(jnp.stack([pick(x, two), got[1]]), 'member', step_two)  16.1 us
    ppermute x2, waiting for transfers between devices, to_owner(): lax.ppermute(jnp.stack([pick(x, one), pick(x, both)]), 'member', step_one)  13.9 us
    ppermute x1, starting transfers between devices, local(): came = lax.ppermute(sent, 'member', SWAP)  13.5 us
    ppermute x2, waiting for transfers between devices, to_owner(): last = lax.ppermute(jnp.stack([pick(x, two), got[1]]), 'member', step_two)  5.13 us
  transfers between devices with their start and end apart: 10, of which 4 were waited for; matrix products, arithmetic and copies ran while one was open for 1% of the time, Pallas kernels for 5%

profile of v3, /device:TPU:95, one launch (start us, length us, event | category | flops | bytes accessed | tf_op | source)
XLA Modules:
  0.0 210.3 jit_solution(7355024039278029614)
XLA Ops:
  0.0 1.3 copy.17
  1.4 2.6 %collective-permute-start = (f32[4,64,256]{2,1,0:T(8,128)S(1)}, f32[4,64,256]{2,1,0:T(8,128)S(1)}, u32[]{:S(2)}, u32[]{:S(2)}) collective-permute-start(f32[4,64,256]{2,1,0:T(8,128)S(1)} %get-tuple-element.18), channel_id=1, source_target_pairs={{0,128},{128,0},{256,384},{384,256},{512,640},{640,512},{768,896},... | collective-permute-start | bytes 786440 | tf_op jit(solution)/shard_map/ppermute | solution.py:209
  4.0 0.3 copy.15
  4.3 0.9 dynamic-slice_bitcast_fusion
  5.2 1.9 collective-permute-start.2
  7.2 0.0 copy-start.10
  7.2 0.0 copy-start.11
  7.2 0.7 copy-done.10
  7.8 0.0 collective-permute-done
  7.9 20.9 %collective-permute-start.4 = (f32[2,128,128]{2,1,0:T(8,128)S(1)}, f32[2,128,128]{2,1,0:T(8,128)S(1)}, u32[]{:S(2)}, u32[]{:S(2)}) collective-permute-start(f32[2,128,128]{2,1,0:T(8,128)S(1)} %pad_maximum_fusion.1), channel_id=1, source_target_pairs={{0,256},{128,896},{256,0},{384,640},{512,768},{640,384},{768,512},... | collective-permute-start | bytes 393224 | tf_op jit(solution)/shard_map/ppermute | solution.py:220
  28.9 0.6 constant_dynamic-slice_fusion
  29.5 1.9 collective-permute-start.1
  31.5 7.7 %collective-permute-done.4 = f32[2,128,128]{2,1,0:T(8,128)S(1)} collective-permute-done((f32[2,128,128]{2,1,0:T(8,128)S(1)}, f32[2,128,128]{2,1,0:T(8,128)S(1)}, u32[]{:S(2)}, u32[]{:S(2)}) %collective-permute-start.4) | collective-permute-done | bytes 131104 | tf_op jit(solution)/shard_map/ppermute | solution.py:220
  39.2 7.9 %collective-permute-start.5 = (f32[2,128,128]{2,1,0:T(8,128)S(1)}, f32[2,128,128]{2,1,0:T(8,128)S(1)}, u32[]{:S(2)}, u32[]{:S(2)}) collective-permute-start(f32[2,128,128]{2,1,0:T(8,128)S(1)} %pad_maximum_fusion.2), channel_id=1, source_target_pairs={{0,768},{128,384},{256,512},{384,128},{512,256},{640,896},{768,0},... | collective-permute-start | bytes 393224 | tf_op jit(solution)/shard_map/ppermute | solution.py:221
  47.1 6.2 %collective-permute-done.1 = f32[2,128,128]{2,1,0:T(8,128)S(1)} collective-permute-done((f32[2,128,128]{2,1,0:T(8,128)S(1)}, f32[2,128,128]{2,1,0:T(8,128)S(1)}, u32[]{:S(2)}, u32[]{:S(2)}) %collective-permute-start.1) | collective-permute-done | bytes 131104 | tf_op jit(solution)/shard_map/ppermute | solution.py:220
  53.3 0.6 fusion.11
  53.9 8.3 %collective-permute-start.6 = (f32[2,128,128]{2,1,0:T(8,128)S(1)}, f32[2,128,128]{2,1,0:T(8,128)S(1)}, u32[]{:S(2)}, u32[]{:S(2)}) collective-permute-start(f32[2,128,128]{2,1,0:T(8,128)S(1)} %pad_maximum_fusion.3), channel_id=1, source_target_pairs={{0,768},{128,384},{256,512},{384,128},{512,256},{640,896},{768,0},... | collective-permute-start | bytes 393224 | tf_op jit(solution)/shard_map/ppermute | solution.py:221
  62.2 0.0 copy-done
  62.2 0.0 copy-done.13
  62.2 0.2 fusion
  62.4 0.1 select_reduce_fusion.coef_ref
  62.5 0.0 collective-permute-done.5
  62.5 0.6 copy-done.9
  63.1 0.0 copy-start.5
  63.1 2.5 %collective-permute-start.7 = (f32[520,128]{1,0:T(8,128)S(1)}, f32[520,128]{1,0:T(8,128)S(1)}, u32[]{:S(2)}, u32[]{:S(2)}) collective-permute-start(f32[520,128]{1,0:T(8,128)S(1)} %select_maximum_fusion.message_ref), channel_id=1, source_target_pairs={{1,0},{2,1},{3,2},{4,3},{5,4},{6,5},{7,6},{8,7},{9,8},{10,9},{11,1... | collective-permute-start | bytes 798728 | tf_op jit(solution)/shard_map/ppermute | solution.py:235
  65.6 0.0 collective-permute-done.2.got_ref
  65.6 0.8 copy-done.12
  66.4 2.2 %shard_map.64 = (f32[2,4,128,256]{3,2,1,0:T(8,128)}, f32[2,4,128,128]{3,2,1,0:T(8,128)}) custom-call(f32[2,4,64,256]{3,2,1,0:T(8,128)} %get-tuple-element.32.mine_ref, f32[2,4,64,256]{3,2,1,0:T(8,128)} %copy-done.12), custom_call_target="tpu_custom_call" | custom-call | flops 49999998976 | bytes 200000000 | tf_op jit(solution)/shard_map/pallas_call | solution.py:177
  68.7 2.2 %collective-permute-start.3 = (f32[2,4,128,128]{3,2,1,0:T(8,128)}, f32[2,4,128,128]{3,2,1,0:T(8,128)S(1)}, u32[]{:S(2)}, u32[]{:S(2)}) collective-permute-start(f32[2,4,128,128]{3,2,1,0:T(8,128)} %get-tuple-element.22), channel_id=1, source_target_pairs={{1,0},{2,1},{3,2},{4,3},{5,4},{6,5},{7,6},{8,7},{9,8},{10,9},{11,1... | collective-permute-start | bytes 1572872 | tf_op jit(solution)/shard_map/ppermute | solution.py:241
  70.8 2.0 shard_map.65
  72.8 5.1 %collective-permute-done.6 = f32[2,128,128]{2,1,0:T(8,128)S(1)} collective-permute-done((f32[2,128,128]{2,1,0:T(8,128)S(1)}, f32[2,128,128]{2,1,0:T(8,128)S(1)}, u32[]{:S(2)}, u32[]{:S(2)}) %collective-permute-start.6) | collective-permute-done | bytes 131104 | tf_op jit(solution)/shard_map/ppermute | solution.py:221
  77.9 0.0 collective-permute-done.7.message_ref
  77.9 0.6 copy-done.8
  78.6 0.1 copy-done.2
  78.7 2.5 %shard_map.66 = (f32[128,128]{1,0:T(8,128)}, f32[264,128]{1,0:T(8,128)}) custom-call(bf16[512,128]{1,0:T(8,128)(2,1)} %get-tuple-element.23.high_ref, bf16[512,128]{1,0:T(8,128)(2,1)} %get-tuple-element.24.low_ref, f32[128,128]{1,0:T(8,128)} %get-tuple-element.25.square_ref, f32[128,128]{1,0:T(8,128)} %get-tuple-element.40.kept_ref, ...), custom_call_target="tpu_custom_call" | custom-call | flops 1000 | bytes 1000 | tf_op jit(solution)/shard_map/pallas_call | solution.py:82
  81.1 35.2 %all-gather.1 = f32[512,128]{1,0:T(8,128)} all-gather(f32[128,128]{1,0:T(8,128)} %get-tuple-element.28), channel_id=3, replica_groups={{0,256,512,768},{128,384,640,896},{1,257,513,769},{129,385,641,897},{2,..., dimensions={0}, use_global_device_ids=true | all-gather | bytes 327680 | tf_op jit(solution)/shard_map/all_gather | solution.py:244
  116.3 3.6 %shard_map.67 = f32[4,128,128]{2,1,0:T(8,128)} custom-call(f32[520,128]{1,0:T(8,128)} %copy-done.2, f32[2,4,128,256]{3,2,1,0:T(8,128)} %get-tuple-element.21.w_ref, f32[4,128,128]{2,1,0:T(8,128)} %bitcast.34), custom_call_target="tpu_custom_call" | custom-call | flops 1000 | bytes 1000 | tf_op jit(solution)/shard_map/pallas_call | solution.py:97
  119.9 17.8 %collective-permute-start.8 = (f32[4,128,128]{2,1,0:T(8,128)}, f32[4,128,128]{2,1,0:T(8,128)S(1)}, u32[]{:S(2)}, u32[]{:S(2)}) collective-permute-start(f32[4,128,128]{2,1,0:T(8,128)} %shard_map.67), channel_id=1, source_target_pairs={{0,1},{1,2},{2,3},{3,4},{4,5},{5,6},{6,7},{7,8},{8,9},{9,10},{10,1... | collective-permute-start | bytes 786440 | tf_op jit(solution)/shard_map/ppermute | solution.py:245
  137.7 50.0 %all-gather = f32[1056,128]{1,0:T(8,128)} all-gather(f32[264,128]{1,0:T(8,128)S(1)} %copy-done.7), channel_id=2, replica_groups={{0,256,512,768},{128,384,640,896},{1,257,513,769},{129,385,641,897},{2,..., dimensions={0}, use_global_device_ids=true | all-gather | bytes 675840 | tf_op jit(solution)/shard_map/all_gather | solution.py:246
  187.7 0.0 collective-permute-done.3.wr_ref
  187.7 0.0 collective-permute-done.8.left_ref
  187.7 0.8 copy-done.4
  188.5 0.1 copy-done.6
  188.6 4.5 %shard_map.68 = (f32[4,64,256]{2,1,0:T(8,128)}, f32[4,64,256]{2,1,0:T(8,128)}) custom-call(f32[12]{0:T(128)} %copy-done.9, f32[2,4,128,256]{3,2,1,0:T(8,128)} %get-tuple-element.21.w_ref, f32[2,4,128,128]{3,2,1,0:T(8,128)} %copy-done.4, f32[4,264,128]{2,1,0:T(8,128)} %bitcast.36, f32[4,128,128]{2,1,0:T(8,128)} %bitcast.35, f32[4,128,128]{2,1,0:T(8,128)} %copy-done.6), custom_call_target="tpu_custom_call" | custom-call | flops 1000 | bytes 1000 | tf_op jit(solution)/shard_map/pallas_call | solution.py:149
  193.1 13.5 %collective-permute-start.9 = (f32[4,64,256]{2,1,0:T(8,128)}, f32[4,64,256]{2,1,0:T(8,128)S(1)}, u32[]{:S(2)}, u32[]{:S(2)}) collective-permute-start(f32[4,64,256]{2,1,0:T(8,128)} %get-tuple-element.30), channel_id=1, source_target_pairs={{0,128},{128,0},{256,384},{384,256},{512,640},{640,512},{768,896},... | collective-permute-start | bytes 786440 | tf_op jit(solution)/shard_map/ppermute | solution.py:249
  206.6 1.4 collective-permute-done.9
  207.9 1.3 fusion.2
  209.2 1.1 copy.18
  (26 shorter events, 0.2 us)
Async XLA Ops:
  0.0 62.2 %copy-start = (f32[8]{0:T(128)S(1)}, f32[8]{0:T(128)}, u32[]{:S(2)}) copy-start(f32[8]{0:T(128)} %param.8) | copy-start | bytes 100
  0.0 4.0 %copy-start.3 = (f32[2,64,8,256]{3,2,1,0:T(8,128)S(1)}, f32[2,64,8,256]{3,2,1,0:T(8,128)}, u32[]{:S(2)}) copy-start(f32[2,64,8,256]{3,2,1,0:T(8,128)} %param.7) | copy-start | bytes 3145732
  1.4 6.5 %collective-permute-start = (f32[4,64,256]{2,1,0:T(8,128)S(1)}, f32[4,64,256]{2,1,0:T(8,128)S(1)}, u32[]{:S(2)}, u32[]{:S(2)}) collective-permute-start(f32[4,64,256]{2,1,0:T(8,128)S(1)} %get-tuple-element.18), channel_id=1, source_target_pairs={{0,128},{128,0},{256,384},{384,256},{512,640},{640,512},{768,896},... | collective-permute-start | bytes 786440 | tf_op jit(solution)/shard_map/ppermute | solution.py:209
  5.2 60.4 %collective-permute-start.2 = (f32[2,4,64,256]{3,2,1,0:T(8,128)S(1)}, f32[2,4,64,256]{3,2,1,0:T(8,128)S(1)}, u32[]{:S(2)}, u32[]{:S(2)}) collective-permute-start(f32[2,4,64,256]{3,2,1,0:T(8,128)S(1)} %get-tuple-element.31), channel_id=1, source_target_pairs={{0,128},{128,0},{256,384},{384,256},{512,640},{640,512},{768,896},... | collective-permute-start | bytes 1572872 | tf_op jit(solution)/shard_map/ppermute | solution.py:240
  7.2 0.7 copy-start.10
  7.2 0.7 copy-start.11
  7.9 31.2 %collective-permute-start.4 = (f32[2,128,128]{2,1,0:T(8,128)S(1)}, f32[2,128,128]{2,1,0:T(8,128)S(1)}, u32[]{:S(2)}, u32[]{:S(2)}) collective-permute-start(f32[2,128,128]{2,1,0:T(8,128)S(1)} %pad_maximum_fusion.1), channel_id=1, source_target_pairs={{0,256},{128,896},{256,0},{384,640},{512,768},{640,384},{768,512},... | collective-permute-start | bytes 393224 | tf_op jit(solution)/shard_map/ppermute | solution.py:220
  29.5 23.7 %collective-permute-start.1 = (f32[2,128,128]{2,1,0:T(8,128)S(1)}, f32[2,128,128]{2,1,0:T(8,128)S(1)}, u32[]{:S(2)}, u32[]{:S(2)}) collective-permute-start(f32[2,128,128]{2,1,0:T(8,128)S(1)} %pad_maximum_fusion), channel_id=1, source_target_pairs={{0,256},{128,896},{256,0},{384,640},{512,768},{640,384},{768,512},... | collective-permute-start | bytes 393224 | tf_op jit(solution)/shard_map/ppermute | solution.py:220
  39.2 23.3 %collective-permute-start.5 = (f32[2,128,128]{2,1,0:T(8,128)S(1)}, f32[2,128,128]{2,1,0:T(8,128)S(1)}, u32[]{:S(2)}, u32[]{:S(2)}) collective-permute-start(f32[2,128,128]{2,1,0:T(8,128)S(1)} %pad_maximum_fusion.2), channel_id=1, source_target_pairs={{0,768},{128,384},{256,512},{384,128},{512,256},{640,896},{768,0},... | collective-permute-start | bytes 393224 | tf_op jit(solution)/shard_map/ppermute | solution.py:221
  53.9 8.3 %copy-start.13 = (s32[8]{0:T(128)S(1)}, s32[8]{0:T(128)}, u32[]{:S(2)}) copy-start(s32[8]{0:T(128)} %param.10) | copy-start | bytes 100
  53.9 24.0 %collective-permute-start.6 = (f32[2,128,128]{2,1,0:T(8,128)S(1)}, f32[2,128,128]{2,1,0:T(8,128)S(1)}, u32[]{:S(2)}, u32[]{:S(2)}) collective-permute-start(f32[2,128,128]{2,1,0:T(8,128)S(1)} %pad_maximum_fusion.3), channel_id=1, source_target_pairs={{0,768},{128,384},{256,512},{384,128},{512,256},{640,896},{768,0},... | collective-permute-start | bytes 393224 | tf_op jit(solution)/shard_map/ppermute | solution.py:221
  62.5 0.6 copy-start.9
  63.1 5.6 %copy-start.5 = (f32[520,128]{1,0:T(8,128)}, f32[520,128]{1,0:T(8,128)S(1)}, u32[]{:S(2)}) copy-start(f32[520,128]{1,0:T(8,128)S(1)} %select_maximum_fusion.message_ref) | copy-start | bytes 798724
  63.1 14.8 %collective-permute-start.7 = (f32[520,128]{1,0:T(8,128)S(1)}, f32[520,128]{1,0:T(8,128)S(1)}, u32[]{:S(2)}, u32[]{:S(2)}) collective-permute-start(f32[520,128]{1,0:T(8,128)S(1)} %select_maximum_fusion.message_ref), channel_id=1, source_target_pairs={{1,0},{2,1},{3,2},{4,3},{5,4},{6,5},{7,6},{8,7},{9,8},{10,9},{11,1... | collective-permute-start | bytes 798728 | tf_op jit(solution)/shard_map/ppermute | solution.py:235
  65.6 0.8 copy-start.12
  68.7 119.0 %collective-permute-start.3 = (f32[2,4,128,128]{3,2,1,0:T(8,128)}, f32[2,4,128,128]{3,2,1,0:T(8,128)S(1)}, u32[]{:S(2)}, u32[]{:S(2)}) collective-permute-start(f32[2,4,128,128]{3,2,1,0:T(8,128)} %get-tuple-element.22), channel_id=1, source_target_pairs={{1,0},{2,1},{3,2},{4,3},{5,4},{6,5},{7,6},{8,7},{9,8},{10,9},{11,1... | collective-permute-start | bytes 1572872 | tf_op jit(solution)/shard_map/ppermute | solution.py:241
  77.9 0.7 copy-start.8
  77.9 0.7 copy-start.2
  116.3 21.5 %copy-start.7 = (f32[264,128]{1,0:T(8,128)S(1)}, f32[264,128]{1,0:T(8,128)}, u32[]{:S(2)}) copy-start(f32[264,128]{1,0:T(8,128)} %get-tuple-element.27) | copy-start | bytes 405508
  119.9 67.8 %collective-permute-start.8 = (f32[4,128,128]{2,1,0:T(8,128)}, f32[4,128,128]{2,1,0:T(8,128)S(1)}, u32[]{:S(2)}, u32[]{:S(2)}) collective-permute-start(f32[4,128,128]{2,1,0:T(8,128)} %shard_map.67), channel_id=1, source_target_pairs={{0,1},{1,2},{2,3},{3,4},{4,5},{5,6},{6,7},{7,8},{8,9},{9,10},{10,1... | collective-permute-start | bytes 786440 | tf_op jit(solution)/shard_map/ppermute | solution.py:245
  187.7 0.8 copy-start.4
  187.7 0.9 copy-start.6
  188.6 19.3 %copy-start.1 = (f32[64,8,256]{2,1,0:T(8,128)S(1)}, f32[64,8,256]{2,1,0:T(8,128)}, u32[]{:S(2)}) copy-start(f32[64,8,256]{2,1,0:T(8,128)} %param.6) | copy-start | bytes 1572868
  193.1 14.8 %collective-permute-start.9 = (f32[4,64,256]{2,1,0:T(8,128)}, f32[4,64,256]{2,1,0:T(8,128)S(1)}, u32[]{:S(2)}, u32[]{:S(2)}) collective-permute-start(f32[4,64,256]{2,1,0:T(8,128)} %get-tuple-element.30), channel_id=1, source_target_pairs={{0,128},{128,0},{256,384},{384,256},{512,640},{640,512},{768,896},... | collective-permute-start | bytes 786440 | tf_op jit(solution)/shard_map/ppermute | solution.py:249

commit v4 on v3

--- a/solution.py
+++ b/solution.py
@@ -55,19 +55,19 @@
 
 
 def covariance_kernel(
-    high_ref, low_ref, square_ref, kept_ref, got_ref, last_ref, message_ref, edge_ref, own_ref
+    high_ref, low_ref, square_ref, kept_ref, got_ref, last_ref, message_ref, out_ref
 ):
     second = centred(kept_ref[...], got_ref[...], last_ref[...])
-    after = centred(message_ref[: high_ref.shape[0]])
-    edge_ref[...] = product(second, after, ROWS)
     first = high_ref[...], low_ref[...]
     d1 = product(second, second, ROWS)
     row = lax.broadcasted_iota(jnp.int32, (BLK, BLK), 0)
     col = lax.broadcasted_iota(jnp.int32, (BLK, BLK), 1)
-    own_ref[:BLK] = jnp.where(row <= col, square_ref[...], d1)
-    own_ref[BLK : 2 * BLK] = product(first, second, ROWS)
+    out_ref[:BLK] = jnp.where(row <= col, square_ref[...], d1)
+    out_ref[BLK : 2 * BLK] = product(first, second, ROWS)
     diagonal = jnp.sum(jnp.where(row == col, d1, 0.0), axis=0, keepdims=True)
-    own_ref[2 * BLK :] = jnp.broadcast_to(diagonal, (8, BLK))
+    out_ref[3 * BLK :] = jnp.broadcast_to(diagonal, (8, BLK))
+    after = centred(message_ref[: high_ref.shape[0]])
+    out_ref[2 * BLK : 3 * BLK] = product(second, after, ROWS)
 
 
 LONG = pl.CostEstimate(flops=50_000_000_000, bytes_accessed=200_000_000, transcendentals=0)
@@ -78,89 +78,82 @@
     ensemble = message.shape[0] - 8
     square = jax.ShapeDtypeStruct((BLK, BLK), jnp.float32)
     half = jax.ShapeDtypeStruct((ensemble, BLK), jnp.bfloat16)
-    first = pl.pallas_call(first_kernel, out_shape=(half, half, square), cost_estimate=LONG)(message)
+    first = pl.pallas_call(first_kernel, out_shape=(half, half, square), cost_estimate=TINY)(message)
     return pl.pallas_call(
         covariance_kernel,
-        out_shape=(square, jax.ShapeDtypeStruct((2 * BLK + 8, BLK), jnp.float32)),
+        out_shape=jax.ShapeDtypeStruct((3 * BLK + 8, BLK), jnp.float32),
         cost_estimate=TINY,
     )(*first, kept, got, last, after)
 
 
-def outward_kernel(message_ref, w_ref, edge_ref, out_ref):
-    mixed = message_ref[:1, :1] * w_ref[0, 0] + message_ref[:1, 1:2] * w_ref[1, 0]
-    out_ref[0] = product(split(mixed), split(edge_ref[0]), PLAIN)
-
-
-def outward(message, w, edge):
+def outward_kernel(message_ref, w_ref, cov_ref, out_ref):
+    for level in range(out_ref.shape[0]):
+        mixed = message_ref[:1, :1] * w_ref[0, level] + message_ref[:1, 1:2] * w_ref[1, level]
+        out_ref[level] = product(split(mixed), split(cov_ref[level]), PLAIN)
+
+
+def outward(message, w, cov):
     levels, members = w.shape[1:3]
-    per_level = pl.BlockSpec((1, BLK, BLK), lambda i: (i, 0, 0))
     return pl.pallas_call(
         outward_kernel,
-        grid=(levels,),
+        grid=(1,),
         in_specs=[
             pl.BlockSpec((8, BLK), lambda i: (message.shape[0] // 8 - 1, 0)),
-            pl.BlockSpec((2, 1, members, BLK), lambda i: (0, i, 0, 1)),
-            per_level,
+            pl.BlockSpec((2, levels, members, BLK), lambda i: (0, 0, 0, 1)),
+            pl.BlockSpec((levels, BLK, BLK), lambda i: (0, 2, 0)),
         ],
-        out_specs=per_level,
+        out_specs=pl.BlockSpec((levels, members, BLK), lambda i: (0, 0, 0)),
         out_shape=jax.ShapeDtypeStruct((levels, members, BLK), jnp.float32),
         cost_estimate=TINY,
-    )(message, w, edge)
-
-
-def increment_kernel(coef_ref, w_ref, wr_ref, own_ref, edge_ref, left_ref, kept_ref, sent_ref):
+    )(message, w, cov)
+
+
+def increment_kernel(coef_ref, w_ref, wr_ref, cov_ref, kept_ref, sent_ref):
     row = lax.broadcasted_iota(jnp.int32, (BLK, BLK), 0)
     col = lax.broadcasted_iota(jnp.int32, (BLK, BLK), 1)
-    packed = own_ref[0, :BLK]
-    upper = jnp.where(row <= col, packed, 0.0)
-    strict = jnp.where(row < col, packed, 0.0)
-    lower = jnp.where(row > col, packed, 0.0)
-    d0 = split(upper + strict.T)
-    d1 = split(lower + lower.T + jnp.where(row == col, own_ref[0, 2 * BLK : 2 * BLK + 1], 0.0))
-    c01 = split(own_ref[0, BLK : 2 * BLK])
-    edge = split(edge_ref[0])
-
-    def mixed(ref, t, j, part=slice(None)):
-        at = t * 6 + j * 2
-        return split(coef_ref[at] * ref[0, 0, :, part] + coef_ref[at + 1] * ref[1, 0, :, part])
-
     here, there = slice(0, BLK), slice(BLK, 2 * BLK)
-    zero = (
-        left_ref[0]
-        + product(mixed(w_ref, 0, 1, here), d0, PLAIN)
-        + product(mixed(w_ref, 0, 2, there), c01, LANES)
-    )
-    one = (
-        product(mixed(w_ref, 1, 0, here), c01, PLAIN)
-        + product(mixed(w_ref, 1, 1, there), d1, PLAIN)
-        + product(mixed(wr_ref, 1, 2), edge, LANES)
-    )
     keep = kept_ref.shape[1]
-    for ref, rows in ((kept_ref, slice(0, keep)), (sent_ref, slice(keep, 2 * keep))):
-        ref[0, :, here] = zero[rows]
-        ref[0, :, there] = one[rows]
-
-
-def increments(coefs, w, w_right, own, edge, left):
+    for level in range(kept_ref.shape[0]):
+        packed = cov_ref[level, :BLK]
+        upper = jnp.where(row <= col, packed, 0.0)
+        strict = jnp.where(row < col, packed, 0.0)
+        lower = jnp.where(row > col, packed, 0.0)
+        diagonal = jnp.where(row == col, cov_ref[level, 3 * BLK : 3 * BLK + 1], 0.0)
+        d0 = split(upper + strict.T)
+        d1 = split(lower + lower.T + diagonal)
+        c01 = split(cov_ref[level, BLK : 2 * BLK])
+        edge = split(cov_ref[level, 2 * BLK : 3 * BLK])
+
+        def mixed(ref, t, j, part=slice(None)):
+            at = t * 6 + j * 2
+            return split(
+                coef_ref[at] * ref[0, level, :, part] + coef_ref[at + 1] * ref[1, level, :, part]
+            )
+
+        zero = product(mixed(w_ref, 0, 1, here), d0, PLAIN) + product(
+            mixed(w_ref, 0, 2, there), c01, LANES
+        )
+        one = (
+            product(mixed(w_ref, 1, 0, here), c01, PLAIN)
+            + product(mixed(w_ref, 1, 1, there), d1, PLAIN)
+            + product(mixed(wr_ref, 1, 2), edge, LANES)
+        )
+        for ref, rows in ((kept_ref, slice(0, keep)), (sent_ref, slice(keep, 2 * keep))):
+            ref[level, :, here] = zero[rows]
+            ref[level, :, there] = one[rows]
+
+
+def increments(coefs, w, w_right, cov):
     levels, members = w.shape[1:3]
-    per_level = lambda *shape: pl.BlockSpec((1,) + shape, lambda i: (i, 0, 0))
-    both = lambda width: pl.BlockSpec((2, 1, members, width), lambda i: (0, i, 0, 0))
     half = jax.ShapeDtypeStruct((levels, members // 2, 2 * BLK), jnp.float32)
+    vmem = pl.BlockSpec(memory_space=pltpu.VMEM)
     return pl.pallas_call(
         increment_kernel,
-        grid=(levels,),
-        in_specs=[
-            pl.BlockSpec(memory_space=pltpu.SMEM),
-            both(2 * BLK),
-            both(BLK),
-            per_level(2 * BLK + 8, BLK),
-            per_level(BLK, BLK),
-            per_level(members, BLK),
-        ],
-        out_specs=(per_level(members // 2, 2 * BLK),) * 2,
+        in_specs=[pl.BlockSpec(memory_space=pltpu.SMEM), vmem, vmem, vmem],
+        out_specs=(vmem, vmem),
         out_shape=(half, half),
         cost_estimate=TINY,
-    )(coefs, w, w_right, own, edge, left)
+    )(coefs, w, w_right, cov)
 
 
 def gather_kernel(mine_ref, got_ref, w_ref, low_ref):
@@ -193,7 +186,7 @@
 
 
 def local(members, weights, taper_table, pair_blocks, pair_taper, pair_batch):
-    member_loc, levels, _ = members.shape
+    member_loc, levels, column_count = members.shape
     ensemble = member_loc * lax.axis_size("member")
     regions = lax.axis_size("region")
     right = [(i, (i + 1) % regions) for i in range(regions)]
@@ -222,8 +215,8 @@
         return pick(x, chip), got[0], last.reshape(-1, BLK)
 
     first, second = to_owner(0), to_owner(1)
-    taken, pair_taper = lax.optimization_barrier((second[1], pair_taper))
-    second = second[0], taken, second[2]
+    taken, pair_taper = lax.optimization_barrier((first[1], pair_taper))
+    first = first[0], taken, first[2]
     tapers = jnp.dot(
         one_hot(pair_taper, taper_table.shape[0]), taper_table, precision=lax.Precision.HIGHEST
     ) / (ensemble - 1)
@@ -240,12 +233,12 @@
     w, low = gathered(mine, lax.ppermute(theirs, "member", SWAP))
     w_right = lax.ppermute(low, "region", left)
 
-    edge, own = covariances(message, *second, after)
-    edges = lax.all_gather(edge, "member", axis_index_groups=GROUPS)
-    from_left = lax.ppermute(outward(after, w, edges), "region", right)
-    owns = lax.all_gather(own, "member", axis_index_groups=GROUPS)
-
-    kept, sent = increments(coefs, w, w_right, owns, edges, from_left)
+    own = covariances(message, *second, after)
+    cov = lax.all_gather(own, "member", axis_index_groups=GROUPS)
+    from_left = lax.ppermute(outward(after, w, cov), "region", right)
+    kept, sent = increments(coefs, w, w_right, cov)
+    from_left = jnp.pad(from_left, ((0, 0), (0, 0), (0, column_count - BLK)))
+    kept, sent = kept + from_left[:, :member_loc], sent + from_left[:, member_loc:]
     came = lax.ppermute(sent, "member", SWAP)
     change = jnp.where(
         core == 0, jnp.concatenate([kept, came]), jnp.concatenate([came, kept])

time: 211 us -> 194 us (0.919)
  the two profiles are of different devices: /device:TPU:95 before, /device:TPU:1 now
where the time goes in v4:
time: 194 us; the launch traced here: 191 us
  starting transfers between devices  83.8 us (43%)
  blocking collectives  59.9 us (31%)
  waiting for transfers between devices  24.3 us (13%)
  Pallas kernels  12.4 us (6%)
  local copies, waits for them, and re-layouts  7.82 us (4%)
  other arithmetic  2.17 us (1%)
    all_gather x1, blocking collectives, local(): cov = lax.all_gather(own, 'member', axis_index_groups=GROUPS)  59.9 us
    ppermute x2, starting transfers between devices, to_owner(): last = lax.ppermute(jnp.stack([pick(x, two), got[1]]), 'member', step_two)  32.1 us
    ppermute x1, starting transfers between devices, local(): lax.ppermute(theirs, 'member', SWAP)  16.1 us
    ppermute x2, starting transfers between devices, to_owner(): lax.ppermute(jnp.stack([pick(x, one), pick(x, both)]), 'member', step_one)  14 us
    ppermute x1, waiting for transfers between devices, local(): from_left = lax.ppermute(outward(after, w, cov), 'region', right)  11.9 us
    ppermute x2, waiting for transfers between devices, to_owner(): lax.ppermute(jnp.stack([pick(x, one), pick(x, both)]), 'member', step_one)  11.2 us
    ppermute x1, starting transfers between devices, local(): came = lax.ppermute(sent, 'member', SWAP)  8.26 us
    ppermute x1, starting transfers between devices, local(): from_left = lax.ppermute(outward(after, w, cov), 'region', right)  7.62 us
  transfers between devices with their start and end apart: 10, of which 5 were waited for; matrix products, arithmetic and copies ran while one was open for 2% of the time, Pallas kernels for 6%

profile of v4, /device:TPU:1, one launch (start us, length us, event | category | flops | bytes accessed | tf_op | source)
XLA Modules:
  0.0 190.9 jit_solution(18184650887761716692)
XLA Ops:
  0.0 0.0 copy-start
  0.0 1.3 copy.17
  1.4 16.1 %collective-permute-start = (f32[4,64,256]{2,1,0:T(8,128)S(1)}, f32[4,64,256]{2,1,0:T(8,128)S(1)}, u32[]{:S(2)}, u32[]{:S(2)}) collective-permute-start(f32[4,64,256]{2,1,0:T(8,128)S(1)} %get-tuple-element.16), channel_id=1, source_target_pairs={{0,128},{128,0},{256,384},{384,256},{512,640},{640,512},{768,896},... | collective-permute-start | bytes 786440 | tf_op jit(solution)/shard_map/ppermute | solution.py:202
  17.4 0.0 copy-done.4
  17.4 0.3 copy.15
  17.8 0.9 dynamic-slice_bitcast_fusion
  18.7 1.9 collective-permute-start.2
  20.6 0.0 copy-start.8
  20.6 0.0 copy-start.9
  20.7 0.7 copy-done.8
  21.3 0.0 copy-done.9
  21.3 0.0 collective-permute-done
  21.4 10.1 %collective-permute-start.1 = (f32[2,128,128]{2,1,0:T(8,128)S(1)}, f32[2,128,128]{2,1,0:T(8,128)S(1)}, u32[]{:S(2)}, u32[]{:S(2)}) collective-permute-start(f32[2,128,128]{2,1,0:T(8,128)S(1)} %pad_maximum_fusion), channel_id=1, source_target_pairs={{0,256},{128,896},{256,0},{384,640},{512,768},{640,384},{768,512},... | collective-permute-start | bytes 393224 | tf_op jit(solution)/shard_map/ppermute | solution.py:213
  31.5 0.7 fusion.6
  32.2 3.9 %collective-permute-start.5 = (f32[2,128,128]{2,1,0:T(8,128)S(1)}, f32[2,128,128]{2,1,0:T(8,128)S(1)}, u32[]{:S(2)}, u32[]{:S(2)}) collective-permute-start(f32[2,128,128]{2,1,0:T(8,128)S(1)} %pad_maximum_fusion.2), channel_id=1, source_target_pairs={{0,256},{128,896},{256,0},{384,640},{512,768},{640,384},{768,512},... | collective-permute-start | bytes 393224 | tf_op jit(solution)/shard_map/ppermute | solution.py:213
  36.1 2.8 %collective-permute-done.1 = f32[2,128,128]{2,1,0:T(8,128)S(1)} collective-permute-done((f32[2,128,128]{2,1,0:T(8,128)S(1)}, f32[2,128,128]{2,1,0:T(8,128)S(1)}, u32[]{:S(2)}, u32[]{:S(2)}) %collective-permute-start.1) | collective-permute-done | bytes 131104 | tf_op jit(solution)/shard_map/ppermute | solution.py:213
  38.9 13.2 %collective-permute-start.4 = (f32[2,128,128]{2,1,0:T(8,128)S(1)}, f32[2,128,128]{2,1,0:T(8,128)S(1)}, u32[]{:S(2)}, u32[]{:S(2)}) collective-permute-start(f32[2,128,128]{2,1,0:T(8,128)S(1)} %pad_maximum_fusion.1), channel_id=1, source_target_pairs={{0,768},{128,384},{256,512},{384,128},{512,256},{640,896},{768,0},... | collective-permute-start | bytes 393224 | tf_op jit(solution)/shard_map/ppermute | solution.py:214
  52.2 8.4 %collective-permute-done.5 = f32[2,128,128]{2,1,0:T(8,128)S(1)} collective-permute-done((f32[2,128,128]{2,1,0:T(8,128)S(1)}, f32[2,128,128]{2,1,0:T(8,128)S(1)}, u32[]{:S(2)}, u32[]{:S(2)}) %collective-permute-start.5) | collective-permute-done | bytes 131104 | tf_op jit(solution)/shard_map/ppermute | solution.py:213
  60.6 0.6 fusion.13
  61.2 18.9 %collective-permute-start.6 = (f32[2,128,128]{2,1,0:T(8,128)S(1)}, f32[2,128,128]{2,1,0:T(8,128)S(1)}, u32[]{:S(2)}, u32[]{:S(2)}) collective-permute-start(f32[2,128,128]{2,1,0:T(8,128)S(1)} %pad_maximum_fusion.3), channel_id=1, source_target_pairs={{0,768},{128,384},{256,512},{384,128},{512,256},{640,896},{768,0},... | collective-permute-start | bytes 393224 | tf_op jit(solution)/shard_map/ppermute | solution.py:214
  80.1 0.2 fusion
  80.3 0.1 select_reduce_fusion.coef_ref
  80.4 0.0 collective-permute-done.4
  80.4 0.5 copy-done.7
  81.0 1.9 %collective-permute-start.7 = (f32[520,128]{1,0:T(8,128)S(1)}, f32[520,128]{1,0:T(8,128)S(1)}, u32[]{:S(2)}, u32[]{:S(2)}) collective-permute-start(f32[520,128]{1,0:T(8,128)S(1)} %select_maximum_fusion.message_ref), channel_id=1, source_target_pairs={{1,0},{2,1},{3,2},{4,3},{5,4},{6,5},{7,6},{8,7},{9,8},{10,9},{11,1... | collective-permute-start | bytes 798728 | tf_op jit(solution)/shard_map/ppermute | solution.py:228
  82.9 0.0 collective-permute-done.2.got_ref
  82.9 0.8 copy-done.10
  83.7 2.3 %shard_map.64 = (f32[2,4,128,256]{3,2,1,0:T(8,128)}, f32[2,4,128,128]{3,2,1,0:T(8,128)}) custom-call(f32[2,4,64,256]{3,2,1,0:T(8,128)} %get-tuple-element.28.mine_ref, f32[2,4,64,256]{3,2,1,0:T(8,128)} %copy-done.10), custom_call_target="tpu_custom_call" | custom-call | flops 49999998976 | bytes 200000000 | tf_op jit(solution)/shard_map/pallas_call | solution.py:170
  86.0 1.9 %shard_map.65 = (bf16[512,128]{1,0:T(8,128)(2,1)}, bf16[512,128]{1,0:T(8,128)(2,1)}, f32[128,128]{1,0:T(8,128)}) custom-call(f32[520,128]{1,0:T(8,128)} %copy-done.3), custom_call_target="tpu_custom_call" | custom-call | flops 1000 | bytes 1000 | tf_op jit(solution)/shard_map/pallas_call | solution.py:81
  87.9 1.9 collective-permute-start.3
  89.8 0.0 collective-permute-done.6
  89.9 0.1 collective-permute-done.7.message_ref
  89.9 0.6 copy-done.6
  90.5 0.1 copy-done.2
  90.6 2.5 %shard_map.66 = f32[392,128]{1,0:T(8,128)} custom-call(bf16[512,128]{1,0:T(8,128)(2,1)} %get-tuple-element.22.high_ref, bf16[512,128]{1,0:T(8,128)(2,1)} %get-tuple-element.23.low_ref, f32[128,128]{1,0:T(8,128)} %get-tuple-element.24.square_ref, f32[128,128]{1,0:T(8,128)} %get-tuple-element.30.kept_ref, f32[128,128]{1,0:T(8,128)} %get-tuple-element.42.got_ref, ...), custom_call_target="tpu_custom_call" | custom-call | flops 1000 | bytes 1000 | tf_op jit(solution)/shard_map/pallas_call | solution.py:82
  93.1 59.9 %all-gather = f32[1568,128]{1,0:T(8,128)} all-gather(f32[392,128]{1,0:T(8,128)} %shard_map.66), channel_id=2, replica_groups={{0,256,512,768},{128,384,640,896},{1,257,513,769},{129,385,641,897},{2,..., dimensions={0}, use_global_device_ids=true | all-gather | bytes 1003520 | tf_op jit(solution)/shard_map/all_gather | solution.py:237
  153.0 2.2 %shard_map.68 = f32[4,128,128]{2,1,0:T(8,128)} custom-call(f32[520,128]{1,0:T(8,128)} %copy-done.2, f32[2,4,128,256]{3,2,1,0:T(8,128)} %get-tuple-element.19.w_ref, f32[4,392,128]{2,1,0:T(8,128)} %bitcast.33), custom_call_target="tpu_custom_call" | custom-call | flops 1000 | bytes 1000 | tf_op jit(solution)/shard_map/pallas_call | solution.py:97
  155.2 7.6 %collective-permute-start.8 = (f32[4,128,128]{2,1,0:T(8,128)}, f32[4,128,128]{2,1,0:T(8,128)S(1)}, u32[]{:S(2)}, u32[]{:S(2)}) collective-permute-start(f32[4,128,128]{2,1,0:T(8,128)} %shard_map.68), channel_id=1, source_target_pairs={{0,1},{1,2},{2,3},{3,4},{4,5},{5,6},{6,7},{7,8},{8,9},{9,10},{10,1... | collective-permute-start | bytes 786440 | tf_op jit(solution)/shard_map/ppermute | solution.py:238
  162.8 0.0 collective-permute-done.3.wr_ref
  162.8 0.0 copy-start.5
  162.8 0.8 copy-done.5
  163.6 3.5 %shard_map.67 = (f32[4,64,256]{2,1,0:T(8,128)}, f32[4,64,256]{2,1,0:T(8,128)}) custom-call(f32[12]{0:T(128)} %copy-done.7, f32[2,4,128,256]{3,2,1,0:T(8,128)} %get-tuple-element.19.w_ref, f32[2,4,128,128]{3,2,1,0:T(8,128)} %copy-done.5, f32[4,392,128]{2,1,0:T(8,128)} %bitcast.34), custom_call_target="tpu_custom_call" | custom-call | flops 1000 | bytes 1000 | tf_op jit(solution)/shard_map/pallas_call | solution.py:150
  167.1 11.9 %collective-permute-done.8 = f32[4,128,128]{2,1,0:T(8,128)S(1)} collective-permute-done((f32[4,128,128]{2,1,0:T(8,128)}, f32[4,128,128]{2,1,0:T(8,128)S(1)}, u32[]{:S(2)}, u32[]{:S(2)}) %collective-permute-start.8) | collective-permute-done | bytes 262176 | tf_op jit(solution)/shard_map/ppermute | solution.py:238
  179.0 1.1 fusion.4
  180.2 8.3 %collective-permute-start.9 = (f32[4,64,256]{2,1,0:T(8,128)S(1)}, f32[4,64,256]{2,1,0:T(8,128)S(1)}, u32[]{:S(2)}, u32[]{:S(2)}) collective-permute-start(f32[4,64,256]{2,1,0:T(8,128)S(1)} %get-tuple-element.36), channel_id=1, source_target_pairs={{0,128},{128,0},{256,384},{384,256},{512,640},{640,512},{768,896},... | collective-permute-start | bytes 786440 | tf_op jit(solution)/shard_map/ppermute | solution.py:242
  188.4 1.1 collective-permute-done.9
  189.6 0.2 fusion.2
  189.8 1.1 copy.18
  (22 shorter events, 0.2 us)
Async XLA Ops:
  0.0 80.1 %copy-start = (f32[8]{0:T(128)S(1)}, f32[8]{0:T(128)}, u32[]{:S(2)}) copy-start(f32[8]{0:T(128)} %param.8) | copy-start | bytes 100
  0.0 17.4 %copy-start.4 = (f32[2,64,8,256]{3,2,1,0:T(8,128)S(1)}, f32[2,64,8,256]{3,2,1,0:T(8,128)}, u32[]{:S(2)}) copy-start(f32[2,64,8,256]{3,2,1,0:T(8,128)} %param.7) | copy-start | bytes 3145732
  1.4 20.0 %collective-permute-start = (f32[4,64,256]{2,1,0:T(8,128)S(1)}, f32[4,64,256]{2,1,0:T(8,128)S(1)}, u32[]{:S(2)}, u32[]{:S(2)}) collective-permute-start(f32[4,64,256]{2,1,0:T(8,128)S(1)} %get-tuple-element.16), channel_id=1, source_target_pairs={{0,128},{128,0},{256,384},{384,256},{512,640},{640,512},{768,896},... | collective-permute-start | bytes 786440 | tf_op jit(solution)/shard_map/ppermute | solution.py:202
  18.7 64.2 %collective-permute-start.2 = (f32[2,4,64,256]{3,2,1,0:T(8,128)S(1)}, f32[2,4,64,256]{3,2,1,0:T(8,128)S(1)}, u32[]{:S(2)}, u32[]{:S(2)}) collective-permute-start(f32[2,4,64,256]{3,2,1,0:T(8,128)S(1)} %get-tuple-element.27), channel_id=1, source_target_pairs={{0,128},{128,0},{256,384},{384,256},{512,640},{640,512},{768,896},... | collective-permute-start | bytes 1572872 | tf_op jit(solution)/shard_map/ppermute | solution.py:233
  20.6 0.7 copy-start.8
  20.6 0.7 copy-start.9
  21.4 17.5 %collective-permute-start.1 = (f32[2,128,128]{2,1,0:T(8,128)S(1)}, f32[2,128,128]{2,1,0:T(8,128)S(1)}, u32[]{:S(2)}, u32[]{:S(2)}) collective-permute-start(f32[2,128,128]{2,1,0:T(8,128)S(1)} %pad_maximum_fusion), channel_id=1, source_target_pairs={{0,256},{128,896},{256,0},{384,640},{512,768},{640,384},{768,512},... | collective-permute-start | bytes 393224 | tf_op jit(solution)/shard_map/ppermute | solution.py:213
  32.2 28.4 %collective-permute-start.5 = (f32[2,128,128]{2,1,0:T(8,128)S(1)}, f32[2,128,128]{2,1,0:T(8,128)S(1)}, u32[]{:S(2)}, u32[]{:S(2)}) collective-permute-start(f32[2,128,128]{2,1,0:T(8,128)S(1)} %pad_maximum_fusion.2), channel_id=1, source_target_pairs={{0,256},{128,896},{256,0},{384,640},{512,768},{640,384},{768,512},... | collective-permute-start | bytes 393224 | tf_op jit(solution)/shard_map/ppermute | solution.py:213
  38.9 41.5 %collective-permute-start.4 = (f32[2,128,128]{2,1,0:T(8,128)S(1)}, f32[2,128,128]{2,1,0:T(8,128)S(1)}, u32[]{:S(2)}, u32[]{:S(2)}) collective-permute-start(f32[2,128,128]{2,1,0:T(8,128)S(1)} %pad_maximum_fusion.1), channel_id=1, source_target_pairs={{0,768},{128,384},{256,512},{384,128},{512,256},{640,896},{768,0},... | collective-permute-start | bytes 393224 | tf_op jit(solution)/shard_map/ppermute | solution.py:214
  61.2 18.9 %copy-start.11 = (s32[8]{0:T(128)S(1)}, s32[8]{0:T(128)}, u32[]{:S(2)}) copy-start(s32[8]{0:T(128)} %param.10) | copy-start | bytes 100
  61.2 28.6 %collective-permute-start.6 = (f32[2,128,128]{2,1,0:T(8,128)S(1)}, f32[2,128,128]{2,1,0:T(8,128)S(1)}, u32[]{:S(2)}, u32[]{:S(2)}) collective-permute-start(f32[2,128,128]{2,1,0:T(8,128)S(1)} %pad_maximum_fusion.3), channel_id=1, source_target_pairs={{0,768},{128,384},{256,512},{384,128},{512,256},{640,896},{768,0},... | collective-permute-start | bytes 393224 | tf_op jit(solution)/shard_map/ppermute | solution.py:214
  80.4 0.5 copy-start.7
  81.0 5.0 %copy-start.3 = (f32[520,128]{1,0:T(8,128)}, f32[520,128]{1,0:T(8,128)S(1)}, u32[]{:S(2)}) copy-start(f32[520,128]{1,0:T(8,128)S(1)} %select_maximum_fusion.message_ref) | copy-start | bytes 798724
  81.0 8.9 %collective-permute-start.7 = (f32[520,128]{1,0:T(8,128)S(1)}, f32[520,128]{1,0:T(8,128)S(1)}, u32[]{:S(2)}, u32[]{:S(2)}) collective-permute-start(f32[520,128]{1,0:T(8,128)S(1)} %select_maximum_fusion.message_ref), channel_id=1, source_target_pairs={{1,0},{2,1},{3,2},{4,3},{5,4},{6,5},{7,6},{8,7},{9,8},{10,9},{11,1... | collective-permute-start | bytes 798728 | tf_op jit(solution)/shard_map/ppermute | solution.py:228
  82.9 0.8 copy-start.10
  87.9 74.9 %collective-permute-start.3 = (f32[2,4,128,128]{3,2,1,0:T(8,128)}, f32[2,4,128,128]{3,2,1,0:T(8,128)S(1)}, u32[]{:S(2)}, u32[]{:S(2)}) collective-permute-start(f32[2,4,128,128]{3,2,1,0:T(8,128)} %get-tuple-element.20), channel_id=1, source_target_pairs={{1,0},{2,1},{3,2},{4,3},{5,4},{6,5},{7,6},{8,7},{9,8},{10,9},{11,1... | collective-permute-start | bytes 1572872 | tf_op jit(solution)/shard_map/ppermute | solution.py:234
  89.9 0.7 copy-start.6
  89.9 0.7 copy-start.2
  155.2 23.9 %collective-permute-start.8 = (f32[4,128,128]{2,1,0:T(8,128)}, f32[4,128,128]{2,1,0:T(8,128)S(1)}, u32[]{:S(2)}, u32[]{:S(2)}) collective-permute-start(f32[4,128,128]{2,1,0:T(8,128)} %shard_map.68), channel_id=1, source_target_pairs={{0,1},{1,2},{2,3},{3,4},{4,5},{5,6},{6,7},{7,8},{8,9},{9,10},{10,1... | collective-permute-start | bytes 786440 | tf_op jit(solution)/shard_map/ppermute | solution.py:238
  162.8 0.8 copy-start.5
  179.0 10.6 %copy-start.1 = (f32[64,8,256]{2,1,0:T(8,128)S(1)}, f32[64,8,256]{2,1,0:T(8,128)}, u32[]{:S(2)}) copy-start(f32[64,8,256]{2,1,0:T(8,128)} %param.6) | copy-start | bytes 1572868
  180.2 9.4 %collective-permute-start.9 = (f32[4,64,256]{2,1,0:T(8,128)S(1)}, f32[4,64,256]{2,1,0:T(8,128)S(1)}, u32[]{:S(2)}, u32[]{:S(2)}) collective-permute-start(f32[4,64,256]{2,1,0:T(8,128)S(1)} %get-tuple-element.36), channel_id=1, source_target_pairs={{0,128},{128,0},{256,384},{384,256},{512,640},{640,512},{768,896},... | collective-permute-start | bytes 786440 | tf_op jit(solution)/shard_map/ppermute | solution.py:242

commit v5 on v4

--- a/solution.py
+++ b/solution.py
@@ -55,7 +55,7 @@
 
 
 def covariance_kernel(
-    high_ref, low_ref, square_ref, kept_ref, got_ref, last_ref, message_ref, out_ref
+    high_ref, low_ref, square_ref, kept_ref, got_ref, last_ref, message_ref, ahead_ref, out_ref
 ):
     second = centred(kept_ref[...], got_ref[...], last_ref[...])
     first = high_ref[...], low_ref[...]
@@ -74,16 +74,17 @@
 TINY = pl.CostEstimate(flops=1000, bytes_accessed=1000, transcendentals=0)
 
 
-def covariances(message, kept, got, last, after):
+def covariances(message, kept, got, last, after, ahead):
     ensemble = message.shape[0] - 8
     square = jax.ShapeDtypeStruct((BLK, BLK), jnp.float32)
     half = jax.ShapeDtypeStruct((ensemble, BLK), jnp.bfloat16)
-    first = pl.pallas_call(first_kernel, out_shape=(half, half, square), cost_estimate=TINY)(message)
+    first = pl.pallas_call(first_kernel, out_shape=(half, half, square), cost_estimate=LONG)(message)
     return pl.pallas_call(
         covariance_kernel,
+        in_specs=[pl.BlockSpec(memory_space=pltpu.VMEM)] * 7 + [pl.BlockSpec(memory_space=pl.ANY)],
         out_shape=jax.ShapeDtypeStruct((3 * BLK + 8, BLK), jnp.float32),
         cost_estimate=TINY,
-    )(*first, kept, got, last, after)
+    )(*first, kept, got, last, after, ahead)
 
 
 def outward_kernel(message_ref, w_ref, cov_ref, out_ref):
@@ -233,7 +234,7 @@
     w, low = gathered(mine, lax.ppermute(theirs, "member", SWAP))
     w_right = lax.ppermute(low, "region", left)
 
-    own = covariances(message, *second, after)
+    own = covariances(message, *second, after, w_right)
     cov = lax.all_gather(own, "member", axis_index_groups=GROUPS)
     from_left = lax.ppermute(outward(after, w, cov), "region", right)
     kept, sent = increments(coefs, w, w_right, cov)

time: 194 us -> 201 us (1.036); the launches traced: 191 us -> 200 us
  waiting for transfers between devices: 24.3 us -> 36.6 us
  starting transfers between devices: 83.8 us -> 80.7 us
    ppermute x1, waiting for transfers between devices: 0.06 us -> 11.5 us  [local(): after = lax.ppermute(message, 'region', left)]
    ppermute x1, starting transfers between devices: 7.62 us -> 1.91 us  [local(): from_left = lax.ppermute(outward(after, w, cov), 'region', right)]
    ppermute x1, starting transfers between devices: 8.26 us -> 10.9 us  [local(): came = lax.ppermute(sent, 'member', SWAP)]
  transfers between devices with their start and end apart: 10 -> 10, of which waited for: 5 -> 5; matrix products, arithmetic and copies ran while one was open for 2% -> 1% of each run, Pallas kernels for 6% -> 4%
where the time goes in v5:
time: 201 us; the launch traced here: 200 us
  starting transfers between devices  80.7 us (40%)
  blocking collectives  60.9 us (30%)
  waiting for transfers between devices  36.6 us (18%)
  Pallas kernels  12.4 us (6%)
  local copies, waits for them, and re-layouts  6.7 us (3%)
  other arithmetic  2.16 us (1%)
    all_gather x1, blocking collectives, local(): cov = lax.all_gather(own, 'member', axis_index_groups=GROUPS)  60.9 us
    ppermute x2, starting transfers between devices, to_owner(): last = lax.ppermute(jnp.stack([pick(x, two), got[1]]), 'member', step_two)  32.1 us
    ppermute x1, starting transfers between devices, local(): lax.ppermute(theirs, 'member', SWAP)  16.1 us
    ppermute x2, starting transfers between devices, to_owner(): lax.ppermute(jnp.stack([pick(x, one), pick(x, both)]), 'member', step_one)  14 us
    ppermute x1, waiting for transfers between devices, local(): from_left = lax.ppermute(outward(after, w, cov), 'region', right)  12.7 us
    ppermute x1, waiting for transfers between devices, local(): after = lax.ppermute(message, 'region', left)  11.5 us
    ppermute x2, waiting for transfers between devices, to_owner(): lax.ppermute(jnp.stack([pick(x, one), pick(x, both)]), 'member', step_one)  11.2 us
    ppermute x1, starting transfers between devices, local(): came = lax.ppermute(sent, 'member', SWAP)  10.9 us
  transfers between devices with their start and end apart: 10, of which 5 were waited for; matrix products, arithmetic and copies ran while one was open for 1% of the time, Pallas kernels for 4%

profile of v5, /device:TPU:1, one launch (start us, length us, event | category | flops | bytes accessed | tf_op | source)
XLA Modules:
  0.0 200.0 jit_solution(5075831532978837605)
XLA Ops:
  0.0 0.0 copy-start
  0.0 1.3 copy.17
  1.4 16.1 %collective-permute-start = (f32[4,64,256]{2,1,0:T(8,128)S(1)}, f32[4,64,256]{2,1,0:T(8,128)S(1)}, u32[]{:S(2)}, u32[]{:S(2)}) collective-permute-start(f32[4,64,256]{2,1,0:T(8,128)S(1)} %get-tuple-element.16), channel_id=1, source_target_pairs={{0,128},{128,0},{256,384},{384,256},{512,640},{640,512},{768,896},... | collective-permute-start | bytes 786440 | tf_op jit(solution)/shard_map/ppermute | solution.py:203
  17.4 0.0 copy-done.4
  17.4 0.3 copy.15
  17.8 0.9 dynamic-slice_bitcast_fusion
  18.7 1.9 collective-permute-start.2
  20.6 0.0 copy-start.8
  20.6 0.0 copy-start.9
  20.7 0.7 copy-done.8
  21.3 0.0 copy-done.9
  21.3 0.0 collective-permute-done
  21.4 10.1 %collective-permute-start.1 = (f32[2,128,128]{2,1,0:T(8,128)S(1)}, f32[2,128,128]{2,1,0:T(8,128)S(1)}, u32[]{:S(2)}, u32[]{:S(2)}) collective-permute-start(f32[2,128,128]{2,1,0:T(8,128)S(1)} %pad_maximum_fusion), channel_id=1, source_target_pairs={{0,256},{128,896},{256,0},{384,640},{512,768},{640,384},{768,512},... | collective-permute-start | bytes 393224 | tf_op jit(solution)/shard_map/ppermute | solution.py:214
  31.5 0.6 fusion.6
  32.2 3.9 %collective-permute-start.5 = (f32[2,128,128]{2,1,0:T(8,128)S(1)}, f32[2,128,128]{2,1,0:T(8,128)S(1)}, u32[]{:S(2)}, u32[]{:S(2)}) collective-permute-start(f32[2,128,128]{2,1,0:T(8,128)S(1)} %pad_maximum_fusion.2), channel_id=1, source_target_pairs={{0,256},{128,896},{256,0},{384,640},{512,768},{640,384},{768,512},... | collective-permute-start | bytes 393224 | tf_op jit(solution)/shard_map/ppermute | solution.py:214
  36.1 2.8 %collective-permute-done.1 = f32[2,128,128]{2,1,0:T(8,128)S(1)} collective-permute-done((f32[2,128,128]{2,1,0:T(8,128)S(1)}, f32[2,128,128]{2,1,0:T(8,128)S(1)}, u32[]{:S(2)}, u32[]{:S(2)}) %collective-permute-start.1) | collective-permute-done | bytes 131104 | tf_op jit(solution)/shard_map/ppermute | solution.py:214
  38.9 13.2 %collective-permute-start.4 = (f32[2,128,128]{2,1,0:T(8,128)S(1)}, f32[2,128,128]{2,1,0:T(8,128)S(1)}, u32[]{:S(2)}, u32[]{:S(2)}) collective-permute-start(f32[2,128,128]{2,1,0:T(8,128)S(1)} %pad_maximum_fusion.1), channel_id=1, source_target_pairs={{0,768},{128,384},{256,512},{384,128},{512,256},{640,896},{768,0},... | collective-permute-start | bytes 393224 | tf_op jit(solution)/shard_map/ppermute | solution.py:215
  52.2 8.4 %collective-permute-done.5 = f32[2,128,128]{2,1,0:T(8,128)S(1)} collective-permute-done((f32[2,128,128]{2,1,0:T(8,128)S(1)}, f32[2,128,128]{2,1,0:T(8,128)S(1)}, u32[]{:S(2)}, u32[]{:S(2)}) %collective-permute-start.5) | collective-permute-done | bytes 131104 | tf_op jit(solution)/shard_map/ppermute | solution.py:214
  60.6 0.6 fusion.13
  61.2 18.9 %collective-permute-start.6 = (f32[2,128,128]{2,1,0:T(8,128)S(1)}, f32[2,128,128]{2,1,0:T(8,128)S(1)}, u32[]{:S(2)}, u32[]{:S(2)}) collective-permute-start(f32[2,128,128]{2,1,0:T(8,128)S(1)} %pad_maximum_fusion.3), channel_id=1, source_target_pairs={{0,768},{128,384},{256,512},{384,128},{512,256},{640,896},{768,0},... | collective-permute-start | bytes 393224 | tf_op jit(solution)/shard_map/ppermute | solution.py:215
  80.1 0.0 copy-done
  80.1 0.0 copy-done.11
  80.1 0.2 fusion
  80.3 0.1 select_reduce_fusion.coef_ref
  80.4 0.0 collective-permute-done.2.got_ref
  80.5 0.8 copy-done.10
  81.2 2.3 %shard_map.64 = (f32[2,4,128,256]{3,2,1,0:T(8,128)}, f32[2,4,128,128]{3,2,1,0:T(8,128)}) custom-call(f32[2,4,64,256]{3,2,1,0:T(8,128)} %get-tuple-element.28.mine_ref, f32[2,4,64,256]{3,2,1,0:T(8,128)} %copy-done.10), custom_call_target="tpu_custom_call" | custom-call | flops 49999998976 | bytes 200000000 | tf_op jit(solution)/shard_map/pallas_call | solution.py:171
  83.5 1.9 collective-permute-start.3
  85.4 0.0 collective-permute-done.4
  85.5 0.0 copy-start.5
  85.5 1.9 collective-permute-start.7
  87.4 2.0 shard_map.65
  89.4 0.0 collective-permute-done.6
  89.4 11.5 %collective-permute-done.7.message_ref = f32[520,128]{1,0:T(8,128)S(1)} collective-permute-done((f32[520,128]{1,0:T(8,128)S(1)}, f32[520,128]{1,0:T(8,128)S(1)}, u32[]{:S(2)}, u32[]{:S(2)}) %collective-permute-start.7) | collective-permute-done | bytes 266272 | tf_op jit(solution)/shard_map/ppermute | solution.py:229
  100.9 0.0 collective-permute-done.3.ahead_ref.wr_ref
  100.9 0.7 copy-done.3
  101.6 0.2 copy-done.2
  101.8 2.5 %shard_map.66 = f32[392,128]{1,0:T(8,128)} custom-call(bf16[512,128]{1,0:T(8,128)(2,1)} %get-tuple-element.22.high_ref, bf16[512,128]{1,0:T(8,128)(2,1)} %get-tuple-element.23.low_ref, f32[128,128]{1,0:T(8,128)} %get-tuple-element.24.square_ref, f32[128,128]{1,0:T(8,128)} %get-tuple-element.30.kept_ref, f32[128,128]{1,0:T(8,128)} %get-tuple-element.42.got_ref, ...), custom_call_target="tpu_custom_call" | custom-call | flops 1000 | bytes 1000 | tf_op jit(solution)/shard_map/pallas_call | solution.py:82
  104.3 60.9 %all-gather = f32[1568,128]{1,0:T(8,128)} all-gather(f32[392,128]{1,0:T(8,128)} %shard_map.66), channel_id=2, replica_groups={{0,256,512,768},{128,384,640,896},{1,257,513,769},{129,385,641,897},{2,..., dimensions={0}, use_global_device_ids=true | all-gather | bytes 1003520 | tf_op jit(solution)/shard_map/all_gather | solution.py:238
  165.2 2.2 %shard_map.68 = f32[4,128,128]{2,1,0:T(8,128)} custom-call(f32[520,128]{1,0:T(8,128)} %copy-done.3, f32[2,4,128,256]{3,2,1,0:T(8,128)} %get-tuple-element.19.w_ref, f32[4,392,128]{2,1,0:T(8,128)} %bitcast.33), custom_call_target="tpu_custom_call" | custom-call | flops 1000 | bytes 1000 | tf_op jit(solution)/shard_map/pallas_call | solution.py:98
  167.4 1.9 collective-permute-start.8
  169.3 3.5 %shard_map.67 = (f32[4,64,256]{2,1,0:T(8,128)}, f32[4,64,256]{2,1,0:T(8,128)}) custom-call(f32[12]{0:T(128)} %copy-done.7, f32[2,4,128,256]{3,2,1,0:T(8,128)} %get-tuple-element.19.w_ref, f32[2,4,128,128]{3,2,1,0:T(8,128)} %copy-done.2, f32[4,392,128]{2,1,0:T(8,128)} %bitcast.34), custom_call_target="tpu_custom_call" | custom-call | flops 1000 | bytes 1000 | tf_op jit(solution)/shard_map/pallas_call | solution.py:151
  172.8 12.7 %collective-permute-done.8 = f32[4,128,128]{2,1,0:T(8,128)S(1)} collective-permute-done((f32[4,128,128]{2,1,0:T(8,128)}, f32[4,128,128]{2,1,0:T(8,128)S(1)}, u32[]{:S(2)}, u32[]{:S(2)}) %collective-permute-start.8) | collective-permute-done | bytes 262176 | tf_op jit(solution)/shard_map/ppermute | solution.py:239
  185.5 1.1 fusion.4
  186.7 10.9 %collective-permute-start.9 = (f32[4,64,256]{2,1,0:T(8,128)S(1)}, f32[4,64,256]{2,1,0:T(8,128)S(1)}, u32[]{:S(2)}, u32[]{:S(2)}) collective-permute-start(f32[4,64,256]{2,1,0:T(8,128)S(1)} %get-tuple-element.36), channel_id=1, source_target_pairs={{0,128},{128,0},{256,384},{384,256},{512,640},{640,512},{768,896},... | collective-permute-start | bytes 786440 | tf_op jit(solution)/shard_map/ppermute | solution.py:243
  197.6 1.1 collective-permute-done.9
  198.7 0.2 fusion.2
  198.9 1.1 copy.18
  (22 shorter events, 0.2 us)
Async XLA Ops:
  0.0 80.1 %copy-start = (f32[8]{0:T(128)S(1)}, f32[8]{0:T(128)}, u32[]{:S(2)}) copy-start(f32[8]{0:T(128)} %param.8) | copy-start | bytes 100
  0.0 17.4 %copy-start.4 = (f32[2,64,8,256]{3,2,1,0:T(8,128)S(1)}, f32[2,64,8,256]{3,2,1,0:T(8,128)}, u32[]{:S(2)}) copy-start(f32[2,64,8,256]{3,2,1,0:T(8,128)} %param.7) | copy-start | bytes 3145732
  1.4 20.0 %collective-permute-start = (f32[4,64,256]{2,1,0:T(8,128)S(1)}, f32[4,64,256]{2,1,0:T(8,128)S(1)}, u32[]{:S(2)}, u32[]{:S(2)}) collective-permute-start(f32[4,64,256]{2,1,0:T(8,128)S(1)} %get-tuple-element.16), channel_id=1, source_target_pairs={{0,128},{128,0},{256,384},{384,256},{512,640},{640,512},{768,896},... | collective-permute-start | bytes 786440 | tf_op jit(solution)/shard_map/ppermute | solution.py:203
  18.7 61.8 %collective-permute-start.2 = (f32[2,4,64,256]{3,2,1,0:T(8,128)S(1)}, f32[2,4,64,256]{3,2,1,0:T(8,128)S(1)}, u32[]{:S(2)}, u32[]{:S(2)}) collective-permute-start(f32[2,4,64,256]{3,2,1,0:T(8,128)S(1)} %get-tuple-element.27), channel_id=1, source_target_pairs={{0,128},{128,0},{256,384},{384,256},{512,640},{640,512},{768,896},... | collective-permute-start | bytes 1572872 | tf_op jit(solution)/shard_map/ppermute | solution.py:234
  20.6 0.7 copy-start.8
  20.6 0.7 copy-start.9
  21.4 17.5 %collective-permute-start.1 = (f32[2,128,128]{2,1,0:T(8,128)S(1)}, f32[2,128,128]{2,1,0:T(8,128)S(1)}, u32[]{:S(2)}, u32[]{:S(2)}) collective-permute-start(f32[2,128,128]{2,1,0:T(8,128)S(1)} %pad_maximum_fusion), channel_id=1, source_target_pairs={{0,256},{128,896},{256,0},{384,640},{512,768},{640,384},{768,512},... | collective-permute-start | bytes 393224 | tf_op jit(solution)/shard_map/ppermute | solution.py:214
  32.2 28.4 %collective-permute-start.5 = (f32[2,128,128]{2,1,0:T(8,128)S(1)}, f32[2,128,128]{2,1,0:T(8,128)S(1)}, u32[]{:S(2)}, u32[]{:S(2)}) collective-permute-start(f32[2,128,128]{2,1,0:T(8,128)S(1)} %pad_maximum_fusion.2), channel_id=1, source_target_pairs={{0,256},{128,896},{256,0},{384,640},{512,768},{640,384},{768,512},... | collective-permute-start | bytes 393224 | tf_op jit(solution)/shard_map/ppermute | solution.py:214
  38.9 46.5 %collective-permute-start.4 = (f32[2,128,128]{2,1,0:T(8,128)S(1)}, f32[2,128,128]{2,1,0:T(8,128)S(1)}, u32[]{:S(2)}, u32[]{:S(2)}) collective-permute-start(f32[2,128,128]{2,1,0:T(8,128)S(1)} %pad_maximum_fusion.1), channel_id=1, source_target_pairs={{0,768},{128,384},{256,512},{384,128},{512,256},{640,896},{768,0},... | collective-permute-start | bytes 393224 | tf_op jit(solution)/shard_map/ppermute | solution.py:215
  61.2 18.9 %copy-start.11 = (s32[8]{0:T(128)S(1)}, s32[8]{0:T(128)}, u32[]{:S(2)}) copy-start(s32[8]{0:T(128)} %param.10) | copy-start | bytes 100
  61.2 28.1 %collective-permute-start.6 = (f32[2,128,128]{2,1,0:T(8,128)S(1)}, f32[2,128,128]{2,1,0:T(8,128)S(1)}, u32[]{:S(2)}, u32[]{:S(2)}) collective-permute-start(f32[2,128,128]{2,1,0:T(8,128)S(1)} %pad_maximum_fusion.3), channel_id=1, source_target_pairs={{0,768},{128,384},{256,512},{384,128},{512,256},{640,896},{768,0},... | collective-permute-start | bytes 393224 | tf_op jit(solution)/shard_map/ppermute | solution.py:215
  80.4 5.0 %copy-start.7 = (f32[12]{0:T(128)}, f32[12]{0:T(128)S(1)}, u32[]{:S(2)}) copy-start(f32[12]{0:T(128)S(1)} %select_reduce_fusion.coef_ref) | copy-start | bytes 148
  80.4 0.8 copy-start.10
  83.5 17.4 %collective-permute-start.3 = (f32[2,4,128,128]{3,2,1,0:T(8,128)}, f32[2,4,128,128]{3,2,1,0:T(8,128)S(1)}, u32[]{:S(2)}, u32[]{:S(2)}) collective-permute-start(f32[2,4,128,128]{3,2,1,0:T(8,128)} %get-tuple-element.20), channel_id=1, source_target_pairs={{1,0},{2,1},{3,2},{4,3},{5,4},{6,5},{7,6},{8,7},{9,8},{10,9},{11,1... | collective-permute-start | bytes 1572872 | tf_op jit(solution)/shard_map/ppermute | solution.py:235
  85.5 1.9 copy-start.5
  85.5 15.4 %collective-permute-start.7 = (f32[520,128]{1,0:T(8,128)S(1)}, f32[520,128]{1,0:T(8,128)S(1)}, u32[]{:S(2)}, u32[]{:S(2)}) collective-permute-start(f32[520,128]{1,0:T(8,128)S(1)} %select_maximum_fusion.message_ref), channel_id=1, source_target_pairs={{1,0},{2,1},{3,2},{4,3},{5,4},{6,5},{7,6},{8,7},{9,8},{10,9},{11,1... | collective-permute-start | bytes 798728 | tf_op jit(solution)/shard_map/ppermute | solution.py:229
  89.4 11.5 %copy-start.6 = (f32[2,128,128]{2,1,0:T(8,128)}, f32[2,128,128]{2,1,0:T(8,128)S(1)}, u32[]{:S(2)}) copy-start(f32[2,128,128]{2,1,0:T(8,128)S(1)} %collective-permute-done.6) | copy-start | bytes 393220
  100.9 0.7 copy-start.3
  100.9 0.9 copy-start.2
  167.4 18.1 %collective-permute-start.8 = (f32[4,128,128]{2,1,0:T(8,128)}, f32[4,128,128]{2,1,0:T(8,128)S(1)}, u32[]{:S(2)}, u32[]{:S(2)}) collective-permute-start(f32[4,128,128]{2,1,0:T(8,128)} %shard_map.68), channel_id=1, source_target_pairs={{0,1},{1,2},{2,3},{3,4},{4,5},{5,6},{6,7},{7,8},{8,9},{9,10},{10,1... | collective-permute-start | bytes 786440 | tf_op jit(solution)/shard_map/ppermute | solution.py:239
  185.5 13.2 %copy-start.1 = (f32[64,8,256]{2,1,0:T(8,128)S(1)}, f32[64,8,256]{2,1,0:T(8,128)}, u32[]{:S(2)}) copy-start(f32[64,8,256]{2,1,0:T(8,128)} %param.6) | copy-start | bytes 1572868
  186.7 12.0 %collective-permute-start.9 = (f32[4,64,256]{2,1,0:T(8,128)S(1)}, f32[4,64,256]{2,1,0:T(8,128)S(1)}, u32[]{:S(2)}, u32[]{:S(2)}) collective-permute-start(f32[4,64,256]{2,1,0:T(8,128)S(1)} %get-tuple-element.36), channel_id=1, source_target_pairs={{0,128},{128,0},{256,384},{384,256},{512,640},{640,512},{768,896},... | collective-permute-start | bytes 786440 | tf_op jit(solution)/shard_map/ppermute | solution.py:243

commit v6 on v4

--- a/solution.py
+++ b/solution.py
@@ -78,7 +78,7 @@
     ensemble = message.shape[0] - 8
     square = jax.ShapeDtypeStruct((BLK, BLK), jnp.float32)
     half = jax.ShapeDtypeStruct((ensemble, BLK), jnp.bfloat16)
-    first = pl.pallas_call(first_kernel, out_shape=(half, half, square), cost_estimate=TINY)(message)
+    first = pl.pallas_call(first_kernel, out_shape=(half, half, square), cost_estimate=LONG)(message)
     return pl.pallas_call(
         covariance_kernel,
         out_shape=jax.ShapeDtypeStruct((3 * BLK + 8, BLK), jnp.float32),
@@ -224,13 +224,14 @@
     slot = targets * 6 + (pair_blocks[:, 1] - targets) * 2 + pair_batch
     coefs = jnp.sum(one_hot(slot, 12) * tapers[:, None], axis=0)
     rows = jnp.pad(coefs[None], ((0, 7), (0, BLK - 12)))
-    message = jnp.concatenate([*first, rows])
-    after = lax.ppermute(message, "region", left)
-
     w = jnp.transpose(weights, (0, 2, 1, 3))
     mine = lax.dynamic_slice_in_dim(w, core * half, half, 1)
     theirs = lax.dynamic_slice_in_dim(w, (1 - core) * half, half, 1)
     w, low = gathered(mine, lax.ppermute(theirs, "member", SWAP))
+    rows, low = lax.optimization_barrier((rows, low))
+    message = jnp.concatenate([*first, rows])
+    after = lax.ppermute(message, "region", left)
+
     w_right = lax.ppermute(low, "region", left)
 
     own = covariances(message, *second, after)

time: 194 us -> 200 us (1.031); the launches traced: 191 us -> 199 us
  waiting for transfers between devices: 24.3 us -> 30 us
  starting transfers between devices: 83.8 us -> 89.2 us
  blocking collectives: 59.9 us -> 57.3 us
    ppermute x1, starting transfers between devices: 8.26 us -> 16.3 us  [local(): came = lax.ppermute(sent, 'member', SWAP)]
    ppermute x1, waiting for transfers between devices: 11.9 us -> 15.3 us  [local(): from_left = lax.ppermute(outward(after, w, cov), 'region', right)]
    ppermute x1, starting transfers between devices: 7.62 us -> 4.81 us  [local(): from_left = lax.ppermute(outward(after, w, cov), 'region', right)]
    all_gather x1, blocking collectives: 59.9 us -> 57.3 us  [local(): cov = lax.all_gather(own, 'member', axis_index_groups=GROUPS)]
    ppermute x1, waiting for transfers between devices: 0.06 us -> 2.37 us  [local(): after = lax.ppermute(message, 'region', left)]
    unnamed x25 -> x27, local copies, waits for them, and re-layouts: 4.78 us -> 4.76 us
  transfers between devices with their start and end apart: 10 -> 10, of which waited for: 5 -> 5; matrix products, arithmetic and copies ran while one was open for 2% -> 1% of each run, Pallas kernels for 6% -> 6%
where the time goes in v6:
time: 200 us; the launch traced here: 199 us
  starting transfers between devices  89.2 us (45%)
  blocking collectives  57.3 us (29%)
  waiting for transfers between devices  30 us (15%)
  Pallas kernels  12.4 us (6%)
  local copies, waits for them, and re-layouts  7.8 us (4%)
  other arithmetic  2.16 us (1%)
    all_gather x1, blocking collectives, local(): cov = lax.all_gather(own, 'member', axis_index_groups=GROUPS)  57.3 us
    ppermute x2, starting transfers between devices, to_owner(): last = lax.ppermute(jnp.stack([pick(x, two), got[1]]), 'member', step_two)  32.1 us
    ppermute x1, starting transfers between devices, local(): came = lax.ppermute(sent, 'member', SWAP)  16.3 us
    ppermute x1, starting transfers between devices, local(): lax.ppermute(theirs, 'member', SWAP)  16.1 us
    ppermute x1, waiting for transfers between devices, local(): from_left = lax.ppermute(outward(after, w, cov), 'region', right)  15.3 us
    ppermute x2, starting transfers between devices, to_owner(): lax.ppermute(jnp.stack([pick(x, one), pick(x, both)]), 'member', step_one)  14 us
    ppermute x2, waiting for transfers between devices, to_owner(): lax.ppermute(jnp.stack([pick(x, one), pick(x, both)]), 'member', step_one)  11.2 us
    ppermute x1, starting transfers between devices, local(): from_left = lax.ppermute(outward(after, w, cov), 'region', right)  4.81 us
  transfers between devices with their start and end apart: 10, of which 5 were waited for; matrix products, arithmetic and copies ran while one was open for 1% of the time, Pallas kernels for 6%

profile of v6, /device:TPU:1, one launch (start us, length us, event | category | flops | bytes accessed | tf_op | source)
XLA Modules:
  0.0 199.3 jit_solution(5292029503797222469)
XLA Ops:
  0.0 1.3 copy.17
  1.4 16.1 %collective-permute-start = (f32[4,64,256]{2,1,0:T(8,128)S(1)}, f32[4,64,256]{2,1,0:T(8,128)S(1)}, u32[]{:S(2)}, u32[]{:S(2)}) collective-permute-start(f32[4,64,256]{2,1,0:T(8,128)S(1)} %get-tuple-element.18), channel_id=1, source_target_pairs={{0,128},{128,0},{256,384},{384,256},{512,640},{640,512},{768,896},... | collective-permute-start | bytes 786440 | tf_op jit(solution)/shard_map/ppermute | solution.py:202
  17.4 0.0 copy-done.3
  17.4 0.3 copy.15
  17.8 0.9 dynamic-slice_bitcast_fusion
  18.7 1.9 collective-permute-start.2
  20.6 0.0 copy-start.8
  20.6 0.0 copy-start.9
  20.7 0.7 copy-done.8
  21.3 0.0 collective-permute-done
  21.4 10.1 %collective-permute-start.1 = (f32[2,128,128]{2,1,0:T(8,128)S(1)}, f32[2,128,128]{2,1,0:T(8,128)S(1)}, u32[]{:S(2)}, u32[]{:S(2)}) collective-permute-start(f32[2,128,128]{2,1,0:T(8,128)S(1)} %pad_maximum_fusion.1), channel_id=1, source_target_pairs={{0,256},{128,896},{256,0},{384,640},{512,768},{640,384},{768,512},... | collective-permute-start | bytes 393224 | tf_op jit(solution)/shard_map/ppermute | solution.py:213
  31.5 0.6 fusion.6
  32.2 3.9 %collective-permute-start.5 = (f32[2,128,128]{2,1,0:T(8,128)S(1)}, f32[2,128,128]{2,1,0:T(8,128)S(1)}, u32[]{:S(2)}, u32[]{:S(2)}) collective-permute-start(f32[2,128,128]{2,1,0:T(8,128)S(1)} %pad_maximum_fusion.3), channel_id=1, source_target_pairs={{0,256},{128,896},{256,0},{384,640},{512,768},{640,384},{768,512},... | collective-permute-start | bytes 393224 | tf_op jit(solution)/shard_map/ppermute | solution.py:213
  36.1 2.8 %collective-permute-done.1 = f32[2,128,128]{2,1,0:T(8,128)S(1)} collective-permute-done((f32[2,128,128]{2,1,0:T(8,128)S(1)}, f32[2,128,128]{2,1,0:T(8,128)S(1)}, u32[]{:S(2)}, u32[]{:S(2)}) %collective-permute-start.1) | collective-permute-done | bytes 131104 | tf_op jit(solution)/shard_map/ppermute | solution.py:213
  38.9 13.2 %collective-permute-start.4 = (f32[2,128,128]{2,1,0:T(8,128)S(1)}, f32[2,128,128]{2,1,0:T(8,128)S(1)}, u32[]{:S(2)}, u32[]{:S(2)}) collective-permute-start(f32[2,128,128]{2,1,0:T(8,128)S(1)} %pad_maximum_fusion.2), channel_id=1, source_target_pairs={{0,768},{128,384},{256,512},{384,128},{512,256},{640,896},{768,0},... | collective-permute-start | bytes 393224 | tf_op jit(solution)/shard_map/ppermute | solution.py:214
  52.2 8.4 %collective-permute-done.5 = f32[2,128,128]{2,1,0:T(8,128)S(1)} collective-permute-done((f32[2,128,128]{2,1,0:T(8,128)S(1)}, f32[2,128,128]{2,1,0:T(8,128)S(1)}, u32[]{:S(2)}, u32[]{:S(2)}) %collective-permute-start.5) | collective-permute-done | bytes 131104 | tf_op jit(solution)/shard_map/ppermute | solution.py:213
  60.6 0.6 fusion.13
  61.2 18.9 %collective-permute-start.6 = (f32[2,128,128]{2,1,0:T(8,128)S(1)}, f32[2,128,128]{2,1,0:T(8,128)S(1)}, u32[]{:S(2)}, u32[]{:S(2)}) collective-permute-start(f32[2,128,128]{2,1,0:T(8,128)S(1)} %pad_maximum_fusion.4), channel_id=1, source_target_pairs={{0,768},{128,384},{256,512},{384,128},{512,256},{640,896},{768,0},... | collective-permute-start | bytes 393224 | tf_op jit(solution)/shard_map/ppermute | solution.py:214
  80.1 0.2 fusion
  80.3 0.1 select_reduce_fusion.coef_ref
  80.4 0.5 copy-done.7
  80.9 0.0 collective-permute-done.2.got_ref
  80.9 0.8 copy-done.10
  81.7 2.3 %shard_map.64 = (f32[2,4,128,256]{3,2,1,0:T(8,128)}, f32[2,4,128,128]{3,2,1,0:T(8,128)}) custom-call(f32[2,4,64,256]{3,2,1,0:T(8,128)} %get-tuple-element.32.mine_ref, f32[2,4,64,256]{3,2,1,0:T(8,128)} %copy-done.10), custom_call_target="tpu_custom_call" | custom-call | flops 49999998976 | bytes 200000000 | tf_op jit(solution)/shard_map/pallas_call | solution.py:170
  84.0 0.0 collective-permute-done.4
  84.0 0.0 copy-start.5
  84.0 2.1 %collective-permute-start.7 = (f32[520,128]{1,0:T(8,128)S(1)}, f32[520,128]{1,0:T(8,128)S(1)}, u32[]{:S(2)}, u32[]{:S(2)}) collective-permute-start(f32[520,128]{1,0:T(8,128)S(1)} %pad_maximum_fusion.message_ref), channel_id=1, source_target_pairs={{1,0},{2,1},{3,2},{4,3},{5,4},{6,5},{7,6},{8,7},{9,8},{10,9},{11,1... | collective-permute-start | bytes 798728 | tf_op jit(solution)/shard_map/ppermute | solution.py:233
  86.1 2.0 shard_map.65
  88.1 0.0 copy-done.11
  88.1 1.9 collective-permute-start.3
  90.0 0.0 collective-permute-done.6
  90.0 0.0 copy-start.6
  90.0 2.4 %collective-permute-done.7.message_ref = f32[520,128]{1,0:T(8,128)S(1)} collective-permute-done((f32[520,128]{1,0:T(8,128)S(1)}, f32[520,128]{1,0:T(8,128)S(1)}, u32[]{:S(2)}, u32[]{:S(2)}) %collective-permute-start.7) | collective-permute-done | bytes 266272 | tf_op jit(solution)/shard_map/ppermute | solution.py:233
  92.4 0.7 copy-done.2
  93.1 2.5 %shard_map.66 = f32[392,128]{1,0:T(8,128)} custom-call(bf16[512,128]{1,0:T(8,128)(2,1)} %get-tuple-element.26.high_ref, bf16[512,128]{1,0:T(8,128)(2,1)} %get-tuple-element.27.low_ref, f32[128,128]{1,0:T(8,128)} %get-tuple-element.28.square_ref, f32[128,128]{1,0:T(8,128)} %get-tuple-element.34.kept_ref, f32[128,128]{1,0:T(8,128)} %get-tuple-element.46.got_ref, ...), custom_call_target="tpu_custom_call" | custom-call | flops 1000 | bytes 1000 | tf_op jit(solution)/shard_map/pallas_call | solution.py:82
  95.5 57.3 %all-gather = f32[1568,128]{1,0:T(8,128)} all-gather(f32[392,128]{1,0:T(8,128)} %shard_map.66), channel_id=2, replica_groups={{0,256,512,768},{128,384,640,896},{1,257,513,769},{129,385,641,897},{2,..., dimensions={0}, use_global_device_ids=true | all-gather | bytes 1003520 | tf_op jit(solution)/shard_map/all_gather | solution.py:238
  152.8 2.2 %shard_map.68 = f32[4,128,128]{2,1,0:T(8,128)} custom-call(f32[520,128]{1,0:T(8,128)} %copy-done.2, f32[2,4,128,256]{3,2,1,0:T(8,128)} %get-tuple-element.21.w_ref, f32[4,392,128]{2,1,0:T(8,128)} %bitcast.33), custom_call_target="tpu_custom_call" | custom-call | flops 1000 | bytes 1000 | tf_op jit(solution)/shard_map/pallas_call | solution.py:97
  155.0 4.8 %collective-permute-start.8 = (f32[4,128,128]{2,1,0:T(8,128)}, f32[4,128,128]{2,1,0:T(8,128)S(1)}, u32[]{:S(2)}, u32[]{:S(2)}) collective-permute-start(f32[4,128,128]{2,1,0:T(8,128)} %shard_map.68), channel_id=1, source_target_pairs={{0,1},{1,2},{2,3},{3,4},{4,5},{5,6},{6,7},{7,8},{8,9},{9,10},{10,1... | collective-permute-start | bytes 786440 | tf_op jit(solution)/shard_map/ppermute | solution.py:239
  159.8 0.0 collective-permute-done.3.wr_ref
  159.8 0.0 copy-start.4
  159.8 0.8 copy-done.4
  160.6 3.5 %shard_map.67 = (f32[4,64,256]{2,1,0:T(8,128)}, f32[4,64,256]{2,1,0:T(8,128)}) custom-call(f32[12]{0:T(128)} %copy-done.7, f32[2,4,128,256]{3,2,1,0:T(8,128)} %get-tuple-element.21.w_ref, f32[2,4,128,128]{3,2,1,0:T(8,128)} %copy-done.4, f32[4,392,128]{2,1,0:T(8,128)} %bitcast.34), custom_call_target="tpu_custom_call" | custom-call | flops 1000 | bytes 1000 | tf_op jit(solution)/shard_map/pallas_call | solution.py:150
  164.1 15.3 %collective-permute-done.8 = f32[4,128,128]{2,1,0:T(8,128)S(1)} collective-permute-done((f32[4,128,128]{2,1,0:T(8,128)}, f32[4,128,128]{2,1,0:T(8,128)S(1)}, u32[]{:S(2)}, u32[]{:S(2)}) %collective-permute-start.8) | collective-permute-done | bytes 262176 | tf_op jit(solution)/shard_map/ppermute | solution.py:239
  179.4 1.1 fusion.4
  180.5 16.3 %collective-permute-start.9 = (f32[4,64,256]{2,1,0:T(8,128)S(1)}, f32[4,64,256]{2,1,0:T(8,128)S(1)}, u32[]{:S(2)}, u32[]{:S(2)}) collective-permute-start(f32[4,64,256]{2,1,0:T(8,128)S(1)} %get-tuple-element.40), channel_id=1, source_target_pairs={{0,128},{128,0},{256,384},{384,256},{512,640},{640,512},{768,896},... | collective-permute-start | bytes 786440 | tf_op jit(solution)/shard_map/ppermute | solution.py:243
  196.8 1.1 collective-permute-done.9
  198.0 0.2 fusion.2
  198.2 1.1 copy.18
  (25 shorter events, 0.2 us)
Async XLA Ops:
  0.0 80.1 %copy-start = (f32[8]{0:T(128)S(1)}, f32[8]{0:T(128)}, u32[]{:S(2)}) copy-start(f32[8]{0:T(128)} %param.8) | copy-start | bytes 100
  0.0 17.4 %copy-start.3 = (f32[2,64,8,256]{3,2,1,0:T(8,128)S(1)}, f32[2,64,8,256]{3,2,1,0:T(8,128)}, u32[]{:S(2)}) copy-start(f32[2,64,8,256]{3,2,1,0:T(8,128)} %param.7) | copy-start | bytes 3145732
  1.4 20.0 %collective-permute-start = (f32[4,64,256]{2,1,0:T(8,128)S(1)}, f32[4,64,256]{2,1,0:T(8,128)S(1)}, u32[]{:S(2)}, u32[]{:S(2)}) collective-permute-start(f32[4,64,256]{2,1,0:T(8,128)S(1)} %get-tuple-element.18), channel_id=1, source_target_pairs={{0,128},{128,0},{256,384},{384,256},{512,640},{640,512},{768,896},... | collective-permute-start | bytes 786440 | tf_op jit(solution)/shard_map/ppermute | solution.py:202
  18.7 62.2 %collective-permute-start.2 = (f32[2,4,64,256]{3,2,1,0:T(8,128)S(1)}, f32[2,4,64,256]{3,2,1,0:T(8,128)S(1)}, u32[]{:S(2)}, u32[]{:S(2)}) collective-permute-start(f32[2,4,64,256]{3,2,1,0:T(8,128)S(1)} %get-tuple-element.31), channel_id=1, source_target_pairs={{0,128},{128,0},{256,384},{384,256},{512,640},{640,512},{768,896},... | collective-permute-start | bytes 1572872 | tf_op jit(solution)/shard_map/ppermute | solution.py:230
  20.6 0.7 copy-start.8
  20.6 0.7 copy-start.9
  21.4 17.5 %collective-permute-start.1 = (f32[2,128,128]{2,1,0:T(8,128)S(1)}, f32[2,128,128]{2,1,0:T(8,128)S(1)}, u32[]{:S(2)}, u32[]{:S(2)}) collective-permute-start(f32[2,128,128]{2,1,0:T(8,128)S(1)} %pad_maximum_fusion.1), channel_id=1, source_target_pairs={{0,256},{128,896},{256,0},{384,640},{512,768},{640,384},{768,512},... | collective-permute-start | bytes 393224 | tf_op jit(solution)/shard_map/ppermute | solution.py:213
  32.2 28.4 %collective-permute-start.5 = (f32[2,128,128]{2,1,0:T(8,128)S(1)}, f32[2,128,128]{2,1,0:T(8,128)S(1)}, u32[]{:S(2)}, u32[]{:S(2)}) collective-permute-start(f32[2,128,128]{2,1,0:T(8,128)S(1)} %pad_maximum_fusion.3), channel_id=1, source_target_pairs={{0,256},{128,896},{256,0},{384,640},{512,768},{640,384},{768,512},... | collective-permute-start | bytes 393224 | tf_op jit(solution)/shard_map/ppermute | solution.py:213
  38.9 45.1 %collective-permute-start.4 = (f32[2,128,128]{2,1,0:T(8,128)S(1)}, f32[2,128,128]{2,1,0:T(8,128)S(1)}, u32[]{:S(2)}, u32[]{:S(2)}) collective-permute-start(f32[2,128,128]{2,1,0:T(8,128)S(1)} %pad_maximum_fusion.2), channel_id=1, source_target_pairs={{0,768},{128,384},{256,512},{384,128},{512,256},{640,896},{768,0},... | collective-permute-start | bytes 393224 | tf_op jit(solution)/shard_map/ppermute | solution.py:214
  61.2 18.9 %copy-start.12 = (s32[8]{0:T(128)S(1)}, s32[8]{0:T(128)}, u32[]{:S(2)}) copy-start(s32[8]{0:T(128)} %param.10) | copy-start | bytes 100
  61.2 28.7 %collective-permute-start.6 = (f32[2,128,128]{2,1,0:T(8,128)S(1)}, f32[2,128,128]{2,1,0:T(8,128)S(1)}, u32[]{:S(2)}, u32[]{:S(2)}) collective-permute-start(f32[2,128,128]{2,1,0:T(8,128)S(1)} %pad_maximum_fusion.4), channel_id=1, source_target_pairs={{0,768},{128,384},{256,512},{384,128},{512,256},{640,896},{768,0},... | collective-permute-start | bytes 393224 | tf_op jit(solution)/shard_map/ppermute | solution.py:214
  80.4 0.5 copy-start.7
  80.9 0.8 copy-start.10
  84.0 2.1 %copy-start.5 = (f32[520,128]{1,0:T(8,128)}, f32[520,128]{1,0:T(8,128)S(1)}, u32[]{:S(2)}) copy-start(f32[520,128]{1,0:T(8,128)S(1)} %pad_maximum_fusion.message_ref) | copy-start | bytes 798724
  84.0 4.0 %copy-start.11 = (f32[2,4,128,128]{3,2,1,0:T(8,128)S(1)}, f32[2,4,128,128]{3,2,1,0:T(8,128)}, u32[]{:S(2)}) copy-start(f32[2,4,128,128]{3,2,1,0:T(8,128)} %get-tuple-element.23) | copy-start | bytes 1572868
  84.0 8.3 %collective-permute-start.7 = (f32[520,128]{1,0:T(8,128)S(1)}, f32[520,128]{1,0:T(8,128)S(1)}, u32[]{:S(2)}, u32[]{:S(2)}) collective-permute-start(f32[520,128]{1,0:T(8,128)S(1)} %pad_maximum_fusion.message_ref), channel_id=1, source_target_pairs={{1,0},{2,1},{3,2},{4,3},{5,4},{6,5},{7,6},{8,7},{9,8},{10,9},{11,1... | collective-permute-start | bytes 798728 | tf_op jit(solution)/shard_map/ppermute | solution.py:233
  88.1 71.7 %collective-permute-start.3 = (f32[2,4,128,128]{3,2,1,0:T(8,128)S(1)}, f32[2,4,128,128]{3,2,1,0:T(8,128)S(1)}, u32[]{:S(2)}, u32[]{:S(2)}) collective-permute-start(f32[2,4,128,128]{3,2,1,0:T(8,128)S(1)} %copy-done.11), channel_id=1, source_target_pairs={{1,0},{2,1},{3,2},{4,3},{5,4},{6,5},{7,6},{8,7},{9,8},{10,9},{11,1... | collective-permute-start | bytes 1572872 | tf_op jit(solution)/shard_map/ppermute | solution.py:235
  90.0 2.4 %copy-start.6 = (f32[2,128,128]{2,1,0:T(8,128)}, f32[2,128,128]{2,1,0:T(8,128)S(1)}, u32[]{:S(2)}) copy-start(f32[2,128,128]{2,1,0:T(8,128)S(1)} %collective-permute-done.6) | copy-start | bytes 393220
  92.4 0.7 copy-start.2
  155.0 24.4 %collective-permute-start.8 = (f32[4,128,128]{2,1,0:T(8,128)}, f32[4,128,128]{2,1,0:T(8,128)S(1)}, u32[]{:S(2)}, u32[]{:S(2)}) collective-permute-start(f32[4,128,128]{2,1,0:T(8,128)} %shard_map.68), channel_id=1, source_target_pairs={{0,1},{1,2},{2,3},{3,4},{4,5},{5,6},{6,7},{7,8},{8,9},{9,10},{10,1... | collective-permute-start | bytes 786440 | tf_op jit(solution)/shard_map/ppermute | solution.py:239
  159.8 0.8 copy-start.4
  179.4 18.6 %copy-start.1 = (f32[64,8,256]{2,1,0:T(8,128)S(1)}, f32[64,8,256]{2,1,0:T(8,128)}, u32[]{:S(2)}) copy-start(f32[64,8,256]{2,1,0:T(8,128)} %param.6) | copy-start | bytes 1572868
  180.5 17.4 %collective-permute-start.9 = (f32[4,64,256]{2,1,0:T(8,128)S(1)}, f32[4,64,256]{2,1,0:T(8,128)S(1)}, u32[]{:S(2)}, u32[]{:S(2)}) collective-permute-start(f32[4,64,256]{2,1,0:T(8,128)S(1)} %get-tuple-element.40), channel_id=1, source_target_pairs={{0,128},{128,0},{256,384},{384,256},{512,640},{640,512},{768,896},... | collective-permute-start | bytes 786440 | tf_op jit(solution)/shard_map/ppermute | solution.py:243

commit v7 on v4

--- a/solution.py
+++ b/solution.py
@@ -9,7 +9,6 @@
 
 BLK = 128
 CHIPS = 4
-GROUPS = [[2 * z + c for z in range(CHIPS)] for c in range(2)]
 SWAP = [(i, i ^ 1) for i in range(2 * CHIPS)]
 NEAR = [z ^ 1 for z in range(CHIPS)]
 CROSS = [CHIPS - 1 - z for z in range(CHIPS)]
@@ -55,19 +54,19 @@
 
 
 def covariance_kernel(
-    high_ref, low_ref, square_ref, kept_ref, got_ref, last_ref, message_ref, out_ref
+    high_ref, low_ref, square_ref, kept_ref, got_ref, last_ref, message_ref, edge_ref, own_ref
 ):
     second = centred(kept_ref[...], got_ref[...], last_ref[...])
     first = high_ref[...], low_ref[...]
     d1 = product(second, second, ROWS)
     row = lax.broadcasted_iota(jnp.int32, (BLK, BLK), 0)
     col = lax.broadcasted_iota(jnp.int32, (BLK, BLK), 1)
-    out_ref[:BLK] = jnp.where(row <= col, square_ref[...], d1)
-    out_ref[BLK : 2 * BLK] = product(first, second, ROWS)
+    own_ref[:BLK] = jnp.where(row <= col, square_ref[...], d1)
+    own_ref[BLK : 2 * BLK] = product(first, second, ROWS)
     diagonal = jnp.sum(jnp.where(row == col, d1, 0.0), axis=0, keepdims=True)
-    out_ref[3 * BLK :] = jnp.broadcast_to(diagonal, (8, BLK))
+    own_ref[2 * BLK :] = jnp.broadcast_to(diagonal, (8, BLK))
     after = centred(message_ref[: high_ref.shape[0]])
-    out_ref[2 * BLK : 3 * BLK] = product(second, after, ROWS)
+    edge_ref[...] = product(second, after, ROWS)
 
 
 LONG = pl.CostEstimate(flops=50_000_000_000, bytes_accessed=200_000_000, transcendentals=0)
@@ -78,51 +77,61 @@
     ensemble = message.shape[0] - 8
     square = jax.ShapeDtypeStruct((BLK, BLK), jnp.float32)
     half = jax.ShapeDtypeStruct((ensemble, BLK), jnp.bfloat16)
-    first = pl.pallas_call(first_kernel, out_shape=(half, half, square), cost_estimate=TINY)(message)
+    first = pl.pallas_call(first_kernel, out_shape=(half, half, square), cost_estimate=LONG)(message)
     return pl.pallas_call(
         covariance_kernel,
-        out_shape=jax.ShapeDtypeStruct((3 * BLK + 8, BLK), jnp.float32),
+        out_shape=(square, jax.ShapeDtypeStruct((2 * BLK + 8, BLK), jnp.float32)),
         cost_estimate=TINY,
     )(*first, kept, got, last, after)
 
 
-def outward_kernel(message_ref, w_ref, cov_ref, out_ref):
-    for level in range(out_ref.shape[0]):
+def pieces(own_ref, near_ref, far_ref):
+    return own_ref[...], near_ref[...], far_ref[0], far_ref[1]
+
+
+def outward_kernel(order_ref, message_ref, w_ref, own_ref, near_ref, far_ref, out_ref):
+    for step, edge in enumerate(pieces(own_ref, near_ref, far_ref)):
+        level = order_ref[step]
         mixed = message_ref[:1, :1] * w_ref[0, level] + message_ref[:1, 1:2] * w_ref[1, level]
-        out_ref[level] = product(split(mixed), split(cov_ref[level]), PLAIN)
-
-
-def outward(message, w, cov):
+        out_ref[level] = product(split(mixed), split(edge), PLAIN)
+
+
+def outward(order, message, w, edges):
     levels, members = w.shape[1:3]
+    whole = lambda x: pl.BlockSpec(x.shape, lambda i: (0,) * x.ndim)
     return pl.pallas_call(
         outward_kernel,
         grid=(1,),
         in_specs=[
+            pl.BlockSpec(memory_space=pltpu.SMEM),
             pl.BlockSpec((8, BLK), lambda i: (message.shape[0] // 8 - 1, 0)),
             pl.BlockSpec((2, levels, members, BLK), lambda i: (0, 0, 0, 1)),
-            pl.BlockSpec((levels, BLK, BLK), lambda i: (0, 2, 0)),
+            *(whole(x) for x in edges),
         ],
         out_specs=pl.BlockSpec((levels, members, BLK), lambda i: (0, 0, 0)),
         out_shape=jax.ShapeDtypeStruct((levels, members, BLK), jnp.float32),
-        cost_estimate=TINY,
-    )(message, w, cov)
-
-
-def increment_kernel(coef_ref, w_ref, wr_ref, cov_ref, kept_ref, sent_ref):
+        cost_estimate=LONG,
+    )(order, message, w, *edges)
+
+
+def increment_kernel(
+    coef_ref, order_ref, w_ref, wr_ref, e0_ref, e1_ref, e2_ref, c0_ref, c1_ref, c2_ref, kept_ref, sent_ref
+):
     row = lax.broadcasted_iota(jnp.int32, (BLK, BLK), 0)
     col = lax.broadcasted_iota(jnp.int32, (BLK, BLK), 1)
     here, there = slice(0, BLK), slice(BLK, 2 * BLK)
     keep = kept_ref.shape[1]
-    for level in range(kept_ref.shape[0]):
-        packed = cov_ref[level, :BLK]
+    found = zip(pieces(e0_ref, e1_ref, e2_ref), pieces(c0_ref, c1_ref, c2_ref))
+    for step, (edge, cov) in enumerate(found):
+        level = order_ref[step]
+        packed = cov[:BLK]
         upper = jnp.where(row <= col, packed, 0.0)
         strict = jnp.where(row < col, packed, 0.0)
         lower = jnp.where(row > col, packed, 0.0)
-        diagonal = jnp.where(row == col, cov_ref[level, 3 * BLK : 3 * BLK + 1], 0.0)
+        diagonal = jnp.where(row == col, cov[2 * BLK : 2 * BLK + 1], 0.0)
         d0 = split(upper + strict.T)
         d1 = split(lower + lower.T + diagonal)
-        c01 = split(cov_ref[level, BLK : 2 * BLK])
-        edge = split(cov_ref[level, 2 * BLK : 3 * BLK])
+        c01 = split(cov[BLK : 2 * BLK])
 
         def mixed(ref, t, j, part=slice(None)):
             at = t * 6 + j * 2
@@ -136,24 +145,24 @@
         one = (
             product(mixed(w_ref, 1, 0, here), c01, PLAIN)
             + product(mixed(w_ref, 1, 1, there), d1, PLAIN)
-            + product(mixed(wr_ref, 1, 2), edge, LANES)
+            + product(mixed(wr_ref, 1, 2), split(edge), LANES)
         )
         for ref, rows in ((kept_ref, slice(0, keep)), (sent_ref, slice(keep, 2 * keep))):
             ref[level, :, here] = zero[rows]
             ref[level, :, there] = one[rows]
 
 
-def increments(coefs, w, w_right, cov):
+def increments(coefs, order, w, w_right, edges, covs):
     levels, members = w.shape[1:3]
     half = jax.ShapeDtypeStruct((levels, members // 2, 2 * BLK), jnp.float32)
-    vmem = pl.BlockSpec(memory_space=pltpu.VMEM)
+    vmem, smem = (pl.BlockSpec(memory_space=m) for m in (pltpu.VMEM, pltpu.SMEM))
     return pl.pallas_call(
         increment_kernel,
-        in_specs=[pl.BlockSpec(memory_space=pltpu.SMEM), vmem, vmem, vmem],
+        in_specs=[smem, smem] + [vmem] * 8,
         out_specs=(vmem, vmem),
         out_shape=(half, half),
         cost_estimate=TINY,
-    )(coefs, w, w_right, cov)
+    )(coefs, order, w, w_right, *edges, *covs)
 
 
 def gather_kernel(mine_ref, got_ref, w_ref, low_ref):
@@ -215,8 +224,8 @@
         return pick(x, chip), got[0], last.reshape(-1, BLK)
 
     first, second = to_owner(0), to_owner(1)
-    taken, pair_taper = lax.optimization_barrier((first[1], pair_taper))
-    first = first[0], taken, first[2]
+    taken, pair_taper = lax.optimization_barrier((second[1], pair_taper))
+    second = second[0], taken, second[2]
     tapers = jnp.dot(
         one_hot(pair_taper, taper_table.shape[0]), taper_table, precision=lax.Precision.HIGHEST
     ) / (ensemble - 1)
@@ -233,10 +242,15 @@
     w, low = gathered(mine, lax.ppermute(theirs, "member", SWAP))
     w_right = lax.ppermute(low, "region", left)
 
-    own = covariances(message, *second, after)
-    cov = lax.all_gather(own, "member", axis_index_groups=GROUPS)
-    from_left = lax.ppermute(outward(after, w, cov), "region", right)
-    kept, sent = increments(coefs, w, w_right, cov)
+    edge, own = covariances(message, *second, after)
+    order = jnp.stack([chip, one, two, both])
+    edge_near = lax.ppermute(edge, "member", step_one)
+    own_near = lax.ppermute(own, "member", step_one)
+    edge_far = lax.ppermute(jnp.stack([edge, edge_near]), "member", step_two)
+    own_far = lax.ppermute(jnp.stack([own, own_near]), "member", step_two)
+    edges = edge, edge_near, edge_far
+    from_left = lax.ppermute(outward(order, after, w, edges), "region", right)
+    kept, sent = increments(coefs, order, w, w_right, edges, (own, own_near, own_far))
     from_left = jnp.pad(from_left, ((0, 0), (0, 0), (0, column_count - BLK)))
     kept, sent = kept + from_left[:, :member_loc], sent + from_left[:, member_loc:]
     came = lax.ppermute(sent, "member", SWAP)

time: 194 us -> 194 us (level)
  the two profiles are of different devices: /device:TPU:1 before, /device:TPU:193 now
where the time goes in v7:
time: 194 us
  starting transfers between devices  114 us (59%)
  waiting for transfers between devices  54.4 us (28%)
  Pallas kernels  12.3 us (6%)
  local copies, waits for them, and re-layouts  9.12 us (5%)
  other arithmetic  3.07 us (2%)
    ppermute x1, starting transfers between devices, local(): came = lax.ppermute(sent, 'member', SWAP)  38.9 us
    ppermute x2, starting transfers between devices, to_owner(): lax.ppermute(jnp.stack([pick(x, one), pick(x, both)]), 'member', step_one)  18 us
    ppermute x2, starting transfers between devices, to_owner(): last = lax.ppermute(jnp.stack([pick(x, two), got[1]]), 'member', step_two)  14.5 us
    ppermute x2, waiting for transfers between devices, to_owner(): last = lax.ppermute(jnp.stack([pick(x, two), got[1]]), 'member', step_two)  11.8 us
    ppermute x2, waiting for transfers between devices, to_owner(): lax.ppermute(jnp.stack([pick(x, one), pick(x, both)]), 'member', step_one)  11.3 us
    ppermute x1, starting transfers between devices, local(): edge_near = lax.ppermute(edge, 'member', step_one)  10.3 us
    ppermute x1, starting transfers between devices, local(): edge_far = lax.ppermute(jnp.stack([edge, edge_near]), 'member', step_two)  9.63 us
    ppermute x1, waiting for transfers between devices, local(): after = lax.ppermute(message, 'region', left)  8.24 us
  transfers between devices with their start and end apart: 14, of which 10 were waited for; matrix products, arithmetic and copies ran while one was open for 2% of the time, Pallas kernels for 6%

profile of v7, /device:TPU:193, one launch (start us, length us, event | category | flops | bytes accessed | tf_op | source)
XLA Modules:
  0.0 193.7 jit_solution(6475663076365694406)
XLA Ops:
  0.0 1.3 copy.17
  1.4 2.6 %collective-permute-start = (f32[4,64,256]{2,1,0:T(8,128)S(1)}, f32[4,64,256]{2,1,0:T(8,128)S(1)}, u32[]{:S(2)}, u32[]{:S(2)}) collective-permute-start(f32[4,64,256]{2,1,0:T(8,128)S(1)} %get-tuple-element.18), channel_id=1, source_target_pairs={{0,128},{128,0},{256,384},{384,256},{512,640},{640,512},{768,896},... | collective-permute-start | bytes 786440 | tf_op jit(solution)/shard_map/ppermute | solution.py:211
  4.0 0.3 copy.15
  4.3 0.9 dynamic-slice_bitcast_fusion
  5.2 1.9 collective-permute-start.2
  7.2 0.0 copy-start.13
  7.2 0.7 copy-done.13
  7.9 16.1 %collective-permute-start.4 = (f32[2,128,128]{2,1,0:T(8,128)S(1)}, f32[2,128,128]{2,1,0:T(8,128)S(1)}, u32[]{:S(2)}, u32[]{:S(2)}) collective-permute-start(f32[2,128,128]{2,1,0:T(8,128)S(1)} %pad_maximum_fusion.2), channel_id=1, source_target_pairs={{0,256},{128,896},{256,0},{384,640},{512,768},{640,384},{768,512},... | collective-permute-start | bytes 393224 | tf_op jit(solution)/shard_map/ppermute | solution.py:222
  24.1 0.7 constant_dynamic-slice_fusion
  24.7 1.9 collective-permute-start.1
  26.7 11.3 %collective-permute-done.4 = f32[2,128,128]{2,1,0:T(8,128)S(1)} collective-permute-done((f32[2,128,128]{2,1,0:T(8,128)S(1)}, f32[2,128,128]{2,1,0:T(8,128)S(1)}, u32[]{:S(2)}, u32[]{:S(2)}) %collective-permute-start.4) | collective-permute-done | bytes 131104 | tf_op jit(solution)/shard_map/ppermute | solution.py:222
  38.0 8.6 %collective-permute-start.5 = (f32[2,128,128]{2,1,0:T(8,128)S(1)}, f32[2,128,128]{2,1,0:T(8,128)S(1)}, u32[]{:S(2)}, u32[]{:S(2)}) collective-permute-start(f32[2,128,128]{2,1,0:T(8,128)S(1)} %pad_maximum_fusion.3), channel_id=1, source_target_pairs={{0,768},{128,384},{256,512},{384,128},{512,256},{640,896},{768,0},... | collective-permute-start | bytes 393224 | tf_op jit(solution)/shard_map/ppermute | solution.py:223
  46.6 0.6 fusion.13
  47.2 5.9 %collective-permute-start.6 = (f32[2,128,128]{2,1,0:T(8,128)S(1)}, f32[2,128,128]{2,1,0:T(8,128)S(1)}, u32[]{:S(2)}, u32[]{:S(2)}) collective-permute-start(f32[2,128,128]{2,1,0:T(8,128)S(1)} %pad_maximum_fusion.4), channel_id=1, source_target_pairs={{0,768},{128,384},{256,512},{384,128},{512,256},{640,896},{768,0},... | collective-permute-start | bytes 393224 | tf_op jit(solution)/shard_map/ppermute | solution.py:223
  53.2 0.2 fusion
  53.4 0.1 select_reduce_fusion.coef_ref
  53.5 11.7 %collective-permute-done.5 = f32[2,128,128]{2,1,0:T(8,128)S(1)} collective-permute-done((f32[2,128,128]{2,1,0:T(8,128)S(1)}, f32[2,128,128]{2,1,0:T(8,128)S(1)}, u32[]{:S(2)}, u32[]{:S(2)}) %collective-permute-start.5) | collective-permute-done | bytes 131104 | tf_op jit(solution)/shard_map/ppermute | solution.py:223
  65.2 2.1 %collective-permute-start.7 = (f32[520,128]{1,0:T(8,128)S(1)}, f32[520,128]{1,0:T(8,128)S(1)}, u32[]{:S(2)}, u32[]{:S(2)}) collective-permute-start(f32[520,128]{1,0:T(8,128)S(1)} %select_maximum_fusion.message_ref), channel_id=1, source_target_pairs={{1,0},{2,1},{3,2},{4,3},{5,4},{6,5},{7,6},{8,7},{9,8},{10,9},{11,1... | collective-permute-start | bytes 798728 | tf_op jit(solution)/shard_map/ppermute | solution.py:237
  67.4 2.0 %shard_map.65 = (bf16[512,128]{1,0:T(8,128)(2,1)}, bf16[512,128]{1,0:T(8,128)(2,1)}, f32[128,128]{1,0:T(8,128)}) custom-call(f32[520,128]{1,0:T(8,128)} %copy-done.7), custom_call_target="tpu_custom_call" | custom-call | flops 49999998976 | bytes 200000000 | tf_op jit(solution)/shard_map/pallas_call | solution.py:80
  69.3 0.1 collective-permute-done.6
  69.4 8.2 %collective-permute-done.7.message_ref = f32[520,128]{1,0:T(8,128)S(1)} collective-permute-done((f32[520,128]{1,0:T(8,128)S(1)}, f32[520,128]{1,0:T(8,128)S(1)}, u32[]{:S(2)}, u32[]{:S(2)}) %collective-permute-start.7) | collective-permute-done | bytes 266272 | tf_op jit(solution)/shard_map/ppermute | solution.py:237
  77.7 0.7 copy-done.8
  78.4 2.4 %shard_map.66 = (f32[128,128]{1,0:T(8,128)}, f32[264,128]{1,0:T(8,128)}) custom-call(bf16[512,128]{1,0:T(8,128)(2,1)} %get-tuple-element.23.high_ref, bf16[512,128]{1,0:T(8,128)(2,1)} %get-tuple-element.24.low_ref, f32[128,128]{1,0:T(8,128)} %get-tuple-element.25.square_ref, f32[128,128]{1,0:T(8,128)} %get-tuple-element.42.kept_ref, ...), custom_call_target="tpu_custom_call" | custom-call | flops 1000 | bytes 1000 | tf_op jit(solution)/shard_map/pallas_call | solution.py:81
  80.8 10.3 %collective-permute-start.8 = (f32[128,128]{1,0:T(8,128)}, f32[128,128]{1,0:T(8,128)S(1)}, u32[]{:S(2)}, u32[]{:S(2)}) collective-permute-start(f32[128,128]{1,0:T(8,128)} %get-tuple-element.27.e0_ref.own_ref), channel_id=1, source_target_pairs={{0,256},{128,896},{256,0},{384,640},{512,768},{640,384},{768,512},... | collective-permute-start | bytes 196616 | tf_op jit(solution)/shard_map/ppermute | solution.py:247
  91.1 0.6 pad_add_fusion.order_ref
  91.7 3.7 %collective-permute-start.10 = (f32[264,128]{1,0:T(8,128)}, f32[264,128]{1,0:T(8,128)S(1)}, u32[]{:S(2)}, u32[]{:S(2)}) collective-permute-start(f32[264,128]{1,0:T(8,128)} %get-tuple-element.28.c0_ref), channel_id=1, source_target_pairs={{0,256},{128,896},{256,0},{384,640},{512,768},{640,384},{768,512},... | collective-permute-start | bytes 405512 | tf_op jit(solution)/shard_map/ppermute | solution.py:248
  95.4 3.6 %collective-permute-done.8.e1_ref.near_ref = f32[128,128]{1,0:T(8,128)S(1)} collective-permute-done((f32[128,128]{1,0:T(8,128)}, f32[128,128]{1,0:T(8,128)S(1)}, u32[]{:S(2)}, u32[]{:S(2)}) %collective-permute-start.8) | collective-permute-done | bytes 65568 | tf_op jit(solution)/shard_map/ppermute | solution.py:247
  99.0 0.9 pad_maximum_fusion.5
  99.9 9.6 %collective-permute-start.9 = (f32[2,128,128]{2,1,0:T(8,128)S(1)}, f32[2,128,128]{2,1,0:T(8,128)S(1)}, u32[]{:S(2)}, u32[]{:S(2)}) collective-permute-start(f32[2,128,128]{2,1,0:T(8,128)S(1)} %pad_maximum_fusion.5), channel_id=1, source_target_pairs={{0,768},{128,384},{256,512},{384,128},{512,256},{640,896},{768,0},... | collective-permute-start | bytes 393224 | tf_op jit(solution)/shard_map/ppermute | solution.py:249
  109.5 0.8 copy-done.15
  110.3 2.3 %shard_map.64 = (f32[2,4,128,256]{3,2,1,0:T(8,128)}, f32[2,4,128,128]{3,2,1,0:T(8,128)}) custom-call(f32[2,4,64,256]{3,2,1,0:T(8,128)} %get-tuple-element.32.mine_ref, f32[2,4,64,256]{3,2,1,0:T(8,128)} %copy-done.15), custom_call_target="tpu_custom_call" | custom-call | flops 49999998976 | bytes 200000000 | tf_op jit(solution)/shard_map/pallas_call | solution.py:179
  112.6 5.7 %collective-permute-start.3 = (f32[2,4,128,128]{3,2,1,0:T(8,128)}, f32[2,4,128,128]{3,2,1,0:T(8,128)S(1)}, u32[]{:S(2)}, u32[]{:S(2)}) collective-permute-start(f32[2,4,128,128]{3,2,1,0:T(8,128)} %get-tuple-element.22), channel_id=1, source_target_pairs={{1,0},{2,1},{3,2},{4,3},{5,4},{6,5},{7,6},{8,7},{9,8},{10,9},{11,1... | collective-permute-start | bytes 1572872 | tf_op jit(solution)/shard_map/ppermute | solution.py:243
  118.3 3.5 %collective-permute-done.10.c1_ref = f32[264,128]{1,0:T(8,128)S(1)} collective-permute-done((f32[264,128]{1,0:T(8,128)}, f32[264,128]{1,0:T(8,128)S(1)}, u32[]{:S(2)}, u32[]{:S(2)}) %collective-permute-start.10) | collective-permute-done | bytes 135200 | tf_op jit(solution)/shard_map/ppermute | solution.py:248
  121.9 0.6 copy-done.4
  122.5 1.9 collective-permute-start.11
  124.4 0.6 copy-done.10
  125.1 2.2 %shard_map.68 = f32[4,128,128]{2,1,0:T(8,128)} custom-call(s32[4]{0:T(128)} %pad_add_fusion.order_ref, f32[520,128]{1,0:T(8,128)} %copy-done.8, f32[2,4,128,256]{3,2,1,0:T(8,128)} %get-tuple-element.21.w_ref, f32[128,128]{1,0:T(8,128)} %get-tuple-element.27.e0_ref.own_ref, f32[128,128]{1,0:T(8,128)} %copy-done.9, f32[2,128,128]{2,1,0:T(8,128)} %copy-done.10), custom_call_target="tpu_custom_call" | custom-call | flops 49999998976 | bytes 200000000 | tf_op jit(solution)/shard_map/pallas_call | solution.py:102
  127.2 5.0 %collective-permute-start.12 = (f32[4,128,128]{2,1,0:T(8,128)}, f32[4,128,128]{2,1,0:T(8,128)S(1)}, u32[]{:S(2)}, u32[]{:S(2)}) collective-permute-start(f32[4,128,128]{2,1,0:T(8,128)} %shard_map.68), channel_id=1, source_target_pairs={{0,1},{1,2},{2,3},{3,4},{4,5},{5,6},{6,7},{7,8},{8,9},{9,10},{10,1... | collective-permute-start | bytes 786440 | tf_op jit(solution)/shard_map/ppermute | solution.py:252
  132.3 4.4 %collective-permute-done.3.wr_ref = f32[2,4,128,128]{3,2,1,0:T(8,128)S(1)} collective-permute-done((f32[2,4,128,128]{3,2,1,0:T(8,128)}, f32[2,4,128,128]{3,2,1,0:T(8,128)S(1)}, u32[]{:S(2)}, u32[]{:S(2)}) %collective-permute-start.3) | collective-permute-done | bytes 524320 | tf_op jit(solution)/shard_map/ppermute | solution.py:243
  136.7 8.2 %collective-permute-done.11.c2_ref = f32[2,264,128]{2,1,0:T(8,128)S(1)} collective-permute-done((f32[2,264,128]{2,1,0:T(8,128)S(1)}, f32[2,264,128]{2,1,0:T(8,128)S(1)}, u32[]{:S(2)}, u32[]{:S(2)}) %collective-permute-start.11) | collective-permute-done | bytes 270368 | tf_op jit(solution)/shard_map/ppermute | solution.py:250
  144.9 0.7 copy-done.6
  145.6 3.5 %shard_map.67 = (f32[4,64,256]{2,1,0:T(8,128)}, f32[4,64,256]{2,1,0:T(8,128)}) custom-call(f32[12]{0:T(128)} %copy-done.12, s32[4]{0:T(128)} %pad_add_fusion.order_ref, f32[2,4,128,256]{3,2,1,0:T(8,128)} %get-tuple-element.21.w_ref, f32[2,4,128,128]{3,2,1,0:T(8,128)} %copy-done.5, f32[128,128]{1,0:T(8,128)} %get-tuple-element.27.e0_ref.own_ref, ...), custom_call_target="tpu_custom_call" | custom-call | flops 1000 | bytes 1000 | tf_op jit(solution)/shard_map/pallas_call | solution.py:159
  149.1 2.1 %collective-permute-done.12 = f32[4,128,128]{2,1,0:T(8,128)S(1)} collective-permute-done((f32[4,128,128]{2,1,0:T(8,128)}, f32[4,128,128]{2,1,0:T(8,128)S(1)}, u32[]{:S(2)}, u32[]{:S(2)}) %collective-permute-start.12) | collective-permute-done | bytes 262176 | tf_op jit(solution)/shard_map/ppermute | solution.py:252
  151.3 1.1 fusion.4
  152.4 38.9 %collective-permute-start.13 = (f32[4,64,256]{2,1,0:T(8,128)S(1)}, f32[4,64,256]{2,1,0:T(8,128)S(1)}, u32[]{:S(2)}, u32[]{:S(2)}) collective-permute-start(f32[4,64,256]{2,1,0:T(8,128)S(1)} %get-tuple-element.40), channel_id=1, source_target_pairs={{0,128},{128,0},{256,384},{384,256},{512,640},{640,512},{768,896},... | collective-permute-start | bytes 786440 | tf_op jit(solution)/shard_map/ppermute | solution.py:256
  191.3 1.1 collective-permute-done.13
  192.4 0.2 fusion.2
  192.6 1.1 copy.18
  (42 shorter events, 0.3 us)
Async XLA Ops:
  0.0 53.2 %copy-start = (f32[8]{0:T(128)S(1)}, f32[8]{0:T(128)}, u32[]{:S(2)}) copy-start(f32[8]{0:T(128)} %param.8) | copy-start | bytes 100
  0.0 4.0 %copy-start.2 = (f32[2,64,8,256]{3,2,1,0:T(8,128)S(1)}, f32[2,64,8,256]{3,2,1,0:T(8,128)}, u32[]{:S(2)}) copy-start(f32[2,64,8,256]{3,2,1,0:T(8,128)} %param.7) | copy-start | bytes 3145732
  1.4 6.5 %collective-permute-start = (f32[4,64,256]{2,1,0:T(8,128)S(1)}, f32[4,64,256]{2,1,0:T(8,128)S(1)}, u32[]{:S(2)}, u32[]{:S(2)}) collective-permute-start(f32[4,64,256]{2,1,0:T(8,128)S(1)} %get-tuple-element.18), channel_id=1, source_target_pairs={{0,128},{128,0},{256,384},{384,256},{512,640},{640,512},{768,896},... | collective-permute-start | bytes 786440 | tf_op jit(solution)/shard_map/ppermute | solution.py:211
  5.2 104.3 %collective-permute-start.2 = (f32[2,4,64,256]{3,2,1,0:T(8,128)S(1)}, f32[2,4,64,256]{3,2,1,0:T(8,128)S(1)}, u32[]{:S(2)}, u32[]{:S(2)}) collective-permute-start(f32[2,4,64,256]{3,2,1,0:T(8,128)S(1)} %get-tuple-element.31), channel_id=1, source_target_pairs={{0,128},{128,0},{256,384},{384,256},{512,640},{640,512},{768,896},... | collective-permute-start | bytes 1572872 | tf_op jit(solution)/shard_map/ppermute | solution.py:242
  7.2 0.7 copy-start.13
  7.2 0.7 copy-start.14
  7.9 30.0 %collective-permute-start.4 = (f32[2,128,128]{2,1,0:T(8,128)S(1)}, f32[2,128,128]{2,1,0:T(8,128)S(1)}, u32[]{:S(2)}, u32[]{:S(2)}) collective-permute-start(f32[2,128,128]{2,1,0:T(8,128)S(1)} %pad_maximum_fusion.2), channel_id=1, source_target_pairs={{0,256},{128,896},{256,0},{384,640},{512,768},{640,384},{768,512},... | collective-permute-start | bytes 393224 | tf_op jit(solution)/shard_map/ppermute | solution.py:222
  24.7 21.8 %collective-permute-start.1 = (f32[2,128,128]{2,1,0:T(8,128)S(1)}, f32[2,128,128]{2,1,0:T(8,128)S(1)}, u32[]{:S(2)}, u32[]{:S(2)}) collective-permute-start(f32[2,128,128]{2,1,0:T(8,128)S(1)} %pad_maximum_fusion.1), channel_id=1, source_target_pairs={{0,256},{128,896},{256,0},{384,640},{512,768},{640,384},{768,512},... | collective-permute-start | bytes 393224 | tf_op jit(solution)/shard_map/ppermute | solution.py:222
  38.0 27.2 %collective-permute-start.5 = (f32[2,128,128]{2,1,0:T(8,128)S(1)}, f32[2,128,128]{2,1,0:T(8,128)S(1)}, u32[]{:S(2)}, u32[]{:S(2)}) collective-permute-start(f32[2,128,128]{2,1,0:T(8,128)S(1)} %pad_maximum_fusion.3), channel_id=1, source_target_pairs={{0,768},{128,384},{256,512},{384,128},{512,256},{640,896},{768,0},... | collective-permute-start | bytes 393224 | tf_op jit(solution)/shard_map/ppermute | solution.py:223
  47.2 6.0 %copy-start.16 = (s32[8]{0:T(128)S(1)}, s32[8]{0:T(128)}, u32[]{:S(2)}) copy-start(s32[8]{0:T(128)} %param.10) | copy-start | bytes 100
  47.2 22.2 %collective-permute-start.6 = (f32[2,128,128]{2,1,0:T(8,128)S(1)}, f32[2,128,128]{2,1,0:T(8,128)S(1)}, u32[]{:S(2)}, u32[]{:S(2)}) collective-permute-start(f32[2,128,128]{2,1,0:T(8,128)S(1)} %pad_maximum_fusion.4), channel_id=1, source_target_pairs={{0,768},{128,384},{256,512},{384,128},{512,256},{640,896},{768,0},... | collective-permute-start | bytes 393224 | tf_op jit(solution)/shard_map/ppermute | solution.py:223
  53.5 11.8 %copy-start.12 = (f32[12]{0:T(128)}, f32[12]{0:T(128)S(1)}, u32[]{:S(2)}) copy-start(f32[12]{0:T(128)S(1)} %select_reduce_fusion.coef_ref) | copy-start | bytes 148
  65.2 2.1 %copy-start.7 = (f32[520,128]{1,0:T(8,128)}, f32[520,128]{1,0:T(8,128)S(1)}, u32[]{:S(2)}) copy-start(f32[520,128]{1,0:T(8,128)S(1)} %select_maximum_fusion.message_ref) | copy-start | bytes 798724
  65.2 12.4 %collective-permute-start.7 = (f32[520,128]{1,0:T(8,128)S(1)}, f32[520,128]{1,0:T(8,128)S(1)}, u32[]{:S(2)}, u32[]{:S(2)}) collective-permute-start(f32[520,128]{1,0:T(8,128)S(1)} %select_maximum_fusion.message_ref), channel_id=1, source_target_pairs={{1,0},{2,1},{3,2},{4,3},{5,4},{6,5},{7,6},{8,7},{9,8},{10,9},{11,1... | collective-permute-start | bytes 798728 | tf_op jit(solution)/shard_map/ppermute | solution.py:237
  69.4 8.2 %copy-start.11 = (f32[2,128,128]{2,1,0:T(8,128)}, f32[2,128,128]{2,1,0:T(8,128)S(1)}, u32[]{:S(2)}) copy-start(f32[2,128,128]{2,1,0:T(8,128)S(1)} %collective-permute-done.6) | copy-start | bytes 393220
  77.7 0.7 copy-start.8
  80.8 18.2 %collective-permute-start.8 = (f32[128,128]{1,0:T(8,128)}, f32[128,128]{1,0:T(8,128)S(1)}, u32[]{:S(2)}, u32[]{:S(2)}) collective-permute-start(f32[128,128]{1,0:T(8,128)} %get-tuple-element.27.e0_ref.own_ref), channel_id=1, source_target_pairs={{0,256},{128,896},{256,0},{384,640},{512,768},{640,384},{768,512},... | collective-permute-start | bytes 196616 | tf_op jit(solution)/shard_map/ppermute | solution.py:247
  91.7 30.1 %collective-permute-start.10 = (f32[264,128]{1,0:T(8,128)}, f32[264,128]{1,0:T(8,128)S(1)}, u32[]{:S(2)}, u32[]{:S(2)}) collective-permute-start(f32[264,128]{1,0:T(8,128)} %get-tuple-element.28.c0_ref), channel_id=1, source_target_pairs={{0,256},{128,896},{256,0},{384,640},{512,768},{640,384},{768,512},... | collective-permute-start | bytes 405512 | tf_op jit(solution)/shard_map/ppermute | solution.py:248
  99.0 0.9 copy-start.9
  99.9 24.5 %collective-permute-start.9 = (f32[2,128,128]{2,1,0:T(8,128)S(1)}, f32[2,128,128]{2,1,0:T(8,128)S(1)}, u32[]{:S(2)}, u32[]{:S(2)}) collective-permute-start(f32[2,128,128]{2,1,0:T(8,128)S(1)} %pad_maximum_fusion.5), channel_id=1, source_target_pairs={{0,768},{128,384},{256,512},{384,128},{512,256},{640,896},{768,0},... | collective-permute-start | bytes 393224 | tf_op jit(solution)/shard_map/ppermute | solution.py:249
  109.5 0.8 copy-start.15
  110.3 11.5 %copy-start.3 = (f32[264,128]{1,0:T(8,128)S(1)}, f32[264,128]{1,0:T(8,128)}, u32[]{:S(2)}) copy-start(f32[264,128]{1,0:T(8,128)} %get-tuple-element.28.c0_ref) | copy-start | bytes 405508
  112.6 24.1 %collective-permute-start.3 = (f32[2,4,128,128]{3,2,1,0:T(8,128)}, f32[2,4,128,128]{3,2,1,0:T(8,128)S(1)}, u32[]{:S(2)}, u32[]{:S(2)}) collective-permute-start(f32[2,4,128,128]{3,2,1,0:T(8,128)} %get-tuple-element.22), channel_id=1, source_target_pairs={{1,0},{2,1},{3,2},{4,3},{5,4},{6,5},{7,6},{8,7},{9,8},{10,9},{11,1... | collective-permute-start | bytes 1572872 | tf_op jit(solution)/shard_map/ppermute | solution.py:243
  121.8 0.6 copy-start.4
  122.5 22.4 %collective-permute-start.11 = (f32[2,264,128]{2,1,0:T(8,128)S(1)}, f32[2,264,128]{2,1,0:T(8,128)S(1)}, u32[]{:S(2)}, u32[]{:S(2)}) collective-permute-start(f32[2,264,128]{2,1,0:T(8,128)S(1)} %pad_maximum_fusion), channel_id=1, source_target_pairs={{0,768},{128,384},{256,512},{384,128},{512,256},{640,896},{768,0},... | collective-permute-start | bytes 811016 | tf_op jit(solution)/shard_map/ppermute | solution.py:250
  124.4 0.7 copy-start.10
  127.2 24.1 %collective-permute-start.12 = (f32[4,128,128]{2,1,0:T(8,128)}, f32[4,128,128]{2,1,0:T(8,128)S(1)}, u32[]{:S(2)}, u32[]{:S(2)}) collective-permute-start(f32[4,128,128]{2,1,0:T(8,128)} %shard_map.68), channel_id=1, source_target_pairs={{0,1},{1,2},{2,3},{3,4},{4,5},{5,6},{6,7},{7,8},{8,9},{9,10},{10,1... | collective-permute-start | bytes 786440 | tf_op jit(solution)/shard_map/ppermute | solution.py:252
  136.7 8.2 %copy-start.5 = (f32[2,4,128,128]{3,2,1,0:T(8,128)}, f32[2,4,128,128]{3,2,1,0:T(8,128)S(1)}, u32[]{:S(2)}) copy-start(f32[2,4,128,128]{3,2,1,0:T(8,128)S(1)} %collective-permute-done.3.wr_ref) | copy-start | bytes 1572868
  144.9 0.7 copy-start.6
  151.3 41.2 %copy-start.1 = (f32[64,8,256]{2,1,0:T(8,128)S(1)}, f32[64,8,256]{2,1,0:T(8,128)}, u32[]{:S(2)}) copy-start(f32[64,8,256]{2,1,0:T(8,128)} %param.6) | copy-start | bytes 1572868
  152.4 40.0 %collective-permute-start.13 = (f32[4,64,256]{2,1,0:T(8,128)S(1)}, f32[4,64,256]{2,1,0:T(8,128)S(1)}, u32[]{:S(2)}, u32[]{:S(2)}) collective-permute-start(f32[4,64,256]{2,1,0:T(8,128)S(1)} %get-tuple-element.40), channel_id=1, source_target_pairs={{0,128},{128,0},{256,384},{384,256},{512,640},{640,512},{768,896},... | collective-permute-start | bytes 786440 | tf_op jit(solution)/shard_map/ppermute | solution.py:256

commit v8 on v7

--- a/solution.py
+++ b/solution.py
@@ -224,8 +224,8 @@
         return pick(x, chip), got[0], last.reshape(-1, BLK)
 
     first, second = to_owner(0), to_owner(1)
-    taken, pair_taper = lax.optimization_barrier((second[1], pair_taper))
-    second = second[0], taken, second[2]
+    taken, pair_taper = lax.optimization_barrier((first[1], pair_taper))
+    first = first[0], taken, first[2]
     tapers = jnp.dot(
         one_hot(pair_taper, taper_table.shape[0]), taper_table, precision=lax.Precision.HIGHEST
     ) / (ensemble - 1)
@@ -233,21 +233,23 @@
     slot = targets * 6 + (pair_blocks[:, 1] - targets) * 2 + pair_batch
     coefs = jnp.sum(one_hot(slot, 12) * tapers[:, None], axis=0)
     rows = jnp.pad(coefs[None], ((0, 7), (0, BLK - 12)))
-    message = jnp.concatenate([*first, rows])
-    after = lax.ppermute(message, "region", left)
-
     w = jnp.transpose(weights, (0, 2, 1, 3))
     mine = lax.dynamic_slice_in_dim(w, core * half, half, 1)
     theirs = lax.dynamic_slice_in_dim(w, (1 - core) * half, half, 1)
     w, low = gathered(mine, lax.ppermute(theirs, "member", SWAP))
-    w_right = lax.ppermute(low, "region", left)
+    rows, low = lax.optimization_barrier((rows, low))
+    message = jnp.concatenate([*first, rows])
+    after = lax.ppermute(message, "region", left)
+
 
     edge, own = covariances(message, *second, after)
     order = jnp.stack([chip, one, two, both])
     edge_near = lax.ppermute(edge, "member", step_one)
     own_near = lax.ppermute(own, "member", step_one)
     edge_far = lax.ppermute(jnp.stack([edge, edge_near]), "member", step_two)
-    own_far = lax.ppermute(jnp.stack([own, own_near]), "member", step_two)
+    out, low = lax.optimization_barrier((jnp.stack([own, own_near]), low))
+    own_far = lax.ppermute(out, "member", step_two)
+    w_right = lax.ppermute(low, "region", left)
     edges = edge, edge_near, edge_far
     from_left = lax.ppermute(outward(order, after, w, edges), "region", right)
     kept, sent = increments(coefs, order, w, w_right, edges, (own, own_near, own_far))

time: 194 us -> 212 us (1.093)
  the two profiles are of different devices: /device:TPU:193 before, /device:TPU:1 now
where the time goes in v8:
time: 212 us; the launch traced here: 211 us
  starting transfers between devices  148 us (70%)
  waiting for transfers between devices  37.4 us (18%)
  Pallas kernels  12.4 us (6%)
  local copies, waits for them, and re-layouts  9.22 us (4%)
  other arithmetic  3.69 us (2%)
    ppermute x1, starting transfers between devices, local(): came = lax.ppermute(sent, 'member', SWAP)  37.1 us
    ppermute x2, starting transfers between devices, to_owner(): last = lax.ppermute(jnp.stack([pick(x, two), got[1]]), 'member', step_two)  32.1 us
    ppermute x1, starting transfers between devices, local(): lax.ppermute(theirs, 'member', SWAP)  16.1 us
    ppermute x2, starting transfers between devices, to_owner(): lax.ppermute(jnp.stack([pick(x, one), pick(x, both)]), 'member', step_one)  14 us
    ppermute x1, starting transfers between devices, local(): w_right = lax.ppermute(low, 'region', left)  13.8 us
    ppermute x1, starting transfers between devices, local(): edge_near = lax.ppermute(edge, 'member', step_one)  12.8 us
    ppermute x2, waiting for transfers between devices, to_owner(): lax.ppermute(jnp.stack([pick(x, one), pick(x, both)]), 'member', step_one)  11.2 us
    ppermute x1, starting transfers between devices, local(): edge_far = lax.ppermute(jnp.stack([edge, edge_near]), 'member', step_two)  10.9 us
  transfers between devices with their start and end apart: 14, of which 8 were waited for; matrix products, arithmetic and copies ran while one was open for 2% of the time, Pallas kernels for 5%

profile of v8, /device:TPU:1, one launch (start us, length us, event | category | flops | bytes accessed | tf_op | source)
XLA Modules:
  0.0 211.1 jit_solution(9011016674056815796)
XLA Ops:
  0.0 1.3 copy.17
  1.4 16.1 %collective-permute-start = (f32[4,64,256]{2,1,0:T(8,128)S(1)}, f32[4,64,256]{2,1,0:T(8,128)S(1)}, u32[]{:S(2)}, u32[]{:S(2)}) collective-permute-start(f32[4,64,256]{2,1,0:T(8,128)S(1)} %get-tuple-element.22), channel_id=1, source_target_pairs={{0,128},{128,0},{256,384},{384,256},{512,640},{640,512},{768,896},... | collective-permute-start | bytes 786440 | tf_op jit(solution)/shard_map/ppermute | solution.py:211
  17.4 0.3 copy.15
  17.8 0.9 dynamic-slice_bitcast_fusion
  18.7 1.9 collective-permute-start.2
  20.6 0.0 copy-start.13
  20.6 0.0 copy-start.14
  20.7 0.7 copy-done.13
  21.4 10.1 %collective-permute-start.1 = (f32[2,128,128]{2,1,0:T(8,128)S(1)}, f32[2,128,128]{2,1,0:T(8,128)S(1)}, u32[]{:S(2)}, u32[]{:S(2)}) collective-permute-start(f32[2,128,128]{2,1,0:T(8,128)S(1)} %pad_maximum_fusion.2), channel_id=1, source_target_pairs={{0,256},{128,896},{256,0},{384,640},{512,768},{640,384},{768,512},... | collective-permute-start | bytes 393224 | tf_op jit(solution)/shard_map/ppermute | solution.py:222
  31.5 0.7 fusion.6
  32.2 3.9 %collective-permute-start.4 = (f32[2,128,128]{2,1,0:T(8,128)S(1)}, f32[2,128,128]{2,1,0:T(8,128)S(1)}, u32[]{:S(2)}, u32[]{:S(2)}) collective-permute-start(f32[2,128,128]{2,1,0:T(8,128)S(1)} %pad_maximum_fusion.4), channel_id=1, source_target_pairs={{0,256},{128,896},{256,0},{384,640},{512,768},{640,384},{768,512},... | collective-permute-start | bytes 393224 | tf_op jit(solution)/shard_map/ppermute | solution.py:222
  36.1 2.8 %collective-permute-done.1 = f32[2,128,128]{2,1,0:T(8,128)S(1)} collective-permute-done((f32[2,128,128]{2,1,0:T(8,128)S(1)}, f32[2,128,128]{2,1,0:T(8,128)S(1)}, u32[]{:S(2)}, u32[]{:S(2)}) %collective-permute-start.1) | collective-permute-done | bytes 131104 | tf_op jit(solution)/shard_map/ppermute | solution.py:222
  38.9 13.2 %collective-permute-start.3 = (f32[2,128,128]{2,1,0:T(8,128)S(1)}, f32[2,128,128]{2,1,0:T(8,128)S(1)}, u32[]{:S(2)}, u32[]{:S(2)}) collective-permute-start(f32[2,128,128]{2,1,0:T(8,128)S(1)} %pad_maximum_fusion.3), channel_id=1, source_target_pairs={{0,768},{128,384},{256,512},{384,128},{512,256},{640,896},{768,0},... | collective-permute-start | bytes 393224 | tf_op jit(solution)/shard_map/ppermute | solution.py:223
  52.2 8.4 %collective-permute-done.4 = f32[2,128,128]{2,1,0:T(8,128)S(1)} collective-permute-done((f32[2,128,128]{2,1,0:T(8,128)S(1)}, f32[2,128,128]{2,1,0:T(8,128)S(1)}, u32[]{:S(2)}, u32[]{:S(2)}) %collective-permute-start.4) | collective-permute-done | bytes 131104 | tf_op jit(solution)/shard_map/ppermute | solution.py:222
  60.6 0.6 fusion.13
  61.2 18.9 %collective-permute-start.5 = (f32[2,128,128]{2,1,0:T(8,128)S(1)}, f32[2,128,128]{2,1,0:T(8,128)S(1)}, u32[]{:S(2)}, u32[]{:S(2)}) collective-permute-start(f32[2,128,128]{2,1,0:T(8,128)S(1)} %pad_maximum_fusion.5), channel_id=1, source_target_pairs={{0,768},{128,384},{256,512},{384,128},{512,256},{640,896},{768,0},... | collective-permute-start | bytes 393224 | tf_op jit(solution)/shard_map/ppermute | solution.py:223
  80.2 0.2 fusion
  80.3 0.1 select_reduce_fusion.coef_ref
  80.4 0.6 copy-done.12
  81.0 0.8 copy-done.15
  81.8 2.3 %shard_map.64 = (f32[2,4,128,256]{3,2,1,0:T(8,128)}, f32[2,4,128,128]{3,2,1,0:T(8,128)}) custom-call(f32[2,4,64,256]{3,2,1,0:T(8,128)} %get-tuple-element.40.mine_ref, f32[2,4,64,256]{3,2,1,0:T(8,128)} %copy-done.15), custom_call_target="tpu_custom_call" | custom-call | flops 49999998976 | bytes 200000000 | tf_op jit(solution)/shard_map/pallas_call | solution.py:179
  84.2 1.9 collective-permute-start.6
  86.1 2.0 shard_map.65
  88.1 3.3 %collective-permute-done.6.message_ref = f32[520,128]{1,0:T(8,128)S(1)} collective-permute-done((f32[520,128]{1,0:T(8,128)S(1)}, f32[520,128]{1,0:T(8,128)S(1)}, u32[]{:S(2)}, u32[]{:S(2)}) %collective-permute-start.6) | collective-permute-done | bytes 266272 | tf_op jit(solution)/shard_map/ppermute | solution.py:242
  91.3 0.7 copy-done.8
  92.0 2.5 %shard_map.66 = (f32[128,128]{1,0:T(8,128)}, f32[264,128]{1,0:T(8,128)}) custom-call(bf16[512,128]{1,0:T(8,128)(2,1)} %get-tuple-element.29.high_ref, bf16[512,128]{1,0:T(8,128)(2,1)} %get-tuple-element.30.low_ref, f32[128,128]{1,0:T(8,128)} %get-tuple-element.31.square_ref, f32[128,128]{1,0:T(8,128)} %get-tuple-element.42.kept_ref, ...), custom_call_target="tpu_custom_call" | custom-call | flops 1000 | bytes 1000 | tf_op jit(solution)/shard_map/pallas_call | solution.py:81
  94.5 12.8 %collective-permute-start.9 = (f32[128,128]{1,0:T(8,128)}, f32[128,128]{1,0:T(8,128)S(1)}, u32[]{:S(2)}, u32[]{:S(2)}) collective-permute-start(f32[128,128]{1,0:T(8,128)} %get-tuple-element.35.e0_ref.own_ref), channel_id=1, source_target_pairs={{0,256},{128,896},{256,0},{384,640},{512,768},{640,384},{768,512},... | collective-permute-start | bytes 196616 | tf_op jit(solution)/shard_map/ppermute | solution.py:247
  107.3 1.9 collective-permute-start.7
  109.2 0.4 collective-permute-done.9.e1_ref.near_ref
  109.6 0.9 pad_maximum_fusion.6
  110.5 10.9 %collective-permute-start.10 = (f32[2,128,128]{2,1,0:T(8,128)S(1)}, f32[2,128,128]{2,1,0:T(8,128)S(1)}, u32[]{:S(2)}, u32[]{:S(2)}) collective-permute-start(f32[2,128,128]{2,1,0:T(8,128)S(1)} %pad_maximum_fusion.6), channel_id=1, source_target_pairs={{0,768},{128,384},{256,512},{384,128},{512,256},{640,896},{768,0},... | collective-permute-start | bytes 393224 | tf_op jit(solution)/shard_map/ppermute | solution.py:249
  121.5 0.6 pad_add_fusion.order_ref
  122.1 8.6 %collective-permute-done.7.c1_ref = f32[264,128]{1,0:T(8,128)S(1)} collective-permute-done((f32[264,128]{1,0:T(8,128)}, f32[264,128]{1,0:T(8,128)S(1)}, u32[]{:S(2)}, u32[]{:S(2)}) %collective-permute-start.7) | collective-permute-done | bytes 135200 | tf_op jit(solution)/shard_map/ppermute | solution.py:248
  130.8 0.6 copy-done.4
  131.4 3.3 %collective-permute-start.11 = (f32[2,264,128]{2,1,0:T(8,128)S(1)}, f32[2,264,128]{2,1,0:T(8,128)S(1)}, u32[]{:S(2)}, u32[]{:S(2)}) collective-permute-start(f32[2,264,128]{2,1,0:T(8,128)S(1)} %pad_maximum_fusion), channel_id=1, source_target_pairs={{0,768},{128,384},{256,512},{384,128},{512,256},{640,896},{768,0},... | collective-permute-start | bytes 811016 | tf_op jit(solution)/shard_map/ppermute | solution.py:251
  134.7 13.8 %collective-permute-start.8 = (f32[2,4,128,128]{3,2,1,0:T(8,128)S(1)}, f32[2,4,128,128]{3,2,1,0:T(8,128)S(1)}, u32[]{:S(2)}, u32[]{:S(2)}) collective-permute-start(f32[2,4,128,128]{3,2,1,0:T(8,128)S(1)} %copy-done.16), channel_id=1, source_target_pairs={{1,0},{2,1},{3,2},{4,3},{5,4},{6,5},{7,6},{8,7},{9,8},{10,9},{11,1... | collective-permute-start | bytes 1572872 | tf_op jit(solution)/shard_map/ppermute | solution.py:252
  148.5 0.6 copy-done.10
  149.2 2.2 %shard_map.68 = f32[4,128,128]{2,1,0:T(8,128)} custom-call(s32[4]{0:T(128)} %pad_add_fusion.order_ref, f32[520,128]{1,0:T(8,128)} %copy-done.8, f32[2,4,128,256]{3,2,1,0:T(8,128)} %get-tuple-element.25.w_ref, f32[128,128]{1,0:T(8,128)} %get-tuple-element.35.e0_ref.own_ref, f32[128,128]{1,0:T(8,128)} %copy-done.9, f32[2,128,128]{2,1,0:T(8,128)} %copy-done.10), custom_call_target="tpu_custom_call" | custom-call | flops 49999998976 | bytes 200000000 | tf_op jit(solution)/shard_map/pallas_call | solution.py:102
  151.3 1.9 collective-permute-start.12
  153.3 6.2 %collective-permute-done.8.wr_ref = f32[2,4,128,128]{3,2,1,0:T(8,128)S(1)} collective-permute-done((f32[2,4,128,128]{3,2,1,0:T(8,128)S(1)}, f32[2,4,128,128]{3,2,1,0:T(8,128)S(1)}, u32[]{:S(2)}, u32[]{:S(2)}) %collective-permute-start.8) | collective-permute-done | bytes 524320 | tf_op jit(solution)/shard_map/ppermute | solution.py:252
  159.5 0.8 copy-done.5
  160.3 3.5 %shard_map.67 = (f32[4,64,256]{2,1,0:T(8,128)}, f32[4,64,256]{2,1,0:T(8,128)}) custom-call(f32[12]{0:T(128)} %copy-done.12, s32[4]{0:T(128)} %pad_add_fusion.order_ref, f32[2,4,128,256]{3,2,1,0:T(8,128)} %get-tuple-element.25.w_ref, f32[2,4,128,128]{3,2,1,0:T(8,128)} %copy-done.5, f32[128,128]{1,0:T(8,128)} %get-tuple-element.35.e0_ref.own_ref, ...), custom_call_target="tpu_custom_call" | custom-call | flops 1000 | bytes 1000 | tf_op jit(solution)/shard_map/pallas_call | solution.py:159
  163.8 6.6 %collective-permute-done.12 = f32[4,128,128]{2,1,0:T(8,128)S(1)} collective-permute-done((f32[4,128,128]{2,1,0:T(8,128)}, f32[4,128,128]{2,1,0:T(8,128)S(1)}, u32[]{:S(2)}, u32[]{:S(2)}) %collective-permute-start.12) | collective-permute-done | bytes 262176 | tf_op jit(solution)/shard_map/ppermute | solution.py:254
  170.4 1.1 fusion.4
  171.5 37.1 %collective-permute-start.13 = (f32[4,64,256]{2,1,0:T(8,128)S(1)}, f32[4,64,256]{2,1,0:T(8,128)S(1)}, u32[]{:S(2)}, u32[]{:S(2)}) collective-permute-start(f32[4,64,256]{2,1,0:T(8,128)S(1)} %get-tuple-element.48), channel_id=1, source_target_pairs={{0,128},{128,0},{256,384},{384,256},{512,640},{640,512},{768,896},... | collective-permute-start | bytes 786440 | tf_op jit(solution)/shard_map/ppermute | solution.py:258
  208.6 1.1 collective-permute-done.13
  209.8 0.2 fusion.2
  210.0 1.1 copy.18
  (45 shorter events, 0.3 us)
Async XLA Ops:
  0.0 80.1 %copy-start = (f32[8]{0:T(128)S(1)}, f32[8]{0:T(128)}, u32[]{:S(2)}) copy-start(f32[8]{0:T(128)} %param.8) | copy-start | bytes 100
  0.0 17.4 %copy-start.2 = (f32[2,64,8,256]{3,2,1,0:T(8,128)S(1)}, f32[2,64,8,256]{3,2,1,0:T(8,128)}, u32[]{:S(2)}) copy-start(f32[2,64,8,256]{3,2,1,0:T(8,128)} %param.7) | copy-start | bytes 3145732
  1.4 20.0 %collective-permute-start = (f32[4,64,256]{2,1,0:T(8,128)S(1)}, f32[4,64,256]{2,1,0:T(8,128)S(1)}, u32[]{:S(2)}, u32[]{:S(2)}) collective-permute-start(f32[4,64,256]{2,1,0:T(8,128)S(1)} %get-tuple-element.22), channel_id=1, source_target_pairs={{0,128},{128,0},{256,384},{384,256},{512,640},{640,512},{768,896},... | collective-permute-start | bytes 786440 | tf_op jit(solution)/shard_map/ppermute | solution.py:211
  18.7 62.4 %collective-permute-start.2 = (f32[2,4,64,256]{3,2,1,0:T(8,128)S(1)}, f32[2,4,64,256]{3,2,1,0:T(8,128)S(1)}, u32[]{:S(2)}, u32[]{:S(2)}) collective-permute-start(f32[2,4,64,256]{3,2,1,0:T(8,128)S(1)} %get-tuple-element.39), channel_id=1, source_target_pairs={{0,128},{128,0},{256,384},{384,256},{512,640},{640,512},{768,896},... | collective-permute-start | bytes 1572872 | tf_op jit(solution)/shard_map/ppermute | solution.py:239
  20.6 0.7 copy-start.13
  20.6 0.7 copy-start.14
  21.4 17.5 %collective-permute-start.1 = (f32[2,128,128]{2,1,0:T(8,128)S(1)}, f32[2,128,128]{2,1,0:T(8,128)S(1)}, u32[]{:S(2)}, u32[]{:S(2)}) collective-permute-start(f32[2,128,128]{2,1,0:T(8,128)S(1)} %pad_maximum_fusion.2), channel_id=1, source_target_pairs={{0,256},{128,896},{256,0},{384,640},{512,768},{640,384},{768,512},... | collective-permute-start | bytes 393224 | tf_op jit(solution)/shard_map/ppermute | solution.py:222
  32.2 28.4 %collective-permute-start.4 = (f32[2,128,128]{2,1,0:T(8,128)S(1)}, f32[2,128,128]{2,1,0:T(8,128)S(1)}, u32[]{:S(2)}, u32[]{:S(2)}) collective-permute-start(f32[2,128,128]{2,1,0:T(8,128)S(1)} %pad_maximum_fusion.4), channel_id=1, source_target_pairs={{0,256},{128,896},{256,0},{384,640},{512,768},{640,384},{768,512},... | collective-permute-start | bytes 393224 | tf_op jit(solution)/shard_map/ppermute | solution.py:222
  38.9 45.2 %collective-permute-start.3 = (f32[2,128,128]{2,1,0:T(8,128)S(1)}, f32[2,128,128]{2,1,0:T(8,128)S(1)}, u32[]{:S(2)}, u32[]{:S(2)}) collective-permute-start(f32[2,128,128]{2,1,0:T(8,128)S(1)} %pad_maximum_fusion.3), channel_id=1, source_target_pairs={{0,768},{128,384},{256,512},{384,128},{512,256},{640,896},{768,0},... | collective-permute-start | bytes 393224 | tf_op jit(solution)/shard_map/ppermute | solution.py:223
  61.2 18.9 %copy-start.17 = (s32[8]{0:T(128)S(1)}, s32[8]{0:T(128)}, u32[]{:S(2)}) copy-start(s32[8]{0:T(128)} %param.10) | copy-start | bytes 100
  61.2 26.8 %collective-permute-start.5 = (f32[2,128,128]{2,1,0:T(8,128)S(1)}, f32[2,128,128]{2,1,0:T(8,128)S(1)}, u32[]{:S(2)}, u32[]{:S(2)}) collective-permute-start(f32[2,128,128]{2,1,0:T(8,128)S(1)} %pad_maximum_fusion.5), channel_id=1, source_target_pairs={{0,768},{128,384},{256,512},{384,128},{512,256},{640,896},{768,0},... | collective-permute-start | bytes 393224 | tf_op jit(solution)/shard_map/ppermute | solution.py:223
  80.4 0.6 copy-start.12
  81.0 0.8 copy-start.15
  84.1 1.9 copy-start.7
  84.2 7.2 %collective-permute-start.6 = (f32[520,128]{1,0:T(8,128)S(1)}, f32[520,128]{1,0:T(8,128)S(1)}, u32[]{:S(2)}, u32[]{:S(2)}) collective-permute-start(f32[520,128]{1,0:T(8,128)S(1)} %pad_maximum_fusion.1.message_ref), channel_id=1, source_target_pairs={{1,0},{2,1},{3,2},{4,3},{5,4},{6,5},{7,6},{8,7},{9,8},{10,9},{11,1... | collective-permute-start | bytes 798728 | tf_op jit(solution)/shard_map/ppermute | solution.py:242
  88.1 3.3 %copy-start.11 = (f32[2,128,128]{2,1,0:T(8,128)}, f32[2,128,128]{2,1,0:T(8,128)S(1)}, u32[]{:S(2)}) copy-start(f32[2,128,128]{2,1,0:T(8,128)S(1)} %collective-permute-done.5) | copy-start | bytes 393220
  91.3 0.7 copy-start.8
  92.0 42.7 %copy-start.16 = (f32[2,4,128,128]{3,2,1,0:T(8,128)S(1)}, f32[2,4,128,128]{3,2,1,0:T(8,128)}, u32[]{:S(2)}) copy-start(f32[2,4,128,128]{3,2,1,0:T(8,128)} %get-tuple-element.34) | copy-start | bytes 1572868
  94.5 15.1 %collective-permute-start.9 = (f32[128,128]{1,0:T(8,128)}, f32[128,128]{1,0:T(8,128)S(1)}, u32[]{:S(2)}, u32[]{:S(2)}) collective-permute-start(f32[128,128]{1,0:T(8,128)} %get-tuple-element.35.e0_ref.own_ref), channel_id=1, source_target_pairs={{0,256},{128,896},{256,0},{384,640},{512,768},{640,384},{768,512},... | collective-permute-start | bytes 196616 | tf_op jit(solution)/shard_map/ppermute | solution.py:247
  107.3 23.4 %collective-permute-start.7 = (f32[264,128]{1,0:T(8,128)}, f32[264,128]{1,0:T(8,128)S(1)}, u32[]{:S(2)}, u32[]{:S(2)}) collective-permute-start(f32[264,128]{1,0:T(8,128)} %get-tuple-element.32.c0_ref), channel_id=1, source_target_pairs={{0,256},{128,896},{256,0},{384,640},{512,768},{640,384},{768,512},... | collective-permute-start | bytes 405512 | tf_op jit(solution)/shard_map/ppermute | solution.py:248
  109.6 0.9 copy-start.9
  109.6 21.1 %copy-start.3 = (f32[264,128]{1,0:T(8,128)S(1)}, f32[264,128]{1,0:T(8,128)}, u32[]{:S(2)}) copy-start(f32[264,128]{1,0:T(8,128)} %get-tuple-element.32.c0_ref) | copy-start | bytes 405508
  110.5 37.9 %collective-permute-start.10 = (f32[2,128,128]{2,1,0:T(8,128)S(1)}, f32[2,128,128]{2,1,0:T(8,128)S(1)}, u32[]{:S(2)}, u32[]{:S(2)}) collective-permute-start(f32[2,128,128]{2,1,0:T(8,128)S(1)} %pad_maximum_fusion.6), channel_id=1, source_target_pairs={{0,768},{128,384},{256,512},{384,128},{512,256},{640,896},{768,0},... | collective-permute-start | bytes 393224 | tf_op jit(solution)/shard_map/ppermute | solution.py:249
  130.7 0.7 copy-start.4
  131.4 21.9 %collective-permute-start.11 = (f32[2,264,128]{2,1,0:T(8,128)S(1)}, f32[2,264,128]{2,1,0:T(8,128)S(1)}, u32[]{:S(2)}, u32[]{:S(2)}) collective-permute-start(f32[2,264,128]{2,1,0:T(8,128)S(1)} %pad_maximum_fusion), channel_id=1, source_target_pairs={{0,768},{128,384},{256,512},{384,128},{512,256},{640,896},{768,0},... | collective-permute-start | bytes 811016 | tf_op jit(solution)/shard_map/ppermute | solution.py:251
  134.7 24.8 %collective-permute-start.8 = (f32[2,4,128,128]{3,2,1,0:T(8,128)S(1)}, f32[2,4,128,128]{3,2,1,0:T(8,128)S(1)}, u32[]{:S(2)}, u32[]{:S(2)}) collective-permute-start(f32[2,4,128,128]{3,2,1,0:T(8,128)S(1)} %copy-done.16), channel_id=1, source_target_pairs={{1,0},{2,1},{3,2},{4,3},{5,4},{6,5},{7,6},{8,7},{9,8},{10,9},{11,1... | collective-permute-start | bytes 1572872 | tf_op jit(solution)/shard_map/ppermute | solution.py:252
  148.5 0.7 copy-start.10
  151.3 19.0 %collective-permute-start.12 = (f32[4,128,128]{2,1,0:T(8,128)}, f32[4,128,128]{2,1,0:T(8,128)S(1)}, u32[]{:S(2)}, u32[]{:S(2)}) collective-permute-start(f32[4,128,128]{2,1,0:T(8,128)} %shard_map.68), channel_id=1, source_target_pairs={{0,1},{1,2},{2,3},{3,4},{4,5},{5,6},{6,7},{7,8},{8,9},{9,10},{10,1... | collective-permute-start | bytes 786440 | tf_op jit(solution)/shard_map/ppermute | solution.py:254
  153.3 6.2 %copy-start.6 = (f32[2,264,128]{2,1,0:T(8,128)}, f32[2,264,128]{2,1,0:T(8,128)S(1)}, u32[]{:S(2)}) copy-start(f32[2,264,128]{2,1,0:T(8,128)S(1)} %collective-permute-done.11.c2_ref) | copy-start | bytes 811012
  159.5 0.8 copy-start.5
  170.4 39.4 %copy-start.1 = (f32[64,8,256]{2,1,0:T(8,128)S(1)}, f32[64,8,256]{2,1,0:T(8,128)}, u32[]{:S(2)}) copy-start(f32[64,8,256]{2,1,0:T(8,128)} %param.6) | copy-start | bytes 1572868
  171.5 38.3 %collective-permute-start.13 = (f32[4,64,256]{2,1,0:T(8,128)S(1)}, f32[4,64,256]{2,1,0:T(8,128)S(1)}, u32[]{:S(2)}, u32[]{:S(2)}) collective-permute-start(f32[4,64,256]{2,1,0:T(8,128)S(1)} %get-tuple-element.48), channel_id=1, source_target_pairs={{0,128},{128,0},{256,384},{384,256},{512,640},{640,512},{768,896},... | collective-permute-start | bytes 786440 | tf_op jit(solution)/shard_map/ppermute | solution.py:258

commit v9 on v8

--- a/solution.py
+++ b/solution.py
@@ -89,14 +89,16 @@
     return own_ref[...], near_ref[...], far_ref[0], far_ref[1]
 
 
-def outward_kernel(order_ref, message_ref, w_ref, own_ref, near_ref, far_ref, out_ref):
+def outward_kernel(
+    order_ref, message_ref, w_ref, own_ref, near_ref, far_ref, ahead_ref, out_ref
+):
     for step, edge in enumerate(pieces(own_ref, near_ref, far_ref)):
         level = order_ref[step]
         mixed = message_ref[:1, :1] * w_ref[0, level] + message_ref[:1, 1:2] * w_ref[1, level]
         out_ref[level] = product(split(mixed), split(edge), PLAIN)
 
 
-def outward(order, message, w, edges):
+def outward(order, message, w, edges, ahead):
     levels, members = w.shape[1:3]
     whole = lambda x: pl.BlockSpec(x.shape, lambda i: (0,) * x.ndim)
     return pl.pallas_call(
@@ -107,11 +109,12 @@
             pl.BlockSpec((8, BLK), lambda i: (message.shape[0] // 8 - 1, 0)),
             pl.BlockSpec((2, levels, members, BLK), lambda i: (0, 0, 0, 1)),
             *(whole(x) for x in edges),
+            pl.BlockSpec(memory_space=pl.ANY),
         ],
         out_specs=pl.BlockSpec((levels, members, BLK), lambda i: (0, 0, 0)),
         out_shape=jax.ShapeDtypeStruct((levels, members, BLK), jnp.float32),
         cost_estimate=LONG,
-    )(order, message, w, *edges)
+    )(order, message, w, *edges, ahead)
 
 
 def increment_kernel(
@@ -241,17 +244,16 @@
     message = jnp.concatenate([*first, rows])
     after = lax.ppermute(message, "region", left)
 
+    w_right = lax.ppermute(low, "region", left)
 
     edge, own = covariances(message, *second, after)
     order = jnp.stack([chip, one, two, both])
     edge_near = lax.ppermute(edge, "member", step_one)
     own_near = lax.ppermute(own, "member", step_one)
     edge_far = lax.ppermute(jnp.stack([edge, edge_near]), "member", step_two)
-    out, low = lax.optimization_barrier((jnp.stack([own, own_near]), low))
-    own_far = lax.ppermute(out, "member", step_two)
-    w_right = lax.ppermute(low, "region", left)
+    own_far = lax.ppermute(jnp.stack([own, own_near]), "member", step_two)
     edges = edge, edge_near, edge_far
-    from_left = lax.ppermute(outward(order, after, w, edges), "region", right)
+    from_left = lax.ppermute(outward(order, after, w, edges, w_right), "region", right)
     kept, sent = increments(coefs, order, w, w_right, edges, (own, own_near, own_far))
     from_left = jnp.pad(from_left, ((0, 0), (0, 0), (0, column_count - BLK)))
     kept, sent = kept + from_left[:, :member_loc], sent + from_left[:, member_loc:]

time: 212 us -> 212 us (level)
  the two profiles are of different devices: /device:TPU:1 before, /device:TPU:193 now
where the time goes in v9:
time: 212 us; the launch traced here: 211 us
  starting transfers between devices  104 us (49%)
  waiting for transfers between devices  80.9 us (38%)
  Pallas kernels  12.3 us (6%)
  local copies, waits for them, and re-layouts  9.27 us (4%)
  other arithmetic  3.69 us (2%)
    ppermute x1, starting transfers between devices, local(): came = lax.ppermute(sent, 'member', SWAP)  42.4 us
    ppermute x1, waiting for transfers between devices, local(): edge_near = lax.ppermute(edge, 'member', step_one)  27.9 us
    ppermute x2, starting transfers between devices, to_owner(): lax.ppermute(jnp.stack([pick(x, one), pick(x, both)]), 'member', step_one)  18 us
    ppermute x2, starting transfers between devices, to_owner(): last = lax.ppermute(jnp.stack([pick(x, two), got[1]]), 'member', step_two)  14.5 us
    ppermute x1, waiting for transfers between devices, local(): edge_far = lax.ppermute(jnp.stack([edge, edge_near]), 'member', step_two)  12.7 us
    ppermute x2, waiting for transfers between devices, to_owner(): lax.ppermute(jnp.stack([pick(x, one), pick(x, both)]), 'member', step_one)  11.4 us
    ppermute x1, starting transfers between devices, local(): edge_near = lax.ppermute(edge, 'member', step_one)  11.3 us
    ppermute x1, waiting for transfers between devices, local(): own_near = lax.ppermute(own, 'member', step_one)  9.39 us
  transfers between devices with their start and end apart: 14, of which 9 were waited for; matrix products, arithmetic and copies ran while one was open for 2% of the time, Pallas kernels for 6%

profile of v9, /device:TPU:193, one launch (start us, length us, event | category | flops | bytes accessed | tf_op | source)
XLA Modules:
  0.0 211.1 jit_solution(17897705070604851642)
XLA Ops:
  0.0 1.3 copy.17
  1.4 2.6 %collective-permute-start = (f32[4,64,256]{2,1,0:T(8,128)S(1)}, f32[4,64,256]{2,1,0:T(8,128)S(1)}, u32[]{:S(2)}, u32[]{:S(2)}) collective-permute-start(f32[4,64,256]{2,1,0:T(8,128)S(1)} %get-tuple-element.20), channel_id=1, source_target_pairs={{0,128},{128,0},{256,384},{384,256},{512,640},{640,512},{768,896},... | collective-permute-start | bytes 786440 | tf_op jit(solution)/shard_map/ppermute | solution.py:214
  4.0 0.3 copy.15
  4.3 0.9 dynamic-slice_bitcast_fusion
  5.2 1.9 collective-permute-start.2
  7.2 0.7 copy-done.13
  7.9 16.1 %collective-permute-start.1 = (f32[2,128,128]{2,1,0:T(8,128)S(1)}, f32[2,128,128]{2,1,0:T(8,128)S(1)}, u32[]{:S(2)}, u32[]{:S(2)}) collective-permute-start(f32[2,128,128]{2,1,0:T(8,128)S(1)} %pad_maximum_fusion.2), channel_id=1, source_target_pairs={{0,256},{128,896},{256,0},{384,640},{512,768},{640,384},{768,512},... | collective-permute-start | bytes 393224 | tf_op jit(solution)/shard_map/ppermute | solution.py:225
  24.1 0.7 fusion.6
  24.7 1.9 collective-permute-start.5
  26.7 11.4 %collective-permute-done.1 = f32[2,128,128]{2,1,0:T(8,128)S(1)} collective-permute-done((f32[2,128,128]{2,1,0:T(8,128)S(1)}, f32[2,128,128]{2,1,0:T(8,128)S(1)}, u32[]{:S(2)}, u32[]{:S(2)}) %collective-permute-start.1) | collective-permute-done | bytes 131104 | tf_op jit(solution)/shard_map/ppermute | solution.py:225
  38.0 8.6 %collective-permute-start.4 = (f32[2,128,128]{2,1,0:T(8,128)S(1)}, f32[2,128,128]{2,1,0:T(8,128)S(1)}, u32[]{:S(2)}, u32[]{:S(2)}) collective-permute-start(f32[2,128,128]{2,1,0:T(8,128)S(1)} %pad_maximum_fusion.3), channel_id=1, source_target_pairs={{0,768},{128,384},{256,512},{384,128},{512,256},{640,896},{768,0},... | collective-permute-start | bytes 393224 | tf_op jit(solution)/shard_map/ppermute | solution.py:226
  46.6 0.6 fusion.13
  47.3 5.9 %collective-permute-start.6 = (f32[2,128,128]{2,1,0:T(8,128)S(1)}, f32[2,128,128]{2,1,0:T(8,128)S(1)}, u32[]{:S(2)}, u32[]{:S(2)}) collective-permute-start(f32[2,128,128]{2,1,0:T(8,128)S(1)} %pad_maximum_fusion.5), channel_id=1, source_target_pairs={{0,768},{128,384},{256,512},{384,128},{512,256},{640,896},{768,0},... | collective-permute-start | bytes 393224 | tf_op jit(solution)/shard_map/ppermute | solution.py:226
  53.2 0.2 fusion
  53.4 0.1 select_reduce_fusion.coef_ref
  53.5 0.6 copy-done.12
  54.1 0.8 copy-done.15
  54.9 2.3 %shard_map.64 = (f32[2,4,128,256]{3,2,1,0:T(8,128)}, f32[2,4,128,128]{3,2,1,0:T(8,128)}) custom-call(f32[2,4,64,256]{3,2,1,0:T(8,128)} %get-tuple-element.36.mine_ref, f32[2,4,64,256]{3,2,1,0:T(8,128)} %copy-done.15), custom_call_target="tpu_custom_call" | custom-call | flops 49999998976 | bytes 200000000 | tf_op jit(solution)/shard_map/pallas_call | solution.py:182
  57.1 8.0 %collective-permute-done.4 = f32[2,128,128]{2,1,0:T(8,128)S(1)} collective-permute-done((f32[2,128,128]{2,1,0:T(8,128)S(1)}, f32[2,128,128]{2,1,0:T(8,128)S(1)}, u32[]{:S(2)}, u32[]{:S(2)}) %collective-permute-start.4) | collective-permute-done | bytes 131104 | tf_op jit(solution)/shard_map/ppermute | solution.py:226
  65.2 2.2 %collective-permute-start.7 = (f32[520,128]{1,0:T(8,128)S(1)}, f32[520,128]{1,0:T(8,128)S(1)}, u32[]{:S(2)}, u32[]{:S(2)}) collective-permute-start(f32[520,128]{1,0:T(8,128)S(1)} %pad_maximum_fusion.1.message_ref), channel_id=1, source_target_pairs={{1,0},{2,1},{3,2},{4,3},{5,4},{6,5},{7,6},{8,7},{9,8},{10,9},{11,1... | collective-permute-start | bytes 798728 | tf_op jit(solution)/shard_map/ppermute | solution.py:245
  67.4 2.5 %collective-permute-start.3 = (f32[2,4,128,128]{3,2,1,0:T(8,128)S(1)}, f32[2,4,128,128]{3,2,1,0:T(8,128)S(1)}, u32[]{:S(2)}, u32[]{:S(2)}) collective-permute-start(f32[2,4,128,128]{3,2,1,0:T(8,128)S(1)} %copy-done.16), channel_id=1, source_target_pairs={{1,0},{2,1},{3,2},{4,3},{5,4},{6,5},{7,6},{8,7},{9,8},{10,9},{11,1... | collective-permute-start | bytes 1572872 | tf_op jit(solution)/shard_map/ppermute | solution.py:247
  69.9 2.0 shard_map.65
  71.8 4.9 %collective-permute-done.7.message_ref = f32[520,128]{1,0:T(8,128)S(1)} collective-permute-done((f32[520,128]{1,0:T(8,128)S(1)}, f32[520,128]{1,0:T(8,128)S(1)}, u32[]{:S(2)}, u32[]{:S(2)}) %collective-permute-start.7) | collective-permute-done | bytes 266272 | tf_op jit(solution)/shard_map/ppermute | solution.py:245
  76.7 0.7 copy-done.8
  77.4 2.4 %shard_map.66 = (f32[128,128]{1,0:T(8,128)}, f32[264,128]{1,0:T(8,128)}) custom-call(bf16[512,128]{1,0:T(8,128)(2,1)} %get-tuple-element.28.high_ref, bf16[512,128]{1,0:T(8,128)(2,1)} %get-tuple-element.29.low_ref, f32[128,128]{1,0:T(8,128)} %get-tuple-element.30.square_ref, f32[128,128]{1,0:T(8,128)} %get-tuple-element.38.kept_ref, ...), custom_call_target="tpu_custom_call" | custom-call | flops 1000 | bytes 1000 | tf_op jit(solution)/shard_map/pallas_call | solution.py:81
  79.8 11.3 %collective-permute-start.8 = (f32[128,128]{1,0:T(8,128)}, f32[128,128]{1,0:T(8,128)S(1)}, u32[]{:S(2)}, u32[]{:S(2)}) collective-permute-start(f32[128,128]{1,0:T(8,128)} %get-tuple-element.31.e0_ref.own_ref), channel_id=1, source_target_pairs={{0,256},{128,896},{256,0},{384,640},{512,768},{640,384},{768,512},... | collective-permute-start | bytes 196616 | tf_op jit(solution)/shard_map/ppermute | solution.py:251
  91.1 2.7 %collective-permute-start.10 = (f32[264,128]{1,0:T(8,128)}, f32[264,128]{1,0:T(8,128)S(1)}, u32[]{:S(2)}, u32[]{:S(2)}) collective-permute-start(f32[264,128]{1,0:T(8,128)} %get-tuple-element.32.c0_ref), channel_id=1, source_target_pairs={{0,256},{128,896},{256,0},{384,640},{512,768},{640,384},{768,512},... | collective-permute-start | bytes 405512 | tf_op jit(solution)/shard_map/ppermute | solution.py:252
  93.8 27.9 %collective-permute-done.8.e1_ref.near_ref = f32[128,128]{1,0:T(8,128)S(1)} collective-permute-done((f32[128,128]{1,0:T(8,128)}, f32[128,128]{1,0:T(8,128)S(1)}, u32[]{:S(2)}, u32[]{:S(2)}) %collective-permute-start.8) | collective-permute-done | bytes 65568 | tf_op jit(solution)/shard_map/ppermute | solution.py:251
  121.7 0.9 pad_maximum_fusion.6
  122.6 1.9 collective-permute-start.9
  124.6 0.6 pad_add_fusion.order_ref
  125.2 9.4 %collective-permute-done.10.c1_ref = f32[264,128]{1,0:T(8,128)S(1)} collective-permute-done((f32[264,128]{1,0:T(8,128)}, f32[264,128]{1,0:T(8,128)S(1)}, u32[]{:S(2)}, u32[]{:S(2)}) %collective-permute-start.10) | collective-permute-done | bytes 135200 | tf_op jit(solution)/shard_map/ppermute | solution.py:252
  134.6 0.6 copy-done.4
  135.2 2.7 %collective-permute-start.11 = (f32[2,264,128]{2,1,0:T(8,128)S(1)}, f32[2,264,128]{2,1,0:T(8,128)S(1)}, u32[]{:S(2)}, u32[]{:S(2)}) collective-permute-start(f32[2,264,128]{2,1,0:T(8,128)S(1)} %pad_maximum_fusion), channel_id=1, source_target_pairs={{0,768},{128,384},{256,512},{384,128},{512,256},{640,896},{768,0},... | collective-permute-start | bytes 811016 | tf_op jit(solution)/shard_map/ppermute | solution.py:254
  137.9 12.7 %collective-permute-done.9.e2_ref.far_ref = f32[2,128,128]{2,1,0:T(8,128)S(1)} collective-permute-done((f32[2,128,128]{2,1,0:T(8,128)S(1)}, f32[2,128,128]{2,1,0:T(8,128)S(1)}, u32[]{:S(2)}, u32[]{:S(2)}) %collective-permute-start.9) | collective-permute-done | bytes 131104 | tf_op jit(solution)/shard_map/ppermute | solution.py:253
  150.6 0.6 copy-done.10
  151.3 0.2 copy-done.5
  151.5 2.2 %shard_map.68 = f32[4,128,128]{2,1,0:T(8,128)} custom-call(s32[4]{0:T(128)} %pad_add_fusion.order_ref, f32[520,128]{1,0:T(8,128)} %copy-done.8, f32[2,4,128,256]{3,2,1,0:T(8,128)} %get-tuple-element.23.w_ref, f32[128,128]{1,0:T(8,128)} %get-tuple-element.31.e0_ref.own_ref, f32[128,128]{1,0:T(8,128)} %copy-done.9, f32[2,128,128]{2,1,0:T(8,128)} %copy-done.10, ...), custom_call_target="tpu_custom_call" | custom-call | flops 49999998976 | bytes 200000000 | tf_op jit(solution)/shard_map/pallas_call | solution.py:104
  153.6 1.9 collective-permute-start.12
  155.6 1.3 collective-permute-done.11.c2_ref
  156.8 0.7 copy-done.6
  157.5 3.5 %shard_map.67 = (f32[4,64,256]{2,1,0:T(8,128)}, f32[4,64,256]{2,1,0:T(8,128)}) custom-call(f32[12]{0:T(128)} %copy-done.12, s32[4]{0:T(128)} %pad_add_fusion.order_ref, f32[2,4,128,256]{3,2,1,0:T(8,128)} %get-tuple-element.23.w_ref, f32[2,4,128,128]{3,2,1,0:T(8,128)} %copy-done.5, f32[128,128]{1,0:T(8,128)} %get-tuple-element.31.e0_ref.own_ref, ...), custom_call_target="tpu_custom_call" | custom-call | flops 1000 | bytes 1000 | tf_op jit(solution)/shard_map/pallas_call | solution.py:162
  161.0 4.2 %collective-permute-done.12 = f32[4,128,128]{2,1,0:T(8,128)S(1)} collective-permute-done((f32[4,128,128]{2,1,0:T(8,128)}, f32[4,128,128]{2,1,0:T(8,128)S(1)}, u32[]{:S(2)}, u32[]{:S(2)}) %collective-permute-start.12) | collective-permute-done | bytes 262176 | tf_op jit(solution)/shard_map/ppermute | solution.py:256
  165.2 1.1 fusion.4
  166.3 42.4 %collective-permute-start.13 = (f32[4,64,256]{2,1,0:T(8,128)S(1)}, f32[4,64,256]{2,1,0:T(8,128)S(1)}, u32[]{:S(2)}, u32[]{:S(2)}) collective-permute-start(f32[4,64,256]{2,1,0:T(8,128)S(1)} %get-tuple-element.44), channel_id=1, source_target_pairs={{0,128},{128,0},{256,384},{384,256},{512,640},{640,512},{768,896},... | collective-permute-start | bytes 786440 | tf_op jit(solution)/shard_map/ppermute | solution.py:260
  208.7 1.1 collective-permute-done.13
  209.8 0.2 fusion.2
  210.0 1.1 copy.18
  (45 shorter events, 0.3 us)
Async XLA Ops:
  0.0 53.2 %copy-start = (f32[8]{0:T(128)S(1)}, f32[8]{0:T(128)}, u32[]{:S(2)}) copy-start(f32[8]{0:T(128)} %param.8) | copy-start | bytes 100
  0.0 4.0 %copy-start.2 = (f32[2,64,8,256]{3,2,1,0:T(8,128)S(1)}, f32[2,64,8,256]{3,2,1,0:T(8,128)}, u32[]{:S(2)}) copy-start(f32[2,64,8,256]{3,2,1,0:T(8,128)} %param.7) | copy-start | bytes 3145732
  1.4 6.5 %collective-permute-start = (f32[4,64,256]{2,1,0:T(8,128)S(1)}, f32[4,64,256]{2,1,0:T(8,128)S(1)}, u32[]{:S(2)}, u32[]{:S(2)}) collective-permute-start(f32[4,64,256]{2,1,0:T(8,128)S(1)} %get-tuple-element.20), channel_id=1, source_target_pairs={{0,128},{128,0},{256,384},{384,256},{512,640},{640,512},{768,896},... | collective-permute-start | bytes 786440 | tf_op jit(solution)/shard_map/ppermute | solution.py:214
  5.2 48.9 %collective-permute-start.2 = (f32[2,4,64,256]{3,2,1,0:T(8,128)S(1)}, f32[2,4,64,256]{3,2,1,0:T(8,128)S(1)}, u32[]{:S(2)}, u32[]{:S(2)}) collective-permute-start(f32[2,4,64,256]{3,2,1,0:T(8,128)S(1)} %get-tuple-element.35), channel_id=1, source_target_pairs={{0,128},{128,0},{256,384},{384,256},{512,640},{640,512},{768,896},... | collective-permute-start | bytes 1572872 | tf_op jit(solution)/shard_map/ppermute | solution.py:242
  7.2 0.7 copy-start.13
  7.2 0.7 copy-start.14
  7.9 30.1 %collective-permute-start.1 = (f32[2,128,128]{2,1,0:T(8,128)S(1)}, f32[2,128,128]{2,1,0:T(8,128)S(1)}, u32[]{:S(2)}, u32[]{:S(2)}) collective-permute-start(f32[2,128,128]{2,1,0:T(8,128)S(1)} %pad_maximum_fusion.2), channel_id=1, source_target_pairs={{0,256},{128,896},{256,0},{384,640},{512,768},{640,384},{768,512},... | collective-permute-start | bytes 393224 | tf_op jit(solution)/shard_map/ppermute | solution.py:225
  24.7 21.9 %collective-permute-start.5 = (f32[2,128,128]{2,1,0:T(8,128)S(1)}, f32[2,128,128]{2,1,0:T(8,128)S(1)}, u32[]{:S(2)}, u32[]{:S(2)}) collective-permute-start(f32[2,128,128]{2,1,0:T(8,128)S(1)} %pad_maximum_fusion.4), channel_id=1, source_target_pairs={{0,256},{128,896},{256,0},{384,640},{512,768},{640,384},{768,512},... | collective-permute-start | bytes 393224 | tf_op jit(solution)/shard_map/ppermute | solution.py:225
  38.0 27.1 %collective-permute-start.4 = (f32[2,128,128]{2,1,0:T(8,128)S(1)}, f32[2,128,128]{2,1,0:T(8,128)S(1)}, u32[]{:S(2)}, u32[]{:S(2)}) collective-permute-start(f32[2,128,128]{2,1,0:T(8,128)S(1)} %pad_maximum_fusion.3), channel_id=1, source_target_pairs={{0,768},{128,384},{256,512},{384,128},{512,256},{640,896},{768,0},... | collective-permute-start | bytes 393224 | tf_op jit(solution)/shard_map/ppermute | solution.py:226
  47.3 5.9 %copy-start.17 = (s32[8]{0:T(128)S(1)}, s32[8]{0:T(128)}, u32[]{:S(2)}) copy-start(s32[8]{0:T(128)} %param.10) | copy-start | bytes 100
  47.3 24.5 %collective-permute-start.6 = (f32[2,128,128]{2,1,0:T(8,128)S(1)}, f32[2,128,128]{2,1,0:T(8,128)S(1)}, u32[]{:S(2)}, u32[]{:S(2)}) collective-permute-start(f32[2,128,128]{2,1,0:T(8,128)S(1)} %pad_maximum_fusion.5), channel_id=1, source_target_pairs={{0,768},{128,384},{256,512},{384,128},{512,256},{640,896},{768,0},... | collective-permute-start | bytes 393224 | tf_op jit(solution)/shard_map/ppermute | solution.py:226
  53.5 0.6 copy-start.12
  54.1 0.8 copy-start.15
  57.1 10.2 %copy-start.16 = (f32[2,4,128,128]{3,2,1,0:T(8,128)S(1)}, f32[2,4,128,128]{3,2,1,0:T(8,128)}, u32[]{:S(2)}) copy-start(f32[2,4,128,128]{3,2,1,0:T(8,128)} %get-tuple-element.25) | copy-start | bytes 1572868
  65.2 4.7 %copy-start.7 = (f32[520,128]{1,0:T(8,128)}, f32[520,128]{1,0:T(8,128)S(1)}, u32[]{:S(2)}) copy-start(f32[520,128]{1,0:T(8,128)S(1)} %pad_maximum_fusion.1.message_ref) | copy-start | bytes 798724
  65.2 11.5 %collective-permute-start.7 = (f32[520,128]{1,0:T(8,128)S(1)}, f32[520,128]{1,0:T(8,128)S(1)}, u32[]{:S(2)}, u32[]{:S(2)}) collective-permute-start(f32[520,128]{1,0:T(8,128)S(1)} %pad_maximum_fusion.1.message_ref), channel_id=1, source_target_pairs={{1,0},{2,1},{3,2},{4,3},{5,4},{6,5},{7,6},{8,7},{9,8},{10,9},{11,1... | collective-permute-start | bytes 798728 | tf_op jit(solution)/shard_map/ppermute | solution.py:245
  67.4 83.2 %collective-permute-start.3 = (f32[2,4,128,128]{3,2,1,0:T(8,128)S(1)}, f32[2,4,128,128]{3,2,1,0:T(8,128)S(1)}, u32[]{:S(2)}, u32[]{:S(2)}) collective-permute-start(f32[2,4,128,128]{3,2,1,0:T(8,128)S(1)} %copy-done.16), channel_id=1, source_target_pairs={{1,0},{2,1},{3,2},{4,3},{5,4},{6,5},{7,6},{8,7},{9,8},{10,9},{11,1... | collective-permute-start | bytes 1572872 | tf_op jit(solution)/shard_map/ppermute | solution.py:247
  71.8 4.9 %copy-start.11 = (f32[2,128,128]{2,1,0:T(8,128)}, f32[2,128,128]{2,1,0:T(8,128)S(1)}, u32[]{:S(2)}) copy-start(f32[2,128,128]{2,1,0:T(8,128)S(1)} %collective-permute-done.6) | copy-start | bytes 393220
  76.7 0.7 copy-start.8
  79.8 41.9 %collective-permute-start.8 = (f32[128,128]{1,0:T(8,128)}, f32[128,128]{1,0:T(8,128)S(1)}, u32[]{:S(2)}, u32[]{:S(2)}) collective-permute-start(f32[128,128]{1,0:T(8,128)} %get-tuple-element.31.e0_ref.own_ref), channel_id=1, source_target_pairs={{0,256},{128,896},{256,0},{384,640},{512,768},{640,384},{768,512},... | collective-permute-start | bytes 196616 | tf_op jit(solution)/shard_map/ppermute | solution.py:251
  91.1 43.5 %collective-permute-start.10 = (f32[264,128]{1,0:T(8,128)}, f32[264,128]{1,0:T(8,128)S(1)}, u32[]{:S(2)}, u32[]{:S(2)}) collective-permute-start(f32[264,128]{1,0:T(8,128)} %get-tuple-element.32.c0_ref), channel_id=1, source_target_pairs={{0,256},{128,896},{256,0},{384,640},{512,768},{640,384},{768,512},... | collective-permute-start | bytes 405512 | tf_op jit(solution)/shard_map/ppermute | solution.py:252
  121.7 0.9 copy-start.9
  121.7 12.8 %copy-start.3 = (f32[264,128]{1,0:T(8,128)S(1)}, f32[264,128]{1,0:T(8,128)}, u32[]{:S(2)}) copy-start(f32[264,128]{1,0:T(8,128)} %get-tuple-element.32.c0_ref) | copy-start | bytes 405508
  122.6 28.0 %collective-permute-start.9 = (f32[2,128,128]{2,1,0:T(8,128)S(1)}, f32[2,128,128]{2,1,0:T(8,128)S(1)}, u32[]{:S(2)}, u32[]{:S(2)}) collective-permute-start(f32[2,128,128]{2,1,0:T(8,128)S(1)} %pad_maximum_fusion.6), channel_id=1, source_target_pairs={{0,768},{128,384},{256,512},{384,128},{512,256},{640,896},{768,0},... | collective-permute-start | bytes 393224 | tf_op jit(solution)/shard_map/ppermute | solution.py:253
  134.6 0.7 copy-start.4
  135.2 21.6 %collective-permute-start.11 = (f32[2,264,128]{2,1,0:T(8,128)S(1)}, f32[2,264,128]{2,1,0:T(8,128)S(1)}, u32[]{:S(2)}, u32[]{:S(2)}) collective-permute-start(f32[2,264,128]{2,1,0:T(8,128)S(1)} %pad_maximum_fusion), channel_id=1, source_target_pairs={{0,768},{128,384},{256,512},{384,128},{512,256},{640,896},{768,0},... | collective-permute-start | bytes 811016 | tf_op jit(solution)/shard_map/ppermute | solution.py:254
  150.6 0.7 copy-start.10
  150.6 0.8 copy-start.5
  153.6 11.5 %collective-permute-start.12 = (f32[4,128,128]{2,1,0:T(8,128)}, f32[4,128,128]{2,1,0:T(8,128)S(1)}, u32[]{:S(2)}, u32[]{:S(2)}) collective-permute-start(f32[4,128,128]{2,1,0:T(8,128)} %shard_map.68), channel_id=1, source_target_pairs={{0,1},{1,2},{2,3},{3,4},{4,5},{5,6},{6,7},{7,8},{8,9},{9,10},{10,1... | collective-permute-start | bytes 786440 | tf_op jit(solution)/shard_map/ppermute | solution.py:256
  156.8 0.7 copy-start.6
  165.2 44.7 %copy-start.1 = (f32[64,8,256]{2,1,0:T(8,128)S(1)}, f32[64,8,256]{2,1,0:T(8,128)}, u32[]{:S(2)}) copy-start(f32[64,8,256]{2,1,0:T(8,128)} %param.6) | copy-start | bytes 1572868
  166.3 43.5 %collective-permute-start.13 = (f32[4,64,256]{2,1,0:T(8,128)S(1)}, f32[4,64,256]{2,1,0:T(8,128)S(1)}, u32[]{:S(2)}, u32[]{:S(2)}) collective-permute-start(f32[4,64,256]{2,1,0:T(8,128)S(1)} %get-tuple-element.44), channel_id=1, source_target_pairs={{0,128},{128,0},{256,384},{384,256},{512,640},{640,512},{768,896},... | collective-permute-start | bytes 786440 | tf_op jit(solution)/shard_map/ppermute | solution.py:260
